TPU v7x, 32 devices: a whole 2x2x4 slice. The times are simulated.
32 devices in a mesh: task: 4 (over y, x), dp: 4 (over z), tensor: 2 (over core).
Axes of the slice: x: 2, y: 2, z: 4, core: 2. Of those that a mesh axis runs over, the one named last changes fastest.
Arguments:
- queries: bfloat16 [4, 2400, 768], P('task', 'dp'), may hold values from -6 to 6
- memory: bfloat16 [4, 28800, 768], P('task', 'dp'), may hold values from -6 to 6
- cotangent: bfloat16 [4, 2400, 768], P('task', 'dp'), may hold values from -6 to 6
- matches: int32 [4, 24, 100], P('task', 'dp'), may hold values from 0 to 99, each once within a row
- counts: int32 [4, 24], P('task', 'dp'), may hold values from 1 to 100
- task_order: int32 [4], replicated, may hold values from 0 to 3, each once
- params: bfloat16 [768, 16, 768], P(None, None, 'tensor'), may hold values from -1.875 to 1.875
- head_bias: bfloat16 [8, 768], P(None, 'tensor'), may hold values from -3 to 3
- row_bias: bfloat16 [3, 2, 768], replicated, may hold values from -3 to 3
- norm_gain: bfloat16 [3, 768], replicated, may hold values from 0.5 to 1.5
Outputs:
- block_out: bfloat16 [4, 2400, 768], P('task', 'dp')
- query_grad: bfloat16 [4, 2400, 768], P('task', ('dp', 'tensor'))
- memory_grad: bfloat16 [4, 28800, 768], P('task', ('dp', 'tensor'))
- param_update: float32 [768, 16, 768], P('dp', None, 'tensor')
- head_bias_update: float32 [8, 768], P(None, 'tensor')
- row_bias_update: float32 [3, 2, 768], replicated
- gain_update: float32 [3, 768], replicated
- gram: float32 [4, 4], replicated
Inputs may be any that keep to these rules, and one draw needn't show every extreme that they name: `matches`: for each image, a permutation of the 100 query slots; only the first counts entries name matched queries. `task_order`: a permutation of the indices 0 to 3.
All inputs are finite; a program needn't handle non-finite values.
Results may differ from a plain program's by a relative error of at most 0.015.
Values may be sent and summed in bfloat16 or wider, within the bound.
A program may use at most 256 MiB of HBM per device.

v0:
```python
import jax
import jax.numpy as jnp
from jax import lax
from jax.sharding import PartitionSpec as P

HD = 64


highest = lax.Precision.HIGHEST


def layer_norm(residual, gain_row, shift_row):
    row_mean = jnp.mean(residual, axis=-1, keepdims=True)
    centred = residual - row_mean
    variance = jnp.mean(centred * centred, axis=-1, keepdims=True)
    return centred * lax.rsqrt(variance + 1e-05) * gain_row + shift_row


def gelu_tanh(hidden):
    return (
        0.5
        * hidden
        * (1.0 + jnp.tanh(0.7978845608028654 * (hidden + 0.044715 * hidden * hidden * hidden)))
    )


def combine_weights(gram_matrix, order_list):
    task_count = gram_matrix.shape[0]
    task_index = jnp.arange(task_count, dtype=jnp.int32)
    summed = jnp.zeros((task_count,), jnp.float32)
    for own_task in range(task_count):
        coeffs = (task_index == own_task).astype(jnp.float32)
        for position in range(task_count):
            chosen = (task_index == order_list[position]).astype(jnp.float32)
            column = jnp.dot(gram_matrix, chosen, precision=highest)
            inner_dot = jnp.sum(coeffs * column)
            square = jnp.sum(chosen * column)
            others = (order_list[position] != own_task).astype(jnp.float32)
            coeffs = coeffs - others * jnp.minimum(inner_dot, 0.0) / (square + 1e-06) * chosen
        summed = summed + coeffs
    return summed


def split_heads(activations):
    image_count, row_count, local_width = activations.shape
    return activations.reshape(image_count, row_count, local_width // HD, HD)


def attend_forward(query_act, key_act, value_act):
    image_count, query_rows, local_width = query_act.shape
    scores = jnp.einsum(
        "nqhd,nkhd->nhqk",
        split_heads(query_act),
        split_heads(key_act),
        preferred_element_type=jnp.float32,
    ) * HD ** (-0.5)
    row_max = jnp.max(scores, axis=-1, keepdims=True)
    log_total = row_max + jnp.log(jnp.sum(jnp.exp(scores - row_max), axis=-1, keepdims=True))
    attn_probs = jnp.exp(scores - log_total).astype(jnp.bfloat16)
    attended = jnp.einsum(
        "nhqk,nkhd->nqhd", attn_probs, split_heads(value_act), preferred_element_type=jnp.float32
    )
    return (attended.reshape(image_count, query_rows, local_width).astype(jnp.bfloat16), log_total)


def attend_backward(query_act, key_act, value_act, log_total, grad_mixed):
    query_heads = split_heads(query_act)
    key_heads = split_heads(key_act)
    value_heads = split_heads(value_act)
    grad_heads = split_heads(grad_mixed)
    scores = jnp.einsum(
        "nqhd,nkhd->nhqk", query_heads, key_heads, preferred_element_type=jnp.float32
    ) * HD ** (-0.5)
    attn_probs = jnp.exp(scores - log_total)
    grad_values = jnp.einsum(
        "nhqk,nqhd->nkhd",
        attn_probs.astype(jnp.bfloat16),
        grad_heads,
        preferred_element_type=jnp.float32,
    )
    grad_probs = jnp.einsum(
        "nqhd,nkhd->nhqk", grad_heads, value_heads, preferred_element_type=jnp.float32
    )
    grad_scores = attn_probs * (
        grad_probs - jnp.sum(attn_probs * grad_probs, axis=-1, keepdims=True)
    )
    scores_low = grad_scores.astype(jnp.bfloat16)
    grad_queries = jnp.einsum(
        "nhqk,nkhd->nqhd", scores_low, key_heads, preferred_element_type=jnp.float32
    ) * HD ** (-0.5)
    grad_keys = jnp.einsum(
        "nhqk,nqhd->nkhd", scores_low, query_heads, preferred_element_type=jnp.float32
    ) * HD ** (-0.5)
    return (
        grad_queries.reshape(query_act.shape).astype(jnp.bfloat16),
        grad_keys.reshape(key_act.shape).astype(jnp.bfloat16),
        grad_values.reshape(value_act.shape).astype(jnp.bfloat16),
    )


def body(
    queries, memory, cotangent, matches, counts, task_order, params, head_bias, row_bias, norm_gain
):
    image_count = matches.shape[1]
    query_count = matches.shape[2]
    model_width = queries.shape[2]
    local_width = params.shape[2]
    memory_count = memory.shape[1] // image_count
    tokens = queries[0].reshape(image_count, query_count, model_width)
    context = memory[0].reshape(image_count, memory_count, model_width)
    head_f = head_bias.astype(jnp.float32)
    row_f = row_bias.astype(jnp.float32)
    gain_f = norm_gain.astype(jnp.float32)
    self_proj = jnp.einsum(
        "nld,dke->nlke", tokens, params[:, 0:3], preferred_element_type=jnp.float32
    )
    self_query = (self_proj[:, :, 0] + head_f[0]).astype(jnp.bfloat16)
    self_key = self_proj[:, :, 1].astype(jnp.bfloat16)
    self_value = (self_proj[:, :, 2] + head_f[1]).astype(jnp.bfloat16)
    self_mixed, self_total = attend_forward(self_query, self_key, self_value)
    self_branch = lax.psum(
        jnp.einsum("nld,ed->nle", self_mixed, params[:, 3], preferred_element_type=jnp.float32),
        "tensor",
    )
    first_sum = tokens.astype(jnp.float32) + self_branch + row_f[0, 0]
    first_out = layer_norm(first_sum, gain_f[0], row_f[0, 1])
    first_low = first_out.astype(jnp.bfloat16)
    cross_query = (
        jnp.einsum("nld,de->nle", first_low, params[:, 4], preferred_element_type=jnp.float32)
        + head_f[2]
    ).astype(jnp.bfloat16)
    cross_proj = jnp.einsum(
        "nmd,dke->nmke", context, params[:, 5:7], preferred_element_type=jnp.float32
    )
    cross_key = cross_proj[:, :, 0].astype(jnp.bfloat16)
    cross_value = (cross_proj[:, :, 1] + head_f[3]).astype(jnp.bfloat16)
    cross_mixed, cross_total = attend_forward(cross_query, cross_key, cross_value)
    cross_branch = lax.psum(
        jnp.einsum("nld,ed->nle", cross_mixed, params[:, 7], preferred_element_type=jnp.float32),
        "tensor",
    )
    second_sum = first_out + cross_branch + row_f[1, 0]
    second_out = layer_norm(second_sum, gain_f[1], row_f[1, 1])
    second_low = second_out.astype(jnp.bfloat16)
    weight_in = params[:, 8:12].reshape(model_width, 4 * local_width)
    weight_out = params[:, 12:16].reshape(model_width, 4 * local_width)
    hidden = jnp.einsum(
        "nld,dj->nlj", second_low, weight_in, preferred_element_type=jnp.float32
    ) + head_f[4:8].reshape(4 * local_width)
    activated = gelu_tanh(hidden).astype(jnp.bfloat16)
    ffn_branch = lax.psum(
        jnp.einsum("nlj,ej->nle", activated, weight_out, preferred_element_type=jnp.float32),
        "tensor",
    )
    third_sum = second_out + ffn_branch + row_f[2, 0]
    block_out = (
        layer_norm(third_sum, gain_f[2], row_f[2, 1])
        .astype(jnp.bfloat16)
        .reshape(1, image_count * query_count, model_width)
    )
    slot_index = jnp.arange(query_count, dtype=jnp.int32)
    box_live = slot_index[None, :] < counts[0][:, None]
    matched = (matches[0][:, :, None] == slot_index[None, None, :]) & box_live[:, :, None]
    live_mask = jnp.sum(matched.astype(jnp.float32), axis=1)
    out_grad = (
        cotangent[0].reshape(image_count, query_count, model_width).astype(jnp.float32)
        * live_mask[:, :, None]
    )
    third_grad, gain_three, shift_three = jax.vjp(layer_norm, third_sum, gain_f[2], row_f[2, 1])[1](
        out_grad
    )
    ffn_low = third_grad.astype(jnp.bfloat16)
    grad_weight_out = jnp.einsum(
        "nle,nlj->ej", ffn_low, activated, preferred_element_type=jnp.float32
    )
    grad_activated = jnp.einsum(
        "nle,ej->nlj", ffn_low, weight_out, preferred_element_type=jnp.float32
    )
    grad_hidden = jax.vjp(gelu_tanh, hidden)[1](grad_activated)[0].astype(jnp.bfloat16)
    grad_weight_in = jnp.einsum(
        "nld,nlj->dj", second_low, grad_hidden, preferred_element_type=jnp.float32
    )
    second_in = third_grad + lax.psum(
        jnp.einsum("nlj,dj->nld", grad_hidden, weight_in, preferred_element_type=jnp.float32),
        "tensor",
    )
    ffn_weights = jnp.concatenate(
        [
            grad_weight_in.reshape(model_width, 4, local_width),
            grad_weight_out.reshape(model_width, 4, local_width),
        ],
        axis=1,
    )
    ffn_small = jnp.concatenate(
        [
            jnp.sum(grad_hidden, axis=(0, 1), dtype=jnp.float32),
            jnp.sum(third_grad, axis=(0, 1)),
            shift_three,
            gain_three,
        ]
    )
    second_grad, gain_two, shift_two = jax.vjp(layer_norm, second_sum, gain_f[1], row_f[1, 1])[1](
        second_in
    )
    cross_low = second_grad.astype(jnp.bfloat16)
    grad_cross_out = jnp.einsum(
        "nle,nld->ed", cross_low, cross_mixed, preferred_element_type=jnp.float32
    )
    grad_cross_mixed = jnp.einsum(
        "nle,ed->nld", cross_low, params[:, 7], preferred_element_type=jnp.float32
    ).astype(jnp.bfloat16)
    grad_cross_query, grad_cross_key, grad_cross_value = attend_backward(
        cross_query, cross_key, cross_value, cross_total, grad_cross_mixed
    )
    grad_cross_pair = jnp.stack([grad_cross_key, grad_cross_value], axis=2)
    grad_cross_qw = jnp.einsum(
        "nld,nle->de", first_low, grad_cross_query, preferred_element_type=jnp.float32
    )
    grad_cross_kv = jnp.einsum(
        "nmd,nmke->dke", context, grad_cross_pair, preferred_element_type=jnp.float32
    )
    memory_part = jnp.einsum(
        "nmke,dke->nmd", grad_cross_pair, params[:, 5:7], preferred_element_type=jnp.float32
    )
    first_in = second_grad + lax.psum(
        jnp.einsum(
            "nle,de->nld", grad_cross_query, params[:, 4], preferred_element_type=jnp.float32
        ),
        "tensor",
    )
    cross_weights = jnp.concatenate(
        [grad_cross_qw[:, None], grad_cross_kv, grad_cross_out[:, None]], axis=1
    )
    cross_bias_sums = jnp.concatenate(
        [
            jnp.sum(grad_cross_query, axis=(0, 1), dtype=jnp.float32),
            jnp.sum(grad_cross_value, axis=(0, 1), dtype=jnp.float32),
        ]
    )
    cross_small = jnp.concatenate(
        [cross_bias_sums, jnp.sum(second_grad, axis=(0, 1)), shift_two, gain_two]
    )
    first_grad, gain_one, shift_one = jax.vjp(layer_norm, first_sum, gain_f[0], row_f[0, 1])[1](
        first_in
    )
    self_low = first_grad.astype(jnp.bfloat16)
    grad_self_out = jnp.einsum(
        "nle,nld->ed", self_low, self_mixed, preferred_element_type=jnp.float32
    )
    grad_self_mixed = jnp.einsum(
        "nle,ed->nld", self_low, params[:, 3], preferred_element_type=jnp.float32
    ).astype(jnp.bfloat16)
    grad_self_query, grad_self_key, grad_self_value = attend_backward(
        self_query, self_key, self_value, self_total, grad_self_mixed
    )
    grad_self_all = jnp.stack([grad_self_query, grad_self_key, grad_self_value], axis=2)
    grad_self_qkv = jnp.einsum(
        "nld,nlke->dke", tokens, grad_self_all, preferred_element_type=jnp.float32
    )
    token_part = jnp.einsum(
        "nlke,dke->nld", grad_self_all, params[:, 0:3], preferred_element_type=jnp.float32
    )
    self_weights = jnp.concatenate([grad_self_qkv, grad_self_out[:, None]], axis=1)
    self_small = jnp.concatenate(
        [
            jnp.sum(grad_self_query, axis=(0, 1), dtype=jnp.float32),
            jnp.sum(grad_self_value, axis=(0, 1), dtype=jnp.float32),
            jnp.sum(first_grad, axis=(0, 1)),
            shift_one,
            gain_one,
        ]
    )
    reduced = (
        lax.psum_scatter(self_weights, "dp", scatter_dimension=0, tiled=True),
        lax.psum_scatter(cross_weights, "dp", scatter_dimension=0, tiled=True),
        lax.psum_scatter(ffn_weights, "dp", scatter_dimension=0, tiled=True),
        lax.psum_scatter(self_small, "dp", scatter_dimension=0, tiled=True),
        lax.psum_scatter(cross_small, "dp", scatter_dimension=0, tiled=True),
        lax.psum_scatter(ffn_small, "dp", scatter_dimension=0, tiled=True),
    )
    weight_shard = jnp.concatenate([reduced[0], reduced[1], reduced[2]], axis=1)
    small_shards = (reduced[3], reduced[4], reduced[5])
    token_rows = token_part.reshape(1, image_count * query_count, model_width)
    input_rows = (token_rows, memory_part.reshape(1, image_count * memory_count, model_width))
    shares = (
        lax.psum_scatter(input_rows[0], "tensor", scatter_dimension=1, tiled=True),
        lax.psum_scatter(input_rows[1], "tensor", scatter_dimension=1, tiled=True),
    )
    token_share = shares[0]
    share_rows = token_share.shape[1]
    residual_share = lax.dynamic_slice_in_dim(
        first_grad.reshape(1, image_count * query_count, model_width),
        lax.axis_index("tensor") * share_rows,
        share_rows,
        1,
    )
    query_grad = (token_share + residual_share).astype(jnp.bfloat16)
    memory_grad = shares[1].astype(jnp.bfloat16)
    gathered = (
        lax.all_gather(weight_shard[None], "task", axis=0, tiled=True),
        lax.all_gather(small_shards[0][None], "task", axis=0, tiled=True),
        lax.all_gather(small_shards[1][None], "task", axis=0, tiled=True),
        lax.all_gather(small_shards[2][None], "task", axis=0, tiled=True),
    )
    task_count = gathered[0].shape[0]
    weight_flat = gathered[0].reshape(task_count, -1)
    gram_part = jnp.einsum("ax,bx->ab", weight_flat, weight_flat, precision=highest)
    shared_share = 1.0 / lax.axis_size("tensor")
    split_entries = (2 * local_width, 2 * local_width, 4 * local_width)
    dp_index = lax.axis_index("dp")
    for small_piece, split_count in zip(gathered[1:], split_entries):
        piece_length = small_piece.shape[1]
        entry_index = jnp.arange(piece_length * lax.axis_size("dp"), dtype=jnp.int32)
        scale_full = jnp.where(entry_index < split_count, 1.0, shared_share).astype(jnp.float32)
        scale_part = lax.dynamic_slice_in_dim(scale_full, dp_index * piece_length, piece_length)
        gram_part = gram_part + jnp.einsum(
            "ax,bx->ab", small_piece * scale_part, small_piece, precision=highest
        )
    gram = lax.psum(gram_part, ("dp", "tensor"))
    task_weights = combine_weights(gram, task_order)
    param_update = jnp.einsum("a,ax->x", task_weights, weight_flat, precision=highest).reshape(
        weight_shard.shape
    )
    small_updates = tuple(
        (
            jnp.einsum("a,ax->x", task_weights, small_piece, precision=highest)
            for small_piece in gathered[1:]
        )
    )
    self_full, cross_piece, ffn_full = lax.all_gather(small_updates, "dp", axis=0, tiled=True)
    head_bias_update = jnp.concatenate(
        [
            self_full[: 2 * local_width].reshape(2, local_width),
            cross_piece[: 2 * local_width].reshape(2, local_width),
            ffn_full[: 4 * local_width].reshape(4, local_width),
        ],
        axis=0,
    )
    row_parts = []
    gain_parts = []
    for full_piece, split_count in zip((self_full, cross_piece, ffn_full), split_entries):
        row_parts.append(
            jnp.stack(
                [
                    full_piece[split_count : split_count + model_width],
                    full_piece[split_count + model_width : split_count + 2 * model_width],
                ],
                axis=0,
            )
        )
        gain_parts.append(full_piece[split_count + 2 * model_width : split_count + 3 * model_width])
    row_bias_update = jnp.stack(row_parts, axis=0)
    gain_update = jnp.stack(gain_parts, axis=0)
    return (
        block_out,
        query_grad,
        memory_grad,
        param_update,
        head_bias_update,
        row_bias_update,
        gain_update,
        gram,
    )


def solution(mesh):
    return jax.shard_map(
        body,
        mesh=mesh,
        in_specs=(
            P("task", "dp", None),
            P("task", "dp", None),
            P("task", "dp", None),
            P("task", "dp", None),
            P("task", "dp"),
            P(),
            P(None, None, "tensor"),
            P(None, "tensor"),
            P(),
            P(),
        ),
        out_specs=(
            P("task", "dp", None),
            P("task", ("dp", "tensor"), None),
            P("task", ("dp", "tensor"), None),
            P("dp", None, "tensor"),
            P(None, "tensor"),
            P(),
            P(),
            P(),
        ),
        check_vma=False,
    )
```

profile of v0, /device:TPU:8, one launch (start us, length us, event | category | flops | bytes accessed | tf_op | source)
XLA Modules:
  0.0 1348.5 jit_solution(15105947877852615395)
XLA Ops:
  14.4 8.8 fusion.104
  36.3 17.3 %fusion.34 = f32[6,1200,2,384]{3,1,2,0:T(8,128)} fusion(bf16[6,1200,768,1]{2,1,3,0:T(8,128)(2,1)} %bitcast.286, bf16[768,2,384]{2,1,0:T(2,128)(2,1)S(1)} %slice.204), kind=kOutput, calls=%fused_computation.115 | convolution fusion | flops 8493465600 | bytes 34357248 | tf_op jit(solution)/shard_map/nmd,dke->nmke/dot_general | solution.py:132
  60.8 8.9 slice.255
  69.8 8.7 copy.153
  78.5 13.9 %copy.150 = f32[6,1200,1,384]{1,3,0,2:T(8,128)} copy(f32[6,1200,1,384]{3,1,2,0:T(8,128)} %slice.255) | data formatting | bytes 22118400 | tf_op jit(solution)/shard_map/slice | solution.py:136
  96.9 11.9 fusion.110
  108.9 9.4 exponential_reduce_fusion
  118.2 11.9 fusion.22
  168.5 18.8 %all-reduce.22.cloned.1.call-done = f32[6,100,768]{2,1,0:T(8,128)} async-done(((f32[6,100,768]{2,1,0:T(8,128)}), f32[6,100,768]{2,1,0:T(8,128)}) %all-reduce.22.cloned.1.call-update) | async-done | bytes 1843216 | tf_op jit(solution)/shard_map/psum | solution.py:151
  207.1 21.8 %all-reduce.24.cloned.1.call-done = f32[6,100,768]{2,1,0:T(8,128)} async-done(((f32[6,100,768]{2,1,0:T(8,128)}), f32[6,100,768]{2,1,0:T(8,128)}) %all-reduce.24.cloned.1.call-update) | async-done | bytes 1843216 | tf_op jit(solution)/shard_map/psum | solution.py:183
  238.2 10.4 convert_reduce_fusion
  248.6 17.9 %multiply_reduce_fusion = (f32[6,6,100]{2,1,0:T(8,128)S(1)}, f32[6,6,100,1200]{3,2,1,0:T(8,128)}) fusion(f32[6,6,100,1200]{3,2,1,0:T(8,128)} %get-tuple-element.103, f32[6,6,100]{2,1,0:T(8,128)S(1)} %log_add_fusion, bf16[6,100,6,64]{1,3,2,0:T(8,128)(2,1)S(1)} %bitcast.263, f32[6,1200,6,64]{1,3,2,0:T(8,128)} %bitcast.250, f32[6,64]{1,0:T(8,128)S(1)} %add.284), kind=kOutput, calls=%fused_computation.1 | convolution fusion | flops 571446016 | bytes 46110336 | tf_op jit(solution)/shard_map/nqhd,nkhd->nhqk/dot_general | solution.py:81
  266.5 16.4 %multiply_convert_fusion = bf16[6,6,100,1200]{3,2,1,0:T(8,128)(2,1)} fusion(f32[6,6,100,1200]{3,2,1,0:T(8,128)} %get-tuple-element.105, f32[6,6,100,1200]{3,2,1,0:T(8,128)} %get-tuple-element.103, f32[6,6,100]{2,1,0:T(8,128)S(1)} %get-tuple-element.104, f32[6,6,100]{2,1,0:T(8,128)S(1)} %log_add_fusion), kind=kLoop, calls=%fused_computation | loop fusion | flops 17280000 | bytes 43228800 | tf_op jit(solution)/shard_map/convert_element_type | solution.py:87
  282.9 9.7 convert_reduce_fusion.2
  306.1 9.4 copy.172
  315.5 9.0 copy.171
  325.4 14.8 %fusion.16 = f32[768,2,384]{0,2,1:T(8,128)S(1)} fusion(bf16[6,1200,768,1]{2,1,3,0:T(8,128)(2,1)} %bitcast.287, bf16[6,1200,1,384]{3,1,2,0:T(8,128)(2,1)} %copy.172, bf16[6,1200,1,384]{3,1,2,0:T(8,128)(2,1)} %copy.171), kind=kOutput, calls=%fused_computation.63 | convolution fusion | flops 8498995200 | bytes 24477696 | tf_op jit(solution)/shard_map/nmd,nmke->dke/dot_general | solution.py:219
  405.5 9.3 pad_maximum_fusion.1
  416.1 15.8 %fusion.5 = f32[6,1200,768,1]{2,1,3,0:T(8,128)} fusion(bf16[6,1200,1,384]{3,1,2,0:T(8,128)(2,1)} %copy.172, bf16[6,1200,1,384]{3,1,2,0:T(8,128)(2,1)} %copy.171, bf16[768,2,384]{2,1,0:T(2,128)(2,1)S(1)} %copy-done.42), kind=kOutput, calls=%fused_computation.15 | convolution fusion | flops 8498995200 | bytes 34357248 | tf_op jit(solution)/shard_map/nmke,dke->nmd/dot_general | solution.py:222
  433.9 268.8 %all-reduce.28.cloned.1.call-done = (f32[768,4,384]{2,1,0:T(4,128)}, f32[768,4,384]{2,1,0:T(4,128)}) async-done(((f32[768,4,384]{2,1,0:T(4,128)}, f32[768,4,384]{2,1,0:T(4,128)}), (f32[768,4,384]{2,1,0:T(4,128)}, f32[768,4,384]{2,1,0:T(4,128)})) %all-reduce.28.cloned.1.call-update) | async-done | bytes 9437200
  704.7 162.6 %reduce-scatter.8.cloned.1.call-done = f32[192,8,384]{2,1,0:T(8,128)} async-done(((f32[768,8,384]{2,1,0:T(8,128)}), f32[192,8,384]{2,1,0:T(8,128)}) %reduce-scatter.8.cloned.1.call-update) | async-done | bytes 2359312 | tf_op jit(solution)/shard_map/reduce_scatter | solution.py:276
  906.4 15.8 %all-reduce.9 = (f32[3072]{0:T(1024)S(1)}, f32[3072]{0:T(1024)S(1)}, f32[3840]{0:T(1024)S(1)}) all-reduce(f32[3072]{0:T(1024)S(1)} %get-tuple-element.120, f32[3072]{0:T(1024)S(1)} %get-tuple-element.121, f32[3840]{0:T(1024)S(1)} %pad_maximum_fusion.13), channel_id=11, replica_groups=mesh['task'=4,'dp'=4,'tensor'=2] {'dp'}, use_global_device_ids=true, to_apply=%region_34.0.clone | all-reduce | flops 9984 | bytes 79872
  922.3 16.6 %all-reduce = f32[3840]{0:T(1024)S(1)} all-reduce(f32[3840]{0:T(1024)S(1)} %dynamic-slice_dynamic-update-slice_fusion), channel_id=5, replica_groups=mesh['task'=4,'dp'=4,'tensor'=2] {'task'}, use_global_device_ids=true, to_apply=%add | all-reduce | flops 3840 | bytes 30720
  946.5 8.4 all-gather.5
  967.6 115.6 %all-gather.10.cloned.1.call-done = f32[768,16,384]{2,1,0:T(8,128)} async-done(((f32[192,16,384]{2,1,0:T(8,128)}), f32[768,16,384]{2,1,0:T(8,128)}) %all-gather.10.cloned.1.call-update) | async-done | bytes 18874384 | tf_op jit(solution)/shard_map/all_gather | solution.py:300
  1083.2 114.0 %fusion.27 = f32[4,4]{1,0:T(4,128)S(1)} fusion(f32[4,192,16,384]{3,2,1,0:T(8,128)} %bitcast.252), kind=kOutput, calls=%fused_computation.100 | convolution fusion | flops 226492416 | bytes 18874432 | tf_op jit(solution)/shard_map/ax,bx->ab/dot_general | solution.py:307
  1197.7 12.8 psum.47
  1234.0 17.6 %all-reduce.1 = f32[3840]{0:T(1024)S(1)} all-reduce(f32[3840]{0:T(1024)S(1)} %dynamic-update-slice.1), channel_id=1, replica_groups=mesh['task'=4,'dp'=4,'tensor'=2] {'dp'}, use_global_device_ids=true, to_apply=%add.1 | all-reduce | flops 3840 | bytes 30720
  1251.7 12.2 all-gather.6
  1263.9 13.2 all-gather.7
  1277.1 23.7 %reshape.338 = f32[4,1179648]{1,0:T(4,128)} reshape(f32[768,16,384]{2,1,0:T(8,128)} %all-gather.10.cloned.1.call-done) | data formatting | bytes 37748736 | tf_op jit(solution)/shard_map/reshape | solution.py:306
  1300.8 36.5 %fusion.81 = f32[1,192,16,384]{3,0,2,1:T(1,128)S(1)} fusion(f32[192,16,384,4]{2,3,1,0:T(4,128)} %bitcast.251, f32[4]{0:T(128)S(1)} %subtract_add_fusion), kind=kOutput, calls=%fused_computation.228 | convolution fusion | flops 56623104 | bytes 23592976 | tf_op jit(solution)/shard_map/a,ax->x/dot_general | solution.py:321
  (340 shorter events, 244.2 us)
Async XLA Ops:
  7.2 85.3 %all-reduce.18.cloned.1.call-start = ((), (), s32[]{:S(2)}) async-start(), calls=%async_computation.2 | async-start | bytes 3833856 | tf_op jit(solution)/shard_map/psum | solution.py:121
  14.4 8.8 copy-start.57
  31.1 123.7 %all-reduce.20.cloned.1.call-start = ((), (), s32[]{:S(2)}) async-start(), calls=%async_computation.3 | async-start | bytes 3833856 | tf_op jit(solution)/shard_map/psum | solution.py:138
  60.8 8.9 copy-start.65
  60.8 9.0 copy-start.62
  118.2 12.0 copy-start.28
  132.3 55.1 %all-reduce.22.cloned.1.call-start = ((), (), s32[]{:S(2)}) async-start(), calls=%async_computation.4 | async-start | bytes 3833856 | tf_op jit(solution)/shard_map/psum | solution.py:151
  165.1 63.8 %all-reduce.24.cloned.1.call-start = ((), (), s32[]{:S(2)}) async-start(), calls=%async_computation.5 | async-start | bytes 3833856 | tf_op jit(solution)/shard_map/psum | solution.py:183
  168.5 24.5 %copy-start.51 = (f32[6,100]{1,0:T(8,128)}, f32[6,100]{1,0:T(8,128)S(1)}, u32[]{:S(2)}) copy-start(f32[6,100]{1,0:T(8,128)S(1)} %convert_reduce_fusion.5) | copy-start | bytes 7204
  195.0 7.3 copy-start.13
  206.6 142.7 %all-reduce.26.cloned.1.call-start = ((), (), s32[]{:S(2)}) async-start(), calls=%async_computation.6 | async-start | bytes 3833856 | tf_op jit(solution)/shard_map/psum | solution.py:225
  292.6 8.1 copy-start.27
  292.6 8.1 copy-start.38
  302.8 399.9 %all-reduce.28.cloned.1.call-start = ((), (), s32[]{:S(2)}) async-start(), calls=%async_computation.10 | async-start | bytes 18874368
  315.5 9.0 copy-start.39
  325.4 14.9 %copy-start.40 = (f32[768,1,384]{0,2,1:T(8,128)S(1)}, f32[768,1,384]{0,2,1:T(8,128)}, u32[]{:S(2)}) copy-start(f32[768,1,384]{0,2,1:T(8,128)} %convolution_bitcast_fusion.4) | copy-start | bytes 3538948
  378.4 488.9 %reduce-scatter.8.cloned.1.call-start = ((), (), s32[]{:S(2)}) async-start(), calls=%async_computation.8 | async-start | bytes 11796480 | tf_op jit(solution)/shard_map/reduce_scatter | solution.py:276
  414.9 545.6 %reduce-scatter.6.cloned.1.call-start = ((), (), s32[]{:S(2)}) async-start(), calls=%async_computation.7 | async-start | bytes 33177600 | tf_op jit(solution)/shard_map/reduce_scatter | solution.py:287
  432.0 651.2 %all-gather.10.cloned.1.call-start = ((), (), s32[]{:S(2)}) async-start(), calls=%async_computation.9 | async-start | bytes 23592960 | tf_op jit(solution)/shard_map/all_gather | solution.py:300
  871.8 10.9 copy-start.52
  871.8 11.0 copy-start.69
  871.9 12.3 copy-start.71
  871.9 17.3 %copy-start.24 = (bf16[6,100,768]{2,1,0:T(8,128)(2,1)S(1)}, bf16[6,100,768]{2,1,0:T(8,128)(2,1)}, u32[]{:S(2)}) copy-start(bf16[6,100,768]{2,1,0:T(8,128)(2,1)} %get-tuple-element.80) | copy-start | bytes 2764804
  871.9 18.5 %copy-start.58 = (f32[768]{0:T(1024)S(1)}, f32[768]{0:T(1024)}, u32[]{:S(2)}) copy-start(f32[768]{0:T(1024)} %get-tuple-element.81) | copy-start | bytes 9220
  871.9 18.5 %copy-start.61 = (f32[768]{0:T(1024)S(1)}, f32[768]{0:T(1024)}, u32[]{:S(2)}) copy-start(f32[768]{0:T(1024)} %get-tuple-element.8) | copy-start | bytes 9220
  871.9 18.5 %copy-start.64 = (f32[1536]{0:T(1024)S(1)}, f32[1536]{0:T(1024)}, u32[]{:S(2)}) copy-start(f32[1536]{0:T(1024)} %get-tuple-element.116) | copy-start | bytes 18436
  871.9 18.5 %copy-start.6 = (f32[6,100,768]{2,1,0:T(8,128)S(1)}, f32[6,100,768]{2,1,0:T(8,128)}, u32[]{:S(2)}) copy-start(f32[6,100,768]{2,1,0:T(8,128)} %copy-done.5) | copy-start | bytes 5529604
  899.0 7.3 copy-start.59
  899.0 7.4 copy-start.60
  903.8 54.5 %copy-start.23 = (f32[1,600,768]{2,1,0:T(8,128)S(1)}, f32[1,600,768]{2,1,0:T(8,128)}, u32[]{:S(2)}) copy-start(f32[1,600,768]{2,1,0:T(8,128)} %reshape.334) | copy-start | bytes 5529604
  903.8 51.0 %collective-permute-start = (f32[4,768]{1,0:T(4,128)S(1)}, f32[4,768]{1,0:T(4,128)S(1)}, u32[]{:S(2)}, u32[]{:S(2)}) collective-permute-start(f32[4,768]{1,0:T(4,128)S(1)} %slice.278), channel_id=1, source_target_pairs={{0,1},{2,3},{4,5},{6,7},{8,9},{10,11},{12,13},{14,15},{16,17},{18,... | collective-permute-start | bytes 36872
  1210.6 90.2 %copy-start.68 = (f32[4,4]{1,0:T(4,128)}, f32[4,4]{1,0:T(4,128)S(1)}, u32[]{:S(2)}) copy-start(f32[4,4]{1,0:T(4,128)S(1)} %psum.47) | copy-start | bytes 196
  (53 other events, 121.8 us)
Sparse Core Ops, SparseCore 0:
  31.3 22.3 all-reduce.17
  132.4 22.3 all-reduce.19
  165.2 22.0 all-reduce.21
  206.7 22.0 all-reduce.23
  302.9 22.0 all-reduce.25
  378.5 324.0 all-reduce.27
  705.0 162.2 reduce-scatter.7
  869.5 33.7 reduce-scatter.5
  905.8 177.4 all-gather.9
where the time goes:
time: 1360 us; the launch traced here: 1350 us
  waiting for transfers between devices  591 us (43%)
  matrix products  334 us (25%)
  local copies, waits for them, and re-layouts  187 us (14%)
  blocking collectives  109 us (8%)
  other arithmetic  80.9 us (6%)
  between operations  42.4 us (3%)
    unnamed x11, waiting for transfers between devices  269 us
    reduce_scatter x1, waiting for transfers between devices, body(): lax.psum_scatter(ffn_weights, 'dp', scatter_dimension=0, tiled=True)  163 us
    all_gather x1, waiting for transfers between devices, body(): lax.all_gather(weight_shard[None], 'task', axis=0, tiled=True)  116 us
    dot_general x1, matrix products, body(): jnp.einsum('ax,bx->ab', weight_flat, weight_flat, precision=highest)  114 us
    unnamed x4, blocking collectives  54.8 us
    dot_general x1, matrix products, body(): jnp.einsum('a,ax->x', task_weights, weight_flat, precision=highest)  36.5 us
    unnamed x175, local copies, waits for them, and re-layouts  35.9 us
  transfers between devices with their start and end apart: 10, of which 6 were waited for; matrix products, arithmetic and copies ran while one was open for 16% of the time, Pallas kernels for 0%

commit v1 on v0

v1 whole, which is shorter than its diff:
```python
import functools

import jax
import jax.numpy as jnp
from jax import lax
from jax.experimental import pallas as pl
from jax.experimental.pallas import tpu as pltpu
from jax.sharding import PartitionSpec as P

HD = 64
GROUP = 4
SLAB = GROUP * HD
BF = jnp.bfloat16
F32 = jnp.float32
MESH_ID = pl.DeviceIdType.MESH
highest = lax.Precision.HIGHEST
VMEM_LIMIT = 60 * 2**20


def combine_weights(gram_matrix, order_list):
    task_count = gram_matrix.shape[0]
    task_index = jnp.arange(task_count, dtype=jnp.int32)
    summed = jnp.zeros((task_count,), F32)
    for own_task in range(task_count):
        coeffs = (task_index == own_task).astype(F32)
        for position in range(task_count):
            chosen = (task_index == order_list[position]).astype(F32)
            column = jnp.sum(gram_matrix * chosen[None, :], axis=1)
            inner_dot = jnp.sum(coeffs * column)
            square = jnp.sum(chosen * column)
            others = (order_list[position] != own_task).astype(F32)
            coeffs = coeffs - others * jnp.minimum(inner_dot, 0.0) / (square + 1e-06) * chosen
        summed = summed + coeffs
    return summed


def mm(a, b):
    return jnp.dot(a, b, preferred_element_type=F32)


def mm_nt(a, b):
    return lax.dot_general(a, b, (((1,), (1,)), ((), ())), preferred_element_type=F32)


def mm_tn(a, b):
    return lax.dot_general(a, b, (((0,), (0,)), ((), ())), preferred_element_type=F32)


def norm_parts(residual):
    row_mean = jnp.mean(residual, axis=-1, keepdims=True)
    centred = residual - row_mean
    variance = jnp.mean(centred * centred, axis=-1, keepdims=True)
    scale = lax.rsqrt(variance + 1e-05)
    return centred * scale, scale


def norm_back(normed, scale, gain_row, grad):
    scaled = grad * gain_row
    first = jnp.mean(scaled, axis=-1, keepdims=True)
    second = jnp.mean(scaled * normed, axis=-1, keepdims=True)
    return scale * (scaled - first - normed * second)


def rows_sum(value):
    return jnp.sum(value, axis=0, keepdims=True)


def gelu_tanh(hidden):
    return (
        0.5
        * hidden
        * (1.0 + jnp.tanh(0.7978845608028654 * (hidden + 0.044715 * hidden * hidden * hidden)))
    )


def gelu_slope(hidden):
    square = hidden * hidden
    tanh = jnp.tanh(0.7978845608028654 * (hidden + 0.044715 * hidden * square))
    inner = 0.7978845608028654 * (1.0 + 3 * 0.044715 * square)
    return 0.5 * (1.0 + tanh) + 0.5 * hidden * (1.0 - tanh * tanh) * inner


def head_mask(head, rows, dtype):
    lane = lax.broadcasted_iota(jnp.int32, (rows, SLAB), 1)
    return (lane // HD == head).astype(F32).astype(dtype)


def stack_heads(slab):
    return jnp.concatenate(
        [slab * head_mask(head, slab.shape[0], slab.dtype) for head in range(GROUP)], axis=0
    )


def unstack_heads(stacked):
    rows = stacked.shape[0] // GROUP
    total = None
    for head in range(GROUP):
        part = stacked[head * rows : (head + 1) * rows] * head_mask(head, rows, stacked.dtype)
        total = part if total is None else total + part
    return total


def scores_of(query_stack, key_slab, valid):
    scores = mm_nt(key_slab, query_stack)
    if valid < key_slab.shape[0]:
        row = lax.broadcasted_iota(jnp.int32, scores.shape, 0)
        scores = jnp.where(row < valid, scores, -1e30)
    return scores


def attend(query_slab, key_slab, value_slab, valid):
    scores = scores_of(stack_heads(query_slab * HD ** (-0.5)), key_slab, valid)
    row_max = jnp.max(scores, axis=0, keepdims=True)
    exps = jnp.exp(scores - row_max)
    total = jnp.sum(exps, axis=0, keepdims=True)
    probs = (exps * (1.0 / total)).astype(BF)
    mixed = unstack_heads(mm_tn(value_slab, probs).T)
    return mixed, row_max + jnp.log(total)


def attend_back(query_slab, key_slab, value_slab, log_total, grad_slab, valid):
    query_stack = stack_heads(query_slab * HD ** (-0.5))
    grad_stack = stack_heads(grad_slab)
    probs = jnp.exp(scores_of(query_stack, key_slab, valid) - log_total)
    grad_value = mm(probs.astype(BF), grad_stack)
    grad_probs = mm_nt(value_slab, grad_stack)
    inner = jnp.sum(probs * grad_probs, axis=0, keepdims=True)
    grad_scores = (probs * (grad_probs - inner)).astype(BF)
    grad_key = mm(grad_scores, query_stack)
    grad_query = unstack_heads(mm_tn(key_slab, grad_scores).T) * HD ** (-0.5)
    return grad_query.astype(BF), grad_key.astype(BF), grad_value.astype(BF)


def gather_kernel(own_ref, bias_ref, full_ref, full_bias_ref, turned, bias_own, remote_send,
                  remote_recv, local_sem):
    step, steps = pl.program_id(0), pl.num_programs(0)
    other = 1 - lax.axis_index("tensor")
    rows, _, width = own_ref.shape
    near, far = pl.ds(0, width), pl.ds(width, width)

    def copies(chunk):
        at = pl.ds(pl.multiple_of(chunk * rows, rows), rows)
        source = turned.at[:, at]
        return (
            pltpu.make_async_remote_copy(
                source, full_ref.at[:, at, far], remote_send.at[chunk], remote_recv.at[chunk],
                device_id={"tensor": other}, device_id_type=MESH_ID,
            ),
            pltpu.make_async_copy(source, full_ref.at[:, at, near], local_sem.at[chunk]),
        )

    def bias_copies():
        return (
            pltpu.make_async_remote_copy(
                bias_own, full_bias_ref.at[:, far], remote_send.at[steps], remote_recv.at[steps],
                device_id={"tensor": other}, device_id_type=MESH_ID,
            ),
            pltpu.make_async_copy(bias_own, full_bias_ref.at[:, near], local_sem.at[steps]),
        )

    @pl.when(step == 0)
    def _():
        barrier = pltpu.get_barrier_semaphore()
        pl.semaphore_signal(barrier, inc=1, device_id={"tensor": other}, device_id_type=MESH_ID)
        pl.semaphore_wait(barrier, 1)
        bias_own[...] = bias_ref[...]
        for copy in bias_copies():
            copy.start()

    turned[:, pl.ds(pl.multiple_of(step * rows, rows), rows)] = jnp.swapaxes(own_ref[...], 0, 1)
    for copy in copies(step):
        copy.start()

    @pl.when(step == steps - 1)
    def _():
        for copy in bias_copies():
            copy.wait()

        def finish(chunk, carry):
            for copy in copies(chunk):
                copy.wait()
            return carry

        lax.fori_loop(0, steps, finish, 0)


def any_spec():
    return pl.BlockSpec(memory_space=pl.ANY)


def whole_spec():
    return pl.BlockSpec(memory_space=pltpu.VMEM)


def params_for(**keys):
    return pltpu.CompilerParams(vmem_limit_bytes=VMEM_LIMIT, **keys)


def self_kernel(images, valid, tokens_ref, weight_ref, head_ref, row_ref, gain_ref, qkv_ref,
                mixed_ref, total_ref, sum_ref, cross_query_ref):
    tokens = tokens_ref[...]
    rows = tokens.shape[0] // images
    width = tokens.shape[1]
    qkv_ref[0] = (mm(tokens, weight_ref[0]) + head_ref[0:1]).astype(BF)
    qkv_ref[1] = mm(tokens, weight_ref[1]).astype(BF)
    qkv_ref[2] = (mm(tokens, weight_ref[2]) + head_ref[1:2]).astype(BF)
    for image in range(images):
        at = slice(image * rows, (image + 1) * rows)
        for group in range(width // SLAB):
            lanes = slice(group * SLAB, (group + 1) * SLAB)
            mixed, log_total = attend(
                qkv_ref[0, at, lanes], qkv_ref[1, at, lanes], qkv_ref[2, at, lanes], valid
            )
            mixed_ref[at, lanes] = mixed.astype(BF)
            total_ref[image * (width // SLAB) + group] = jnp.broadcast_to(
                log_total, total_ref.shape[1:]
            )
    first_sum = tokens.astype(F32) + mm_nt(mixed_ref[...], weight_ref[3]) + row_ref[0:1]
    sum_ref[...] = first_sum
    first_low = (norm_parts(first_sum)[0] * gain_ref[0:1] + row_ref[1:2]).astype(BF)
    cross_query_ref[...] = (mm(first_low, weight_ref[4]) + head_ref[2:3]).astype(BF)


def cross_kernel(context_ref, query_ref, key_w_ref, value_w_ref, head_ref, key_ref, value_ref,
                 mixed_ref, total_ref):
    context = context_ref[...]
    key_ref[...] = mm(context, key_w_ref[0]).astype(BF)
    value_ref[...] = (mm(context, value_w_ref[0]) + head_ref[3:4]).astype(BF)
    mixed, log_total = attend(query_ref[...], key_ref[...], value_ref[...], key_ref.shape[0])
    mixed_ref[...] = mixed.astype(BF)
    total_ref[0] = jnp.broadcast_to(log_total, total_ref.shape[1:])


def ffn_kernel(
    images, blocks, sum_ref, mixed_ref, cotangent_ref, matches_ref, counts_ref, cross_w_ref, in_ref,
    out_ref, head_ref, row_ref, gain_ref,
    block_ref, grad_in_ref, grad_out_ref, cross_grad_ref, mixed_grad_ref, residual_ref, small_ref,
    second_sum, second_low_t, low_t, hidden, activated, branch, third_grad,
):
    step = pl.program_id(0)
    rows = sum_ref.shape[0] // images

    @pl.when(step == 0)
    def _():
        first_out = norm_parts(sum_ref[...])[0] * gain_ref[0:1] + row_ref[1:2]
        second_sum[...] = first_out + mm_nt(mixed_ref[...], cross_w_ref[0]) + row_ref[2:3]
        branch[...] = jnp.zeros_like(branch)
        small_ref[...] = jnp.zeros_like(small_ref)

    def second_out():
        return norm_parts(second_sum[...])[0] * gain_ref[1:2] + row_ref[3:4]

    @pl.when(step < blocks)
    def _():
        second_low = second_out().astype(BF)
        pre = mm(second_low, in_ref[0]) + head_ref[pl.ds(4 + step, 1)]
        hidden[step] = pre
        act = gelu_tanh(pre).astype(BF)
        activated[step] = act
        branch[...] += mm_nt(act, out_ref[0])

    @pl.when(step == blocks - 1)
    def _():
        second = second_out()
        second_low_t[...] = second.astype(BF).T
        third_sum = second + branch[...] + row_ref[4:5]
        normed, scale = norm_parts(third_sum)
        block_ref[...] = (normed * gain_ref[2:3] + row_ref[5:6]).astype(BF)
        count = matches_ref.shape[2]
        slot = lax.broadcasted_iota(jnp.int32, (rows, count), 0)
        box = lax.broadcasted_iota(jnp.int32, (rows, count), 1)
        grads = []
        for image in range(images):
            live = (matches_ref[image] == slot) & (box < counts_ref[image])
            mask = jnp.sum(jnp.where(live, 1.0, 0.0), axis=1, keepdims=True)
            cot = cotangent_ref[image * rows : (image + 1) * rows].astype(F32)
            grads.append(cot * mask)
        out_grad = jnp.concatenate(grads, axis=0)
        grad = norm_back(normed, scale, gain_ref[2:3], out_grad)
        third_grad[...] = grad
        low_t[...] = grad.astype(BF).T
        small_ref[12:13] = rows_sum(grad)
        small_ref[13:14] = rows_sum(out_grad)
        small_ref[16:17] = rows_sum(out_grad * normed)
        branch[...] = jnp.zeros_like(branch)

    @pl.when(step >= blocks)
    def _():
        block = step - blocks
        ffn_low = third_grad[...].astype(BF)
        grad_out_ref[0] = mm(low_t[...], activated[block]).astype(BF)
        grad_hidden = mm(ffn_low, out_ref[0]) * gelu_slope(hidden[block])
        grad_low = grad_hidden.astype(BF)
        small_ref[pl.ds(4 + block, 1)] = rows_sum(grad_low.astype(F32))
        grad_in_ref[0] = mm(second_low_t[...], grad_low).astype(BF)
        branch[...] += mm_nt(grad_low, in_ref[0])

    @pl.when(step == 2 * blocks - 1)
    def _():
        second_in = third_grad[...] + branch[...]
        normed, scale = norm_parts(second_sum[...])
        grad = norm_back(normed, scale, gain_ref[1:2], second_in)
        residual_ref[...] = grad
        small_ref[10:11] = rows_sum(grad)
        small_ref[11:12] = rows_sum(second_in)
        small_ref[15:16] = rows_sum(second_in * normed)
        cross_low = grad.astype(BF)
        cross_grad_ref[...] = mm(cross_low.T, mixed_ref[...]).astype(BF)
        mixed_grad_ref[...] = mm(cross_low, cross_w_ref[0]).astype(BF)


def cross_back_kernel(
    context_ref, query_ref, key_ref, value_ref, total_ref, mixed_grad_ref, key_w_ref, value_w_ref,
    query_grad_ref, context_grad_ref, key_wg_ref, value_wg_ref, small_ref,
    context_t, acc, key_acc, value_acc,
):
    image, group = pl.program_id(0), pl.program_id(1)
    last_image, last_group = pl.num_programs(0) - 1, pl.num_programs(1) - 1

    @pl.when(group == 0)
    def _():
        context_t[...] = context_ref[...].T

    @pl.when((image == 0) & (group == 0))
    def _():
        small_ref[...] = jnp.zeros_like(small_ref)

    grad_query, grad_key, grad_value = attend_back(
        query_ref[...], key_ref[...], value_ref[...], total_ref[0, 0:1], mixed_grad_ref[...],
        key_ref.shape[0],
    )
    query_grad_ref[...] = grad_query
    lanes = pl.ds(pl.multiple_of(group * SLAB, SLAB), SLAB)
    small_ref[0:1, lanes] += rows_sum(grad_query.astype(F32))
    small_ref[1:2, lanes] += rows_sum(grad_value.astype(F32))
    key_wg = mm(context_t[...], grad_key)
    value_wg = mm(context_t[...], grad_value)
    context_part = mm_nt(grad_key, key_w_ref[0]) + mm_nt(grad_value, value_w_ref[0])

    @pl.when(group == 0)
    def _():
        acc[...] = context_part

    @pl.when((group > 0) & (group < last_group))
    def _():
        acc[...] += context_part

    @pl.when(group == last_group)
    def _():
        context_grad_ref[...] = (acc[...] + context_part).astype(BF)

    @pl.when(image == 0)
    def _():
        key_acc[:, lanes] = key_wg
        value_acc[:, lanes] = value_wg

    @pl.when(image > 0)
    def _():
        key_acc[:, lanes] += key_wg
        value_acc[:, lanes] += value_wg

    @pl.when(image == last_image)
    def _():
        key_wg_ref[:, lanes] = key_acc[:, lanes].astype(BF)
        value_wg_ref[:, lanes] = value_acc[:, lanes].astype(BF)


def self_back_kernel(
    images, valid, tokens_ref, weight_ref, row_ref, gain_ref, qkv_ref, mixed_ref, total_ref, sum_ref,
    residual_ref, cross_query_grad_ref,
    query_grad_ref, cross_wg_ref, self_wg_ref, small_ref, qkv_grad,
):
    small_ref[...] = jnp.zeros_like(small_ref)
    tokens = tokens_ref[...]
    rows = tokens.shape[0] // images
    width = tokens.shape[1]
    normed, scale = norm_parts(sum_ref[...])
    first_low = (normed * gain_ref[0:1] + row_ref[1:2]).astype(BF)
    cross_query_grad = cross_query_grad_ref[...]
    cross_wg_ref[...] = mm(first_low.T, cross_query_grad).astype(BF)
    first_in = residual_ref[...] + mm_nt(cross_query_grad, weight_ref[4])
    first_grad = norm_back(normed, scale, gain_ref[0:1], first_in)
    small_ref[2:3] = rows_sum(first_grad)
    small_ref[3:4] = rows_sum(first_in)
    small_ref[4:5] = rows_sum(first_in * normed)
    self_low = first_grad.astype(BF)
    self_wg_ref[3] = mm(self_low.T, mixed_ref[...]).astype(BF)
    mixed_grad = mm(self_low, weight_ref[3]).astype(BF)
    for image in range(images):
        at = slice(image * rows, (image + 1) * rows)
        for group in range(width // SLAB):
            lanes = slice(group * SLAB, (group + 1) * SLAB)
            grads = attend_back(
                qkv_ref[0, at, lanes], qkv_ref[1, at, lanes], qkv_ref[2, at, lanes],
                total_ref[image * (width // SLAB) + group, 0:1], mixed_grad[at, lanes], valid,
            )
            for which in range(3):
                qkv_grad[which, at, lanes] = grads[which]
    tokens_t = tokens.T
    total = first_grad
    for which in range(3):
        grad = qkv_grad[which]
        self_wg_ref[which] = mm(tokens_t, grad).astype(BF)
        total = total + mm_nt(grad, weight_ref[which])
    small_ref[0:1] = rows_sum(qkv_grad[0].astype(F32))
    small_ref[1:2] = rows_sum(qkv_grad[2].astype(F32))
    query_grad_ref[...] = total.astype(BF)


def gram_kernel(parts_ref, gram_ref):
    tasks = parts_ref.shape[0]

    @pl.when(pl.program_id(0) == 0)
    def _():
        gram_ref[...] = jnp.zeros_like(gram_ref)

    shares = [parts_ref[task, 0].astype(F32) for task in range(tasks)]
    for a in range(tasks):
        for b in range(a, tasks):
            gram_ref[a * tasks + b : a * tasks + b + 1] += rows_sum(shares[a] * shares[b])


def update_kernel(weights_ref, parts_ref, update_ref):
    tasks, blocks = parts_ref.shape[:2]
    for block in range(blocks):
        total = weights_ref[0] * parts_ref[0, block].astype(F32)
        for task in range(1, tasks):
            total += weights_ref[task] * parts_ref[task, block].astype(F32)
        update_ref[:, block, :] = total


def body(
    queries, memory, cotangent, matches, counts, task_order, params, head_bias, row_bias, norm_gain
):
    all_images = matches.shape[1]
    valid = matches.shape[2]
    width = queries.shape[2]
    half = params.shape[2]
    block_count = params.shape[1]
    blocks = (block_count - 8) // 2
    cores = lax.axis_size("tensor")
    images = all_images // cores
    keys = memory.shape[1] // all_images
    padded = -(-valid // 16) * 16
    rows = images * padded
    groups = width // SLAB
    stack = GROUP * padded
    core = lax.axis_index("tensor")

    def own_rows(array):
        split = array[0].reshape(all_images, valid, width)
        mine = lax.dynamic_slice_in_dim(split, core * images, images, 0)
        return jnp.pad(mine, ((0, 0), (0, padded - valid), (0, 0))).reshape(rows, width)

    tokens = own_rows(queries)
    own_cotangent = own_rows(cotangent)
    own_matches = lax.dynamic_slice_in_dim(matches[0], core * images, images, 0)[:, None, :]
    own_counts = lax.dynamic_slice_in_dim(counts[0], core * images, images, 0)
    context = memory[0]
    row_f = jnp.pad(row_bias.astype(F32).reshape(6, width), ((0, 2), (0, 0)))
    gain_f = jnp.pad(norm_gain.astype(F32), ((0, 5), (0, 0)))
    own_bias = jnp.pad(head_bias, ((0, 8), (0, 0)))
    chunk = 96
    weights, full_bias = pl.pallas_call(
        gather_kernel,
        grid=(width // chunk,),
        out_shape=(
            jax.ShapeDtypeStruct((block_count, width, cores * half), BF),
            jax.ShapeDtypeStruct((16, cores * half), BF),
        ),
        in_specs=[
            pl.BlockSpec((chunk, block_count, half), lambda i: (i, 0, 0)),
            pl.BlockSpec((16, half), lambda i: (0, 0)),
        ],
        out_specs=(any_spec(), any_spec()),
        scratch_shapes=[
            pltpu.VMEM((block_count, width, half), BF),
            pltpu.VMEM((16, half), BF),
            pltpu.SemaphoreType.DMA((width // chunk + 1,)),
            pltpu.SemaphoreType.DMA((width // chunk + 1,)),
            pltpu.SemaphoreType.DMA((width // chunk + 1,)),
        ],
        compiler_params=params_for(collective_id=0, has_side_effects=True),
        name="gather_weights",
    )(params, own_bias)
    head_f = full_bias.astype(F32)

    def const(shape, *index):
        return pl.BlockSpec(shape, lambda *_: index)

    total_shape = jax.ShapeDtypeStruct((images * groups, 8, stack), F32)
    low_rows = jax.ShapeDtypeStruct((rows, width), BF)
    full_rows = jax.ShapeDtypeStruct((rows, width), F32)
    small_shape = jax.ShapeDtypeStruct((24, width), F32)
    one_block = jax.ShapeDtypeStruct((width, width), BF)
    small_spec = const((24, width), 0, 0)
    vec8 = const((8, width), 0, 0)
    head_spec = const((16, width), 0, 0)
    rows_spec = const((rows, width), 0, 0)

    qkv, self_mixed, self_total, first_sum, cross_query = pl.pallas_call(
        functools.partial(self_kernel, images, valid),
        grid=(1,),
        out_shape=(
            jax.ShapeDtypeStruct((3, rows, width), BF), low_rows, total_shape, full_rows, low_rows,
        ),
        in_specs=[rows_spec, const((5, width, width), 0, 0, 0), head_spec, vec8, vec8],
        out_specs=(
            const((3, rows, width), 0, 0, 0), rows_spec, const(total_shape.shape, 0, 0, 0),
            rows_spec, rows_spec,
        ),
        compiler_params=params_for(),
        name="self_forward",
    )(tokens, weights, head_f, row_f, gain_f)

    start = (core * images).astype(jnp.int32).reshape(1)
    context_all = pl.BlockSpec((keys, width), lambda i, g, s: (s[0] + i, 0))
    slab_q = pl.BlockSpec((padded, SLAB), lambda i, g, *_: (i, g))
    slab_k = pl.BlockSpec((keys, SLAB), lambda i, g, *_: (i, g))
    slab_t = pl.BlockSpec((1, 8, stack), lambda i, g, *_: (i * groups + g, 0, 0))

    def slab_w(block):
        return pl.BlockSpec((1, width, SLAB), lambda i, g, *_: (block, 0, g))

    def with_start(kernel):
        return lambda start_ref, *refs: kernel(*refs)

    key_rows = jax.ShapeDtypeStruct((images * keys, width), BF)
    keys_act, values_act, cross_mixed, cross_total = pl.pallas_call(
        with_start(cross_kernel),
        grid_spec=pltpu.PrefetchScalarGridSpec(
            num_scalar_prefetch=1,
            grid=(images, groups),
            in_specs=[
                context_all, slab_q, slab_w(5), slab_w(6),
                pl.BlockSpec((16, SLAB), lambda i, g, *_: (0, g)),
            ],
            out_specs=(slab_k, slab_k, slab_q, slab_t),
        ),
        out_shape=(key_rows, key_rows, low_rows, total_shape),
        compiler_params=params_for(),
        name="cross_forward",
    )(start, context, cross_query, weights, weights, head_f)

    (
        block_rows, grad_in, grad_out, cross_out_wg, mixed_grad, second_grad, ffn_small,
    ) = pl.pallas_call(
        functools.partial(ffn_kernel, images, blocks),
        grid=(2 * blocks,),
        out_shape=(
            low_rows,
            jax.ShapeDtypeStruct((blocks, width, width), BF),
            jax.ShapeDtypeStruct((blocks, width, width), BF),
            one_block, low_rows, full_rows, small_shape,
        ),
        in_specs=[
            rows_spec, rows_spec, rows_spec,
            const(own_matches.shape, 0, 0, 0),
            pl.BlockSpec(memory_space=pltpu.SMEM),
            const((1, width, width), 7, 0, 0),
            pl.BlockSpec((1, width, width), lambda s: (8 + s % blocks, 0, 0)),
            pl.BlockSpec((1, width, width), lambda s: (8 + blocks + s % blocks, 0, 0)),
            head_spec, vec8, vec8,
        ],
        out_specs=(
            rows_spec,
            pl.BlockSpec((1, width, width), lambda s: (jnp.maximum(s - blocks, 0), 0, 0)),
            pl.BlockSpec((1, width, width), lambda s: (jnp.maximum(s - blocks, 0), 0, 0)),
            const((width, width), 0, 0), rows_spec, rows_spec, small_spec,
        ),
        scratch_shapes=[
            pltpu.VMEM((rows, width), F32),
            pltpu.VMEM((width, rows), BF),
            pltpu.VMEM((width, rows), BF),
            pltpu.VMEM((blocks, rows, width), F32),
            pltpu.VMEM((blocks, rows, width), BF),
            pltpu.VMEM((rows, width), F32),
            pltpu.VMEM((rows, width), F32),
        ],
        compiler_params=params_for(),
        name="ffn",
    )(
        first_sum, cross_mixed, own_cotangent, own_matches, own_counts, weights, weights, weights,
        head_f, row_f, gain_f,
    )

    cross_query_grad, context_grad, key_wg, value_wg, cross_small = pl.pallas_call(
        with_start(cross_back_kernel),
        grid_spec=pltpu.PrefetchScalarGridSpec(
            num_scalar_prefetch=1,
            grid=(images, groups),
            in_specs=[
                context_all, slab_q, slab_k, slab_k, slab_t, slab_q, slab_w(5), slab_w(6),
            ],
            out_specs=(
                slab_q,
                pl.BlockSpec((keys, width), lambda i, g, *_: (i, 0)),
                const((width, width), 0, 0), const((width, width), 0, 0), small_spec,
            ),
            scratch_shapes=[
                pltpu.VMEM((width, keys), BF),
                pltpu.VMEM((keys, width), F32),
                pltpu.VMEM((width, width), F32),
                pltpu.VMEM((width, width), F32),
            ],
        ),
        out_shape=(low_rows, key_rows, one_block, one_block, small_shape),
        compiler_params=params_for(),
        name="cross_backward",
    )(start, context, cross_query, keys_act, values_act, cross_total, mixed_grad, weights, weights)

    token_grad, cross_query_wg, self_wg, self_small = pl.pallas_call(
        functools.partial(self_back_kernel, images, valid),
        grid=(1,),
        out_shape=(
            low_rows, one_block, jax.ShapeDtypeStruct((4, width, width), BF), small_shape,
        ),
        in_specs=[
            rows_spec, const((5, width, width), 0, 0, 0), vec8, vec8,
            const((3, rows, width), 0, 0, 0), rows_spec, const(total_shape.shape, 0, 0, 0),
            rows_spec, rows_spec, rows_spec,
        ],
        out_specs=(
            rows_spec, const((width, width), 0, 0), const((4, width, width), 0, 0, 0), small_spec,
        ),
        scratch_shapes=[pltpu.VMEM((3, rows, width), BF)],
        compiler_params=params_for(),
        name="self_backward",
    )(
        tokens, weights, row_f, gain_f, qkv, self_mixed, self_total, first_sum, second_grad,
        cross_query_grad,
    )

    def unpad(array):
        return array.reshape(images, padded, width)[:, :valid].reshape(1, images * valid, width)

    block_out = lax.all_gather(unpad(block_rows), "tensor", axis=1, tiled=True)
    query_grad = unpad(token_grad)
    memory_grad = context_grad[None]

    small = jnp.concatenate(
        [
            self_small[0:2], cross_small[0:2], ffn_small[4:8],
            self_small[2:4], ffn_small[10:14], self_small[4:5], ffn_small[15:17],
        ],
        axis=0,
    )
    grads = jnp.concatenate(
        [
            self_wg,
            jnp.stack([cross_query_wg, key_wg, value_wg, cross_out_wg]),
            grad_in,
            grad_out,
        ],
        axis=0,
    )
    swap = [(0, 1), (1, 0)]
    grads = (
        grads[:, :, :half].astype(F32) + lax.ppermute(grads[:, :, half:], "tensor", swap).astype(F32)
    ).astype(BF)
    head_small = small[:8, :half] + lax.ppermute(small[:8, half:], "tensor", swap)
    row_small = lax.psum(small[8:], ("dp", "tensor"))
    head_small = lax.psum(head_small, "dp")
    shard = lax.psum_scatter(grads, "dp", scatter_dimension=1, tiled=True)
    all_shards = lax.all_gather(shard, "task", axis=0, tiled=False)
    all_head = lax.all_gather(head_small, "task", axis=0, tiled=False)
    all_row = lax.all_gather(row_small, "task", axis=0, tiled=False)
    tasks = all_shards.shape[0]
    share_rows = shard.shape[1]
    sums = pl.pallas_call(
        gram_kernel,
        grid=(block_count,),
        out_shape=jax.ShapeDtypeStruct((tasks * tasks, half), F32),
        in_specs=[pl.BlockSpec((tasks, 1, share_rows, half), lambda k: (0, k, 0, 0))],
        out_specs=const((tasks * tasks, half), 0, 0),
        compiler_params=params_for(),
        name="gram",
    )(all_shards)
    upper = jnp.sum(sums, axis=1).reshape(tasks, tasks)
    gram_weights = upper + upper.T - jnp.diag(jnp.diag(upper))
    gram_weights = lax.psum(gram_weights, ("dp", "tensor"))
    gram_heads = jnp.einsum("axy,bxy->ab", all_head, all_head, precision=highest)
    gram_heads = lax.psum(gram_heads, "tensor")
    gram = gram_weights + gram_heads + jnp.einsum(
        "axy,bxy->ab", all_row, all_row, precision=highest
    )
    task_weights = combine_weights(gram, task_order)
    tile = 64 if share_rows % 64 == 0 else share_rows
    param_update = pl.pallas_call(
        update_kernel,
        grid=(share_rows // tile,),
        out_shape=jax.ShapeDtypeStruct((share_rows, block_count, half), F32),
        in_specs=[
            pl.BlockSpec(memory_space=pltpu.SMEM),
            pl.BlockSpec((tasks, block_count, tile, half), lambda r: (0, 0, r, 0)),
        ],
        out_specs=pl.BlockSpec((tile, block_count, half), lambda r: (r, 0, 0)),
        compiler_params=params_for(),
        name="update",
    )(task_weights, all_shards)
    head_bias_update = jnp.einsum("a,axy->xy", task_weights, all_head, precision=highest)
    row_update = jnp.einsum("a,axy->xy", task_weights, all_row, precision=highest)
    return (
        block_out, query_grad, memory_grad, param_update, head_bias_update,
        row_update[:6].reshape(3, 2, width), row_update[6:9], gram,
    )


def solution(mesh):
    return jax.shard_map(
        body,
        mesh=mesh,
        in_specs=(
            P("task", "dp", None),
            P("task", "dp", None),
            P("task", "dp", None),
            P("task", "dp", None),
            P("task", "dp"),
            P(),
            P(None, None, "tensor"),
            P(None, "tensor"),
            P(),
            P(),
        ),
        out_specs=(
            P("task", "dp", None),
            P("task", ("dp", "tensor"), None),
            P("task", ("dp", "tensor"), None),
            P("dp", None, "tensor"),
            P(None, "tensor"),
            P(),
            P(),
            P(),
        ),
        check_vma=False,
    )
```

time: 1360 us -> 573 us (0.42)
  the two profiles are of different devices: /device:TPU:8 before, /device:TPU:0 now
where the time goes in v1:
time: 573 us; the launch traced here: 565 us
  waiting for transfers between devices  225 us (39%)
  Pallas kernels  164 us (29%)
  blocking collectives  70.1 us (12%)
  local copies, waits for them, and re-layouts  41.6 us (7%)
  between operations  38.8 us (7%)
  other arithmetic  23.4 us (4%)
    reduce_scatter x1, waiting for transfers between devices, body(): shard = lax.psum_scatter(grads, 'dp', scatter_dimension=1, tiled=True)  164 us
    pallas_call x1, Pallas kernels, body(): pl.pallas_call(with_start(cross_back_kernel), grid_spec=pltpu.PrefetchSca...  52.2 us
    all_gather x1, waiting for transfers between devices, body(): all_shards = lax.all_gather(shard, 'task', axis=0, tiled=False)  46.6 us
    psum x1, blocking collectives, body(): row_small = lax.psum(small[8:], ('dp', 'tensor'))  28.8 us
    pallas_call x1, Pallas kernels, body(): pl.pallas_call(with_start(cross_kernel), grid_spec=pltpu.PrefetchScalarGr...  25.5 us
    pallas_call x1, Pallas kernels, body(): pl.pallas_call(functools.partial(ffn_kernel, images, blocks), grid=(2 * b...  25.2 us
    psum x1, blocking collectives, body(): head_small = lax.psum(head_small, 'dp')  18.3 us
    pallas_call x1, Pallas kernels, body(): pl.pallas_call(gather_kernel, grid=(width // chunk,), out_shape=(jax.Shap...  16.7 us
  transfers between devices with their start and end apart: 4, of which 3 were waited for; matrix products, arithmetic and copies ran while one was open for 2% of the time, Pallas kernels for 0%

profile of v1, /device:TPU:0, one launch (start us, length us, event | category | flops | bytes accessed | tf_op | source)
XLA Modules:
  0.0 565.5 jit_solution(16156047130655941755)
XLA Ops:
  7.3 1.3 reshape_squeeze.6
  8.6 1.3 reshape_squeeze.7
  10.8 1.3 pad.24.bias_ref
  12.1 16.7 %gather_weights.1 = (bf16[16,768,768]{2,1,0:T(8,128)(2,1)}, bf16[16,768]{1,0:T(8,128)(2,1)}) custom-call(bf16[768,16,384]{2,1,0:T(8,128)(2,1)} %own_ref.1, bf16[16,384]{1,0:T(8,128)(2,1)} %pad.24.bias_ref), custom_call_target="tpu_custom_call" | custom-call | tf_op jit(solution)/shard_map/gather_weights/pallas_call | solution.py:464
  28.8 1.4 convert_element_type.49.head_ref.refs_4_
  32.8 8.8 %self_forward.1 = (bf16[3,336,768]{2,1,0:T(8,128)(2,1)}, bf16[336,768]{1,0:T(8,128)(2,1)}, f32[9,8,448]{2,1,0:T(8,128)}, f32[336,768]{1,0:T(8,128)}, bf16[336,768]{1,0:T(8,128)(2,1)}) custom-call(bf16[336,768]{1,0:T(8,128)(2,1)} %bitcast.58, bf16[16,768,768]{2,1,0:T(8,128)(2,1)} %get-tuple-element.35.weight_ref.refs_2_.refs_3_.cross_w_ref.in_ref.out_ref.refs_6_.refs_7_, ...), custom_call_target="tpu_custom_call" | custom-call | tf_op jit(solution)/shard_map/self_forward/pallas_call | solution.py:501
  41.6 25.5 %cross_forward.1 = (bf16[3600,768]{1,0:T(8,128)(2,1)}, bf16[3600,768]{1,0:T(8,128)(2,1)}, bf16[336,768]{1,0:T(8,128)(2,1)}, f32[9,8,448]{2,1,0:T(8,128)}) custom-call(s32[1]{0:T(128)} %bitcast.1.start_ref, bf16[7200,768]{1,0:T(8,128)(2,1)} %bitcast.52, bf16[336,768]{1,0:T(8,128)(2,1)} %get-tuple-element.38.refs_1_, ...), custom_call_target="tpu_custom_call" | custom-call | tf_op jit(solution)/shard_map/cross_forward/pallas_call | solution.py:529
  67.1 25.2 %ffn.1 = (bf16[336,768]{1,0:T(8,128)(2,1)}, bf16[4,768,768]{2,1,0:T(8,128)(2,1)}, bf16[4,768,768]{2,1,0:T(8,128)(2,1)}, bf16[768,768]{1,0:T(8,128)(2,1)}, bf16[3...) custom-call(f32[336,768]{1,0:T(8,128)} %get-tuple-element.37.sum_ref, ...), custom_call_target="tpu_custom_call" | custom-call | tf_op jit(solution)/shard_map/ffn/pallas_call | solution.py:547
  92.4 52.2 %cross_backward.1 = (bf16[336,768]{1,0:T(8,128)(2,1)}, bf16[3600,768]{1,0:T(8,128)(2,1)}, bf16[768,768]{1,0:T(8,128)(2,1)}, bf16[768,768]{1,0:T(8,128)(2,1)}, f32[24,768]{1,0:T(8,128)}) custom-call(s32[1]{0:T(128)} %bitcast.1.start_ref, bf16[7200,768]{1,0:T(8,128)(2,1)} %bitcast.53, bf16[336,768]{1,0:T(8,128)(2,1)} %get-tuple-element.38.refs_1_, ...), custom_call_target="tpu_custom_call" | custom-call | tf_op jit(solution)/shard_map/cross_backward/pallas_call | solution.py:587
  144.5 16.2 %self_backward.1 = (bf16[336,768]{1,0:T(8,128)(2,1)}, bf16[768,768]{1,0:T(8,128)(2,1)}, bf16[4,768,768]{2,1,0:T(8,128)(2,1)}, f32[24,768]{1,0:T(8,128)}) custom-call(bf16[336,768]{1,0:T(8,128)(2,1)} %bitcast.59, bf16[16,768,768]{2,1,0:T(8,128)(2,1)} %get-tuple-element.35.weight_ref.refs_2_.refs_3_.cross_w_ref.in_ref.out_ref.refs_6_.refs_7_, ...), custom_call_target="tpu_custom_call" | custom-call | tf_op jit(solution)/shard_map/self_backward/pallas_call | solution.py:612
  160.8 4.9 constant_dynamic-update-slice_fusion.2
  170.2 4.9 constant_dynamic-update-slice_fusion.1
  175.1 2.4 constant_dynamic-update-slice_fusion
  177.5 8.6 %slice.113 = bf16[16,768,384]{2,1,0:T(8,128)(2,1)} slice(bf16[16,768,768]{2,1,0:T(8,128)(2,1)} %constant_dynamic-update-slice_fusion), slice={[0:16], [0:768], [384:768]} | slice | bytes 18874368 | tf_op jit(solution)/shard_map/slice | solution.py:659
  186.5 14.5 %collective-permute-done = bf16[16,768,384]{2,1,0:T(8,128)(2,1)S(1)} collective-permute-done((bf16[16,768,384]{2,1,0:T(8,128)(2,1)}, bf16[16,768,384]{2,1,0:T(8,128)(2,1)S(1)}, u32[]{:S(2)}, u32[]{:S(2)}) %collective-permute-start) | collective-permute-done | bytes 9437216 | tf_op jit(solution)/shard_map/ppermute | solution.py:659
  201.0 8.7 %add_convert_fusion = bf16[16,768,384]{2,1,0:T(8,128)(2,1)} fusion(bf16[16,768,384]{2,1,0:T(8,128)(2,1)S(1)} %collective-permute-done, bf16[16,768,768]{2,1,0:T(8,128)(2,1)} %constant_dynamic-update-slice_fusion), kind=kLoop, calls=%fused_computation.1 | loop fusion | flops 18874368 | bytes 28311552 | tf_op jit(solution)/shard_map/convert_element_type | solution.py:660
  209.8 164.0 %reduce-scatter.2.cloned.1.call-done = bf16[16,192,384]{2,1,0:T(8,128)(2,1)} async-done(((bf16[16,768,384]{2,1,0:T(8,128)(2,1)}), bf16[16,192,384]{2,1,0:T(8,128)(2,1)}) %reduce-scatter.2.cloned.1.call-update) | async-done | bytes 2359312 | tf_op jit(solution)/shard_map/reduce_scatter | solution.py:664
  380.0 1.3 fusion.22
  381.3 3.2 all_gather.21
  396.9 18.3 %psum.29 = f32[1,8,384]{2,1,0:T(8,128)S(1)} all-reduce(f32[1,8,384]{2,1,0:T(8,128)S(1)} %fusion.7), channel_id=1, replica_groups=mesh['task'=4,'dp'=4,'tensor'=2] {'dp'}, use_global_device_ids=true, to_apply=%region_3.4 | all-reduce | flops 3072 | bytes 24576 | tf_op jit(solution)/shard_map/psum | solution.py:663
  415.2 8.5 %all_gather.25 = f32[4,8,384]{2,1,0:T(8,128)S(1)} all-gather(f32[1,8,384]{2,1,0:T(8,128)S(1)} %psum.29), channel_id=1, replica_groups=mesh['task'=4,'dp'=4,'tensor'=2] {'task'}, dimensions={0}, use_global_device_ids=true | all-gather | bytes 61440 | tf_op jit(solution)/shard_map/all_gather | solution.py:666
  424.0 2.5 psum.30
  426.5 46.6 %all-gather.3.cloned.1.call-done = bf16[64,192,384]{2,1,0:T(8,128)(2,1)} async-done(((bf16[16,192,384]{2,1,0:T(8,128)(2,1)}), bf16[64,192,384]{2,1,0:T(8,128)(2,1)}) %all-gather.3.cloned.1.call-update) | async-done | bytes 9437200 | tf_op jit(solution)/shard_map/all_gather | solution.py:665
  473.1 11.1 %gram.1 = f32[16,384]{1,0:T(8,128)} custom-call(bf16[4,16,192,384]{3,2,1,0:T(8,128)(2,1)} %bitcast.54), custom_call_target="tpu_custom_call" | custom-call | tf_op jit(solution)/shard_map/gram/pallas_call | solution.py:670
  486.0 28.8 %all-reduce.5 = (f32[1,9,768]{2,1,0:T(8,128)S(1)}, f32[4,4]{1,0:T(4,128)S(1)}) all-reduce(f32[1,9,768]{2,1,0:T(8,128)S(1)} %maximum_bitcast_fusion, f32[4,4]{1,0:T(4,128)S(1)} %fusion.8), channel_id=1, replica_groups=mesh['task'=4,'dp'=4,'tensor'=2] {'dp','tensor'}, use_global_device_ids=true, to_apply=%region_5.6 | all-reduce | flops 6928 | bytes 55424 | tf_op jit(solution)/shard_map/psum | solution.py:662
  514.8 8.7 %all_gather.27 = f32[4,9,768]{2,1,0:T(8,128)S(1)} all-gather(f32[1,9,768]{2,1,0:T(8,128)S(1)} %get-tuple-element.102), channel_id=1, replica_groups=mesh['task'=4,'dp'=4,'tensor'=2] {'task'}, dimensions={0}, use_global_device_ids=true | all-gather | bytes 138240 | tf_op jit(solution)/shard_map/all_gather | solution.py:667
  523.5 1.4 multiply_reduce_fusion.1
  524.8 1.3 fusion.11
  529.6 2.0 multiply_reduce_fusion.15
  535.0 2.6 multiply_reduce_fusion.14
  541.1 2.0 multiply_reduce_fusion.13
  549.0 7.9 %update.1 = f32[192,16,384]{2,1,0:T(8,128)} custom-call(f32[4]{0:T(128)} %copy-done.9, bf16[4,16,192,384]{3,2,1,0:T(8,128)(2,1)} %bitcast.55), custom_call_target="tpu_custom_call" | custom-call | tf_op jit(solution)/shard_map/update/pallas_call | solution.py:689
  (80 shorter events, 22.4 us)
Async XLA Ops:
  7.2 23.9 %copy-start = (s32[1,6,100]{2,0,1:T(1,128)S(1)}, s32[1,6,100]{2,0,1:T(1,128)}, u32[]{:S(2)}) copy-start(s32[1,6,100]{2,0,1:T(1,128)} %param.13) | copy-start | bytes 7204
  7.2 23.0 %copy-start.8 = (bf16[3,2,768]{2,1,0:T(2,128)(2,1)S(1)}, bf16[3,2,768]{2,1,0:T(2,128)(2,1)}, u32[]{:S(2)}) copy-start(bf16[3,2,768]{2,1,0:T(2,128)(2,1)} %param.18) | copy-start | bytes 27652
  7.2 24.4 %copy-start.12 = (s32[1,6]{1,0:T(1,128)S(1)}, s32[1,6]{1,0:T(1,128)}, u32[]{:S(2)}) copy-start(s32[1,6]{1,0:T(1,128)} %param.14) | copy-start | bytes 76
  7.2 25.0 %copy-start.11 = (bf16[3,768]{1,0:T(4,128)(2,1)S(1)}, bf16[3,768]{1,0:T(4,128)(2,1)}, u32[]{:S(2)}) copy-start(bf16[3,768]{1,0:T(4,128)(2,1)} %param.19) | copy-start | bytes 13828
  7.2 366.6 %reduce-scatter.2.cloned.1.call-start = ((), (), s32[]{:S(2)}) async-start(), calls=%async_computation.1 | async-start | bytes 11796480 | tf_op jit(solution)/shard_map/reduce_scatter | solution.py:664
  160.7 5.0 copy-start.5
  160.7 6.1 %copy-start.4 = (bf16[768,768]{1,0:T(8,128)(2,1)S(1)}, bf16[768,768]{1,0:T(8,128)(2,1)}, u32[]{:S(2)}) copy-start(bf16[768,768]{1,0:T(8,128)(2,1)} %get-tuple-element.54) | copy-start | bytes 3538948
  160.7 7.2 %copy-start.3 = (bf16[768,768]{1,0:T(8,128)(2,1)S(1)}, bf16[768,768]{1,0:T(8,128)(2,1)}, u32[]{:S(2)}) copy-start(bf16[768,768]{1,0:T(8,128)(2,1)} %get-tuple-element.55) | copy-start | bytes 3538948
  160.7 8.3 %copy-start.2 = (bf16[768,768]{1,0:T(8,128)(2,1)S(1)}, bf16[768,768]{1,0:T(8,128)(2,1)}, u32[]{:S(2)}) copy-start(bf16[768,768]{1,0:T(8,128)(2,1)} %get-tuple-element.56) | copy-start | bytes 3538948
  165.7 9.4 %slice-start = ((s8[4718592]{0:T(1024)(128)(4,1)}), s8[4194304]{0:T(1024)(128)(4,1)S(1)}, s32[]{:S(2)}) async-start(s8[4718592]{0:T(1024)(128)(4,1)} %bitcast.56), calls=%async_computation.3 | async-start | bytes 8388608
  169.0 6.1 %slice-start.1 = ((s8[4718592]{0:T(1024)(128)(4,1)}), s8[524288]{0:T(1024)(128)(4,1)S(1)}, s32[]{:S(2)}) async-start(s8[4718592]{0:T(1024)(128)(4,1)} %bitcast.56), calls=%async_computation.4 | async-start | bytes 1048576
  186.2 14.9 %collective-permute-start = (bf16[16,768,384]{2,1,0:T(8,128)(2,1)}, bf16[16,768,384]{2,1,0:T(8,128)(2,1)S(1)}, u32[]{:S(2)}, u32[]{:S(2)}) collective-permute-start(bf16[16,768,384]{2,1,0:T(8,128)(2,1)} %slice.113), channel_id=1, source_target_pairs={{0,1},{1,0},{2,3},{3,2},{4,5},{5,4},{6,7},{7,6},{8,9},{9,8},{10,11... | collective-permute-start | bytes 28311560 | tf_op jit(solution)/shard_map/ppermute | solution.py:659
  209.7 168.1 %copy-start.7 = (bf16[336,768]{1,0:T(8,128)(2,1)S(1)}, bf16[336,768]{1,0:T(8,128)(2,1)}, u32[]{:S(2)}) copy-start(bf16[336,768]{1,0:T(8,128)(2,1)} %get-tuple-element.40) | copy-start | bytes 1548292
  209.7 168.3 %copy-start.10 = (s32[4]{0:T(128)S(1)}, s32[4]{0:T(128)}, u32[]{:S(2)}) copy-start(s32[4]{0:T(128)} %param.15) | copy-start | bytes 52
  209.7 185.2 %copy-start.6 = (bf16[336,768]{1,0:T(8,128)(2,1)S(1)}, bf16[336,768]{1,0:T(8,128)(2,1)}, u32[]{:S(2)}) copy-start(bf16[336,768]{1,0:T(8,128)(2,1)} %get-tuple-element.50) | copy-start | bytes 1548292
  209.8 263.4 %all-gather.3.cloned.1.call-start = ((), (), s32[]{:S(2)}) async-start(), calls=%async_computation.2 | async-start | bytes 11796480 | tf_op jit(solution)/shard_map/all_gather | solution.py:665
  376.2 20.7 %collective-permute-start.1 = (f32[8,384]{1,0:T(8,128)S(1)}, f32[8,384]{1,0:T(8,128)S(1)}, u32[]{:S(2)}, u32[]{:S(2)}) collective-permute-start(f32[8,384]{1,0:T(8,128)S(1)} %slice.115), channel_id=1, source_target_pairs={{0,1},{1,0},{2,3},{3,2},{4,5},{5,4},{6,7},{7,6},{8,9},{9,8},{10,11... | collective-permute-start | bytes 36872 | tf_op jit(solution)/shard_map/ppermute | solution.py:661
  473.1 85.1 %copy-start.1 = (s32[1,6,100]{2,0,1:T(1,128)S(1)}, s32[1,6,100]{2,0,1:T(1,128)}, u32[]{:S(2)}) copy-start(s32[1,6,100]{2,0,1:T(1,128)} %param.13) | copy-start | bytes 7204
  547.8 1.2 copy-start.9
Sparse Core Ops, SparseCore 0:
  209.9 163.8 reduce-scatter.1
  375.6 97.4 all-gather.2

commit v2 on v1

--- a/solution.py
+++ b/solution.py
@@ -405,6 +405,569 @@
     small_ref[0:1] = rows_sum(qkv_grad[0].astype(F32))
     small_ref[1:2] = rows_sum(qkv_grad[2].astype(F32))
     query_grad_ref[...] = total.astype(BF)
+
+
+def task_peers(tasks):
+    me = lax.axis_index("task")
+    return [lax.rem(me + shift, tasks) for shift in range(1, tasks)]
+
+
+def task_senders(tasks):
+    me = lax.axis_index("task")
+    return [lax.rem(me + tasks - shift, tasks) for shift in range(1, tasks)]
+
+
+def send(source, target, send_sem, recv_sem, **device):
+    return pltpu.make_async_remote_copy(
+        source, target, send_sem, recv_sem, device_id=device, device_id_type=MESH_ID
+    )
+
+
+def greet(depth, tasks):
+    me = lax.axis_index("dp")
+    barrier = pltpu.get_barrier_semaphore()
+    for peer in task_peers(tasks):
+        pl.semaphore_signal(barrier, inc=1, device_id={"task": peer}, device_id_type=MESH_ID)
+    for shift in range(1, depth):
+        pl.semaphore_signal(
+            barrier, inc=1, device_id={"dp": lax.rem(me + shift, depth)}, device_id_type=MESH_ID
+        )
+    pl.semaphore_signal(
+        barrier, inc=1, device_id={"tensor": 1 - lax.axis_index("tensor")}, device_id_type=MESH_ID
+    )
+    pl.semaphore_wait(barrier, tasks + depth - 1)
+
+
+class Chain:
+    def __init__(self, depth, tasks, near, far, passed, parts, sems):
+        self.depth, self.tasks = depth, tasks
+        self.near, self.far, self.passed, self.parts = near, far, passed, parts
+        (self.near_sem, self.far_send, self.far_recv, self.pass_send, self.pass_recv,
+         self.part_send, self.part_recv) = sems
+        self.chunks = passed.shape[1]
+        self.rows, self.half = passed.shape[2:]
+        self.me = lax.axis_index("dp")
+        self.task = lax.axis_index("task")
+        self.is_end = (self.me == 0) | (self.me == depth - 1)
+
+    @staticmethod
+    def scratch(blocks, rows, half, tasks):
+        chunks = 2 * blocks
+        return [
+            pltpu.VMEM((2, blocks, 2 * rows, half), BF),
+            pltpu.VMEM((2, blocks, 2 * rows, half), BF),
+            pltpu.VMEM((2, chunks, rows, half), BF),
+            pltpu.VMEM((tasks, chunks, rows // tasks, half), BF),
+            pltpu.SemaphoreType.DMA((2, blocks)),
+            pltpu.SemaphoreType.DMA((2, blocks)),
+            pltpu.SemaphoreType.DMA((2, blocks)),
+            pltpu.SemaphoreType.DMA((2, chunks, 2)),
+            pltpu.SemaphoreType.DMA((2, chunks, 2)),
+            pltpu.SemaphoreType.DMA((chunks, tasks - 1)),
+            pltpu.SemaphoreType.DMA((chunks, tasks - 1)),
+        ]
+
+    def near_copy(self, source, way, block):
+        return pltpu.make_async_copy(
+            source, self.near.at[way, block], self.near_sem.at[way, block]
+        )
+
+    def far_copy(self, source, way, block):
+        return send(
+            source, self.far.at[way, block], self.far_send.at[way, block],
+            self.far_recv.at[way, block], tensor=1 - lax.axis_index("tensor"),
+        )
+
+    def load(self, block, source):
+        for way in range(2):
+            rows = pl.ds(way * 2 * self.rows, 2 * self.rows)
+            self.near_copy(source.at[rows, pl.ds(0, self.half)], way, block).start()
+            self.far_copy(source.at[rows, pl.ds(self.half, self.half)], way, block).start()
+
+    def pass_copy(self, way, chunk, sub):
+        rows = pl.ds(sub * (self.rows // 2), self.rows // 2)
+        piece = self.passed.at[way, chunk, rows]
+        target = self.me - 1 if way == 0 else self.me + 1
+        return send(
+            piece, piece, self.pass_send.at[way, chunk, sub], self.pass_recv.at[way, chunk, sub],
+            dp=target,
+        )
+
+    def part_rows(self, peer):
+        size = self.rows // self.tasks
+        return pl.ds(pl.multiple_of(peer * size, size), size)
+
+    def part_copy(self, way, chunk, shift, peer):
+        return send(
+            self.passed.at[way, chunk, self.part_rows(peer)], self.parts.at[self.task, chunk],
+            self.part_send.at[chunk, shift], self.part_recv.at[chunk, shift], task=peer,
+        )
+
+    def lag(self, way):
+        return self.depth - 1 - self.me if way == 0 else self.me
+
+    def steps(self):
+        return self.chunks + self.depth - 1
+
+    def step(self, index):
+        for way in range(2):
+            chunk = index - self.lag(way)
+
+            @pl.when((chunk >= 0) & (chunk < self.chunks))
+            def _(way=way, chunk=chunk):
+                self.chunk_step(way, chunk)
+
+    def chunk_step(self, way, chunk):
+        block = chunk // 2
+        part = chunk - 2 * block
+        first, last = self.lag(way) == 0, self.lag(way) == self.depth - 1
+
+        @pl.when(part == 0)
+        def _():
+            piece = self.near.at[way, block]
+            self.near_copy(piece, way, block).wait()
+            self.far_copy(piece, way, block).wait_recv()
+
+        sub_rows = self.rows // 2
+        for sub in range(2):
+            at = pl.ds(pl.multiple_of(part * self.rows + sub * sub_rows, sub_rows), sub_rows)
+            rows = pl.ds(sub * sub_rows, sub_rows)
+
+            def own():
+                return self.near[way, block, at].astype(F32) + self.far[way, block, at].astype(F32)
+
+            @pl.when(first)
+            def _():
+                self.passed[way, chunk, rows] = own().astype(BF)
+
+            @pl.when(jnp.logical_not(first))
+            def _():
+                self.pass_copy(way, chunk, sub).wait_recv()
+                self.passed[way, chunk, rows] = (
+                    own() + self.passed[way, chunk, rows].astype(F32)
+                ).astype(BF)
+
+            @pl.when(jnp.logical_not(last))
+            def _():
+                self.pass_copy(way, chunk, sub).start()
+
+        @pl.when(last)
+        def _():
+            for shift, peer in enumerate(task_peers(self.tasks)):
+                self.part_copy(way, chunk, shift, peer).start()
+            self.parts[self.task, chunk] = self.passed[way, chunk, self.part_rows(self.task)]
+
+    def wait_parts(self, chunk):
+        for shift, peer in enumerate(task_senders(self.tasks)):
+            landed = self.parts.at[peer, chunk]
+            send(
+                landed, landed, self.part_send.at[chunk, shift], self.part_recv.at[chunk, shift],
+                task=peer,
+            ).wait_recv()
+
+    def finish(self):
+        def blocks(block, carry):
+            for way in range(2):
+                self.far_copy(self.near.at[way, block], way, block).wait_send()
+            return carry
+
+        lax.fori_loop(0, self.chunks // 2, blocks, 0)
+
+        def chunks(chunk, carry):
+            for way in range(2):
+
+                @pl.when(self.lag(way) != self.depth - 1)
+                def _(way=way):
+                    for sub in range(2):
+                        self.pass_copy(way, chunk, sub).wait_send()
+
+                @pl.when(self.lag(way) == self.depth - 1)
+                def _(way=way):
+                    for shift, peer in enumerate(task_peers(self.tasks)):
+                        self.part_copy(way, chunk, shift, peer).wait_send()
+
+            return carry
+
+        lax.fori_loop(0, self.chunks, chunks, 0)
+
+
+def pairs_of(tasks):
+    return [(a, b) for a in range(tasks) for b in range(a, tasks)]
+
+
+def weights_of(gram, order_ref, tasks):
+    totals = [0.0] * tasks
+    for own in range(tasks):
+        coeffs = [jnp.full_like(gram[0, 0], 1.0 if t == own else 0.0) for t in range(tasks)]
+        for position in range(tasks):
+            chosen = [
+                jnp.where(order_ref[position] == t, 1.0, 0.0).astype(F32) for t in range(tasks)
+            ]
+            column = [sum(gram[t, j] * chosen[j] for j in range(tasks)) for t in range(tasks)]
+            inner = sum(coeffs[t] * column[t] for t in range(tasks))
+            square = sum(chosen[t] * column[t] for t in range(tasks))
+            others = 1.0 - chosen[own]
+            share = others * jnp.minimum(inner, 0.0) / (square + 1e-06)
+            coeffs = [coeffs[t] - share * chosen[t] for t in range(tasks)]
+        totals = [total + coeff for total, coeff in zip(totals, coeffs)]
+    return totals
+
+
+GROUPS = 4
+
+
+def reduce_kernel(depth, tasks, layout, order_ref, small_ref, *refs):
+    sources, refs = refs[: len(layout)], refs[len(layout) :]
+    (update_ref, small_out_ref, gram_ref), refs = refs[:3], refs[3:]
+    chain = Chain(depth, tasks, *refs[:4], refs[4:11])
+    (
+        small_far, small_pass, small_all, small_both, gram_acc, gram_task, gram_core, gram_end,
+        hop, out,
+        small_far_sem, small_pass_sem, small_task_sem, small_dp_sem, small_core_sem,
+        gram_task_sem, gram_core_sem, gram_dp_sem, hop_sem, out_sem,
+    ) = refs[11:]
+    me, task, core = (lax.axis_index(axis) for axis in ("dp", "task", "tensor"))
+    half = chain.half
+    is_end = chain.is_end
+    top = me == 0
+    greet(depth, tasks)
+    small_copy = send(
+        small_ref.at[:, pl.ds(half, half)], small_far, small_far_sem.at[0], small_far_sem.at[1],
+        tensor=1 - core,
+    )
+    small_copy.start()
+    for index, (source, blocks) in enumerate(zip(sources, layout)):
+        base = sum(len(entry) for entry in layout[:index])
+        for block in range(len(blocks)):
+            chain.load(base + block, source.at[block])
+    block_order = [block for blocks in layout for block in blocks]
+
+    def small_hop():
+        return send(
+            small_pass, small_pass, small_pass_sem.at[0], small_pass_sem.at[1], dp=me - 1
+        )
+
+    def small_task_copy(shift, peer):
+        return send(
+            small_pass, small_all.at[task], small_task_sem.at[0, shift],
+            small_task_sem.at[1, shift], task=peer,
+        )
+
+    gram_acc[...] = jnp.zeros_like(gram_acc)
+    pairs = pairs_of(tasks)
+
+    def add_products(shares):
+        for index, (a, b) in enumerate(pairs):
+            product = shares[a] * shares[b]
+            total = product[0:8]
+            for row in range(8, product.shape[0], 8):
+                total = total + product[row : row + 8]
+            gram_acc[index * 8 : index * 8 + 8] += total
+
+    def step(index, carry):
+        chain.step(index)
+
+        @pl.when(index == chain.lag(0))
+        def _():
+            small_copy.wait_recv()
+            total = small_ref[:, pl.ds(0, half)] + small_far[...]
+
+            @pl.when(me == depth - 1)
+            def _():
+                small_pass[...] = total
+
+            @pl.when(me < depth - 1)
+            def _():
+                small_hop().wait_recv()
+                small_pass[...] += total
+
+            @pl.when(me > 0)
+            def _():
+                small_hop().start()
+
+            @pl.when(top)
+            def _():
+                for shift, peer in enumerate(task_peers(tasks)):
+                    small_task_copy(shift, peer).start()
+                small_all[task] = small_pass[...]
+
+        landed = index - (depth - 1) - 2
+
+        @pl.when(is_end & (landed >= 0))
+        def _():
+            chain.wait_parts(landed)
+            add_products([chain.parts[t, landed].astype(F32) for t in range(tasks)])
+
+        return carry
+
+    lax.fori_loop(0, chain.steps() + 2, step, 0)
+
+    @pl.when(top)
+    def _():
+        for shift, peer in enumerate(task_senders(tasks)):
+            landed = small_all.at[peer]
+            send(
+                landed, landed, small_task_sem.at[0, shift], small_task_sem.at[1, shift], task=peer
+            ).wait_recv()
+
+    lanes = gram_task.shape[2]
+
+    def gram_task_copy(shift, peer):
+        return send(
+            gram_task.at[task], gram_task.at[task], gram_task_sem.at[0, shift],
+            gram_task_sem.at[1, shift], task=peer,
+        )
+
+    def gram_core_copy(which):
+        return send(
+            gram_core.at[which], gram_core.at[which], gram_core_sem.at[0], gram_core_sem.at[1],
+            tensor=1 - core,
+        )
+
+    def gram_dp_copy(end, shift):
+        return send(
+            gram_end.at[end], gram_end.at[end], gram_dp_sem.at[0, end, shift],
+            gram_dp_sem.at[1, end, shift], dp=lax.rem((depth - 1) * end + shift + 1, depth),
+        )
+
+    def one_number(values):
+        return jnp.sum(jnp.sum(values, axis=0, keepdims=True), axis=1, keepdims=True)
+
+    @pl.when(is_end)
+    def _():
+        gram_task[task] = jnp.zeros(gram_task.shape[1:], F32)
+        for index in range(len(pairs)):
+            gram_task[task, index : index + 1] = jnp.broadcast_to(
+                one_number(gram_acc[index * 8 : index * 8 + 8]), (1, lanes)
+            )
+        for shift, peer in enumerate(task_peers(tasks)):
+            gram_task_copy(shift, peer).start()
+
+    @pl.when(top)
+    def _():
+        small_all_values = [small_all[t] for t in range(tasks)]
+        for index, (a, b) in enumerate(pairs):
+            gram_end[0, index : index + 1] = jnp.broadcast_to(
+                one_number(small_all_values[a] * small_all_values[b]), (1, lanes)
+            )
+
+    @pl.when(is_end)
+    def _():
+        for shift, peer in enumerate(task_senders(tasks)):
+            landed = gram_task.at[peer]
+            send(
+                landed, landed, gram_task_sem.at[0, shift], gram_task_sem.at[1, shift], task=peer
+            ).wait_recv()
+        total = gram_task[0]
+        for t in range(1, tasks):
+            total = total + gram_task[t]
+
+        @pl.when(top)
+        def _():
+            gram_core[core] = total + gram_end[0]
+
+        @pl.when(jnp.logical_not(top))
+        def _():
+            gram_core[core] = total
+
+        gram_core_copy(core).start()
+        gram_core_copy(1 - core).wait_recv()
+
+    for end in range(2):
+
+        @pl.when(me == (depth - 1) * end)
+        def _(end=end):
+            gram_end[end] = gram_core[0] + gram_core[1]
+            for shift in range(depth - 1):
+                gram_dp_copy(end, shift).start()
+
+    for end in range(2):
+        for shift in range(depth - 1):
+
+            @pl.when(me == ((depth - 1) * end + shift + 1) % depth)
+            def _(end=end, shift=shift):
+                gram_dp_copy(end, shift).wait_recv()
+
+    gram = {}
+    for index, (a, b) in enumerate(pairs):
+        row = slice(index, index + 1)
+        gram[a, b] = gram[b, a] = gram_end[0, row] + gram_end[1, row]
+    for a in range(tasks):
+        for b in range(tasks):
+            gram_ref[a * tasks + b : a * tasks + b + 1] = gram[a, b]
+    weights = [
+        jnp.concatenate([weight] * (half // lanes), axis=1)
+        for weight in weights_of(gram, order_ref, tasks)
+    ]
+
+    blocks = chain.chunks // 2
+    group = blocks // GROUPS
+    share = chain.rows // tasks
+    mine = pl.ds(pl.multiple_of(task * share, share), share)
+    own_part = jnp.minimum(me, 1)
+
+    def hop_copy(index):
+        return send(
+            hop.at[pl.ds(index * group, group)], out.at[pl.ds(index * group, group), mine],
+            hop_sem.at[0, index], hop_sem.at[1, index],
+            dp=jnp.where(top, 1, depth - 2),
+        )
+
+    def out_copy(index, shift, peer):
+        piece = out.at[pl.ds(index * group, group), mine]
+        return send(piece, piece, out_sem.at[0, index, shift], out_sem.at[1, index, shift], task=peer)
+
+    def weighted(chunk):
+        total = weights[0] * chain.parts[0, chunk].astype(F32)
+        for t in range(1, tasks):
+            total = total + weights[t] * chain.parts[t, chunk].astype(F32)
+        return total.astype(BF)
+
+    def small_dp_copy(shift):
+        return send(
+            small_both.at[0], small_both.at[0], small_dp_sem.at[0, shift],
+            small_dp_sem.at[1, shift], dp=shift + 1,
+        )
+
+    def small_core_copy():
+        return send(
+            small_both.at[0], small_both.at[1], small_core_sem.at[0], small_core_sem.at[1],
+            tensor=1 - core,
+        )
+
+    @pl.when(top)
+    def _():
+        total = weights[0] * small_all[0]
+        for t in range(1, tasks):
+            total = total + weights[t] * small_all[t]
+        small_both[0] = total
+        for shift in range(depth - 1):
+            small_dp_copy(shift).start()
+
+    @pl.when(is_end)
+    def _():
+        for index in range(GROUPS):
+
+            def other(block, carry):
+                hop[block] = weighted(2 * block + 1 - own_part)
+                return carry
+
+            lax.fori_loop(index * group, (index + 1) * group, other, 0)
+            hop_copy(index).start()
+
+            def own(block, carry):
+                out[block, mine] = weighted(2 * block + own_part)
+                return carry
+
+            lax.fori_loop(index * group, (index + 1) * group, own, 0)
+            for shift, peer in enumerate(task_peers(tasks)):
+                out_copy(index, shift, peer).start()
+
+    @pl.when(jnp.logical_not(is_end))
+    def _():
+        for index in range(GROUPS):
+            hop_copy(index).wait_recv()
+            for shift, peer in enumerate(task_peers(tasks)):
+                out_copy(index, shift, peer).start()
+
+    for shift in range(depth - 1):
+
+        @pl.when(me == shift + 1)
+        def _(shift=shift):
+            small_dp_copy(shift).wait_recv()
+
+    small_core_copy().start()
+
+    for index in range(GROUPS):
+        for shift, peer in enumerate(task_senders(tasks)):
+            piece = out.at[
+                pl.ds(index * group, group), pl.ds(pl.multiple_of(peer * share, share), share)
+            ]
+            send(
+                piece, piece, out_sem.at[0, index, shift], out_sem.at[1, index, shift], task=peer
+            ).wait_recv()
+        for block in range(index * group, (index + 1) * group):
+            update_ref[:, block_order[block], :] = out[block].astype(F32)
+
+    small_core_copy().wait_recv()
+    small_out_ref[...] = small_both[...]
+
+    small_copy.wait_send()
+    small_core_copy().wait_send()
+    chain.finish()
+
+    @pl.when(me > 0)
+    def _():
+        small_hop().wait_send()
+
+    @pl.when(top)
+    def _():
+        for shift, peer in enumerate(task_peers(tasks)):
+            small_task_copy(shift, peer).wait_send()
+        for shift in range(depth - 1):
+            small_dp_copy(shift).wait_send()
+
+    for end in range(2):
+
+        @pl.when(me == (depth - 1) * end)
+        def _(end=end):
+            for shift in range(depth - 1):
+                gram_dp_copy(end, shift).wait_send()
+
+    @pl.when(is_end)
+    def _():
+        gram_core_copy(core).wait_send()
+        for shift, peer in enumerate(task_peers(tasks)):
+            gram_task_copy(shift, peer).wait_send()
+        for index in range(GROUPS):
+            hop_copy(index).wait_send()
+
+    for index in range(GROUPS):
+        for shift, peer in enumerate(task_peers(tasks)):
+            out_copy(index, shift, peer).wait_send()
+
+
+def reduce_by_chain(order, small, sources, layout, depth, tasks, half):
+    blocks = sum(len(entry) for entry in layout)
+    rows = sources[0].shape[1] // 4
+    pair_rows = 8 * len(pairs_of(tasks))
+    dma = pltpu.SemaphoreType.DMA
+    return pl.pallas_call(
+        functools.partial(reduce_kernel, depth, tasks, layout),
+        out_shape=(
+            jax.ShapeDtypeStruct((rows, blocks, half), F32),
+            jax.ShapeDtypeStruct((2, *small.shape[:1], half), F32),
+            jax.ShapeDtypeStruct((16, 128), F32),
+        ),
+        in_specs=[pl.BlockSpec(memory_space=pltpu.SMEM), whole_spec()]
+        + [any_spec()] * len(sources),
+        out_specs=(whole_spec(), whole_spec(), whole_spec()),
+        scratch_shapes=Chain.scratch(blocks, rows, half, tasks)
+        + [
+            pltpu.VMEM((small.shape[0], half), F32),
+            pltpu.VMEM((small.shape[0], half), F32),
+            pltpu.VMEM((tasks, small.shape[0], half), F32),
+            pltpu.VMEM((2, small.shape[0], half), F32),
+            pltpu.VMEM((pair_rows, half), F32),
+            pltpu.VMEM((tasks, 16, 128), F32),
+            pltpu.VMEM((2, 16, 128), F32),
+            pltpu.VMEM((2, 16, 128), F32),
+            pltpu.VMEM((blocks, rows // tasks, half), BF),
+            pltpu.VMEM((blocks, rows, half), BF),
+            dma((2,)),
+            dma((2,)),
+            dma((2, tasks - 1)),
+            dma((2, depth - 1)),
+            dma((2,)),
+            dma((2, tasks - 1)),
+            dma((2,)),
+            dma((2, 2, depth - 1)),
+            dma((2, GROUPS)),
+            dma((2, GROUPS, tasks - 1)),
+        ],
+        compiler_params=params_for(collective_id=1, has_side_effects=True),
+        name="reduce",
+    )(order, small, *sources)
 
 
 def gram_kernel(parts_ref, gram_ref):
@@ -638,13 +1201,39 @@
     query_grad = unpad(token_grad)
     memory_grad = context_grad[None]
 
+    def by_halves(array):
+        halves = array.reshape(array.shape[0], cores, half)
+        return jnp.where(core == 0, halves, halves[:, ::-1]).reshape(array.shape)
+
     small = jnp.concatenate(
         [
             self_small[0:2], cross_small[0:2], ffn_small[4:8],
-            self_small[2:4], ffn_small[10:14], self_small[4:5], ffn_small[15:17],
+            by_halves(
+                jnp.concatenate(
+                    [self_small[2:4], ffn_small[10:14], self_small[4:5], ffn_small[15:17]], axis=0
+                )
+            ),
+            jnp.zeros((7, width), F32),
         ],
         axis=0,
     )
+    depth, tasks = lax.axis_size("dp"), lax.axis_size("task")
+    if depth == 4 and tasks == 4 and cores == 2:
+        param_update, small_update, gram_rows = reduce_by_chain(
+            task_order, small,
+            [grad_in, grad_out, self_wg, cross_query_wg[None], key_wg[None], value_wg[None],
+             cross_out_wg[None]],
+            [range(8, 8 + blocks), range(8 + blocks, block_count), range(4), [4], [5], [6], [7]],
+            depth, tasks, half,
+        )
+        row_update = by_halves(
+            jnp.concatenate([small_update[0, 8:17], small_update[1, 8:17]], axis=1)
+        )
+        return (
+            block_out, query_grad, memory_grad, param_update, small_update[0, :8],
+            row_update[:6].reshape(3, 2, width), row_update[6:9],
+            gram_rows[: tasks * tasks, 0].reshape(tasks, tasks),
+        )
     grads = jnp.concatenate(
         [
             self_wg,
@@ -659,7 +1248,7 @@
         grads[:, :, :half].astype(F32) + lax.ppermute(grads[:, :, half:], "tensor", swap).astype(F32)
     ).astype(BF)
     head_small = small[:8, :half] + lax.ppermute(small[:8, half:], "tensor", swap)
-    row_small = lax.psum(small[8:], ("dp", "tensor"))
+    row_small = lax.psum(by_halves(small[8:17]), ("dp", "tensor"))
     head_small = lax.psum(head_small, "dp")
     shard = lax.psum_scatter(grads, "dp", scatter_dimension=1, tiled=True)
     all_shards = lax.all_gather(shard, "task", axis=0, tiled=False)

time: 573 us -> 364 us (0.64)
  the two profiles are of different devices: /device:TPU:0 before, /device:TPU:8 now
where the time goes in v2:
time: 364 us; the launch traced here: 362 us
  Pallas kernels  334 us (92%)
  local copies, waits for them, and re-layouts  21.9 us (6%)
    pallas_call x1, Pallas kernels, reduce_by_chain(): pl.pallas_call(functools.partial(reduce_kernel, depth, tasks, layout), ou...  190 us
    pallas_call x1, Pallas kernels, body(): pl.pallas_call(with_start(cross_back_kernel), grid_spec=pltpu.PrefetchSca...  51.8 us
    pallas_call x1, Pallas kernels, body(): pl.pallas_call(with_start(cross_kernel), grid_spec=pltpu.PrefetchScalarGr...  25.5 us
    pallas_call x1, Pallas kernels, body(): pl.pallas_call(functools.partial(ffn_kernel, images, blocks), grid=(2 * b...  25.2 us
    pallas_call x1, Pallas kernels, body(): pl.pallas_call(gather_kernel, grid=(width // chunk,), out_shape=(jax.Shap...  16.7 us
    pallas_call x1, Pallas kernels, body(): pl.pallas_call(functools.partial(self_back_kernel, images, valid), grid=(...  16.2 us
    pallas_call x1, Pallas kernels, body(): pl.pallas_call(functools.partial(self_kernel, images, valid), grid=(1,),...  8.84 us

profile of v2, /device:TPU:8, one launch (start us, length us, event | category | flops | bytes accessed | tf_op | source)
XLA Modules:
  0.0 362.4 jit_solution(18117889087259119836)
XLA Ops:
  0.7 1.3 reshape_squeeze.10
  2.0 1.3 reshape_squeeze.9
  3.4 0.8 pad.23
  4.2 0.6 pad.24.bias_ref
  4.8 16.7 %gather_weights.1 = (bf16[16,768,768]{2,1,0:T(8,128)(2,1)}, bf16[16,768]{1,0:T(8,128)(2,1)}) custom-call(bf16[768,16,384]{2,1,0:T(8,128)(2,1)} %own_ref.1, bf16[16,384]{1,0:T(8,128)(2,1)} %pad.24.bias_ref), custom_call_target="tpu_custom_call" | custom-call | tf_op jit(solution)/shard_map/gather_weights/pallas_call | solution.py:1027
  21.5 1.4 convert_element_type.14.head_ref.refs_4_
  22.9 0.6 pad_convert_fusion
  23.5 8.8 %self_forward.1 = (bf16[3,336,768]{2,1,0:T(8,128)(2,1)}, bf16[336,768]{1,0:T(8,128)(2,1)}, f32[9,8,448]{2,1,0:T(8,128)}, f32[336,768]{1,0:T(8,128)}, bf16[336,768]{1,0:T(8,128)(2,1)}) custom-call(bf16[336,768]{1,0:T(8,128)(2,1)} %bitcast.27, bf16[16,768,768]{2,1,0:T(8,128)(2,1)} %get-tuple-element.38.weight_ref.refs_2_.refs_3_.cross_w_ref.in_ref.out_ref.refs_6_.refs_7_, ...), custom_call_target="tpu_custom_call" | custom-call | tf_op jit(solution)/shard_map/self_forward/pallas_call | solution.py:1064
  32.3 25.5 %cross_forward.1 = (bf16[3600,768]{1,0:T(8,128)(2,1)}, bf16[3600,768]{1,0:T(8,128)(2,1)}, bf16[336,768]{1,0:T(8,128)(2,1)}, f32[9,8,448]{2,1,0:T(8,128)}) custom-call(s32[1]{0:T(128)} %bitcast.1.start_ref, bf16[7200,768]{1,0:T(8,128)(2,1)} %bitcast.25, bf16[336,768]{1,0:T(8,128)(2,1)} %get-tuple-element.41.refs_1_, ...), custom_call_target="tpu_custom_call" | custom-call | tf_op jit(solution)/shard_map/cross_forward/pallas_call | solution.py:1092
  57.8 0.9 pad.29
  58.7 0.6 dynamic-slice_bitcast_fusion.matches_ref
  59.2 0.6 fusion.counts_ref
  59.8 25.2 %ffn.1 = (bf16[336,768]{1,0:T(8,128)(2,1)}, bf16[4,768,768]{2,1,0:T(8,128)(2,1)}, bf16[4,768,768]{2,1,0:T(8,128)(2,1)}, bf16[768,768]{1,0:T(8,128)(2,1)}, bf16[3...) custom-call(f32[336,768]{1,0:T(8,128)} %get-tuple-element.40.sum_ref, ...), custom_call_target="tpu_custom_call" | custom-call | tf_op jit(solution)/shard_map/ffn/pallas_call | solution.py:1110
  85.0 51.8 %cross_backward.1 = (bf16[336,768]{1,0:T(8,128)(2,1)}, bf16[3600,768]{1,0:T(8,128)(2,1)}, bf16[768,768]{1,0:T(8,128)(2,1)}, bf16[768,768]{1,0:T(8,128)(2,1)}, f32[24,768]{1,0:T(8,128)}) custom-call(s32[1]{0:T(128)} %bitcast.1.start_ref, bf16[7200,768]{1,0:T(8,128)(2,1)} %bitcast.26, bf16[336,768]{1,0:T(8,128)(2,1)} %get-tuple-element.41.refs_1_, ...), custom_call_target="tpu_custom_call" | custom-call | tf_op jit(solution)/shard_map/cross_backward/pallas_call | solution.py:1150
  136.8 16.2 %self_backward.1 = (bf16[336,768]{1,0:T(8,128)(2,1)}, bf16[768,768]{1,0:T(8,128)(2,1)}, bf16[4,768,768]{2,1,0:T(8,128)(2,1)}, f32[24,768]{1,0:T(8,128)}) custom-call(bf16[336,768]{1,0:T(8,128)(2,1)} %bitcast.28, bf16[16,768,768]{2,1,0:T(8,128)(2,1)} %get-tuple-element.38.weight_ref.refs_2_.refs_3_.cross_w_ref.in_ref.out_ref.refs_6_.refs_7_, ...), custom_call_target="tpu_custom_call" | custom-call | tf_op jit(solution)/shard_map/self_backward/pallas_call | solution.py:1175
  153.0 0.8 fusion.1
  153.8 0.7 slice.56
  154.6 0.8 fusion.2
  155.3 0.8 slice.57
  156.3 0.7 slice.52
  157.0 2.6 concatenate.15.small_ref
  159.6 190.2 %reduce.3 = (f32[192,16,384]{2,1,0:T(8,128)}, f32[2,24,384]{2,1,0:T(8,128)}, f32[16,128]{1,0:T(8,128)}) custom-call(s32[4]{0:T(128)} %order_ref.1, f32[24,768]{1,0:T(8,128)} %concatenate.15.small_ref, bf16[4,768,768]{2,1,0:T(8,128)(2,1)} %get-tuple-element.58.refs_0_, bf16[4,768,768]{2,1,0:T(8,128)(2,1)} %get-tuple-element.59.refs_1_, ...), custom_call_target="tpu_custom_call" | custom-call | tf_op jit(solution)/shard_map/reduce/pallas_call | solution.py:935
  349.9 0.8 slice_bitcast_fusion.1
  350.7 0.6 reshape.72
  351.3 0.6 slice.68
  351.9 1.3 slice_bitcast_fusion.2
  353.2 0.8 slice_reduce_fusion
  354.0 0.7 reshape_squeeze.11
  354.7 0.8 reshape.69
  355.9 3.3 all_gather.3
  359.1 1.1 copy.33
  360.2 2.2 copy.36
  (35 shorter events, 0.6 us)
Async XLA Ops:
  0.6 58.0 %copy-start = (s32[1,6,100]{2,0,1:T(1,128)S(1)}, s32[1,6,100]{2,0,1:T(1,128)}, u32[]{:S(2)}) copy-start(s32[1,6,100]{2,0,1:T(1,128)} %param.13) | copy-start | bytes 7204
  0.7 3.5 copy-start.7
  4.8 18.0 %copy-start.5 = (bf16[3,2,768]{2,1,0:T(2,128)(2,1)S(1)}, bf16[3,2,768]{2,1,0:T(2,128)(2,1)}, u32[]{:S(2)}) copy-start(bf16[3,2,768]{2,1,0:T(2,128)(2,1)} %param.18) | copy-start | bytes 27652
  4.8 18.0 %copy-start.6 = (bf16[3,768]{1,0:T(4,128)(2,1)S(1)}, bf16[3,768]{1,0:T(4,128)(2,1)}, u32[]{:S(2)}) copy-start(bf16[3,768]{1,0:T(4,128)(2,1)} %param.19) | copy-start | bytes 13828
  32.3 26.9 %copy-start.8 = (s32[1,6]{1,0:T(1,128)S(1)}, s32[1,6]{1,0:T(1,128)}, u32[]{:S(2)}) copy-start(s32[1,6]{1,0:T(1,128)} %param.14) | copy-start | bytes 76
  159.6 195.1 %copy-start.4 = (bf16[336,768]{1,0:T(8,128)(2,1)S(1)}, bf16[336,768]{1,0:T(8,128)(2,1)}, u32[]{:S(2)}) copy-start(bf16[336,768]{1,0:T(8,128)(2,1)} %get-tuple-element.53) | copy-start | bytes 1548292
  159.6 196.0 %copy-start.3 = (bf16[336,768]{1,0:T(8,128)(2,1)S(1)}, bf16[336,768]{1,0:T(8,128)(2,1)}, u32[]{:S(2)}) copy-start(bf16[336,768]{1,0:T(8,128)(2,1)} %get-tuple-element.43) | copy-start | bytes 1548292
  355.9 4.3 %copy-start.2 = (f32[192,16,384]{2,1,0:T(8,128)S(1)}, f32[192,16,384]{2,1,0:T(8,128)}, u32[]{:S(2)}) copy-start(f32[192,16,384]{2,1,0:T(8,128)} %get-tuple-element.105) | copy-start | bytes 14155780
  359.1 3.3 copy-start.1

commit v3 on v2

--- a/solution.py
+++ b/solution.py
@@ -14,7 +14,7 @@
 F32 = jnp.float32
 MESH_ID = pl.DeviceIdType.MESH
 highest = lax.Precision.HIGHEST
-VMEM_LIMIT = 60 * 2**20
+VMEM_LIMIT = 62 * 2**20
 
 
 def combine_weights(gram_matrix, order_list):
@@ -309,82 +309,100 @@
         mixed_grad_ref[...] = mm(cross_low, cross_w_ref[0]).astype(BF)
 
 
+def cross_back_step(
+    image, group, images, groups, context_ref, query_ref, key_ref, value_ref, total_ref,
+    mixed_grad_ref, key_w_ref, value_w_ref, context_grad_ref, small_ref, context_t, acc, key_acc,
+    value_acc, unit,
+):
+    @pl.when(group == 0)
+    def _():
+        context_t[...] = context_ref[...].T
+
+    unit(0)
+    grad_query, grad_key, grad_value = attend_back(
+        query_ref[...], key_ref[...], value_ref[...], total_ref[0, 0:1], mixed_grad_ref[...],
+        key_ref.shape[0],
+    )
+    lanes = pl.ds(pl.multiple_of(group * SLAB, SLAB), SLAB)
+    small_ref[2:3, lanes] += rows_sum(grad_query.astype(F32))
+    small_ref[3:4, lanes] += rows_sum(grad_value.astype(F32))
+    unit(1)
+    key_wg = mm(context_t[...], grad_key)
+    unit(2)
+    value_wg = mm(context_t[...], grad_value)
+    unit(3)
+    context_part = mm_nt(grad_key, key_w_ref[0]) + mm_nt(grad_value, value_w_ref[0])
+
+    @pl.when(group == 0)
+    def _():
+        acc[...] = context_part
+
+    @pl.when((group > 0) & (group < groups - 1))
+    def _():
+        acc[...] += context_part
+
+    @pl.when(group == groups - 1)
+    def _():
+        context_grad_ref[...] = (acc[...] + context_part).astype(BF)
+
+    @pl.when(image == 0)
+    def _():
+        key_acc[:, lanes] = key_wg
+        value_acc[:, lanes] = value_wg
+
+    @pl.when(image > 0)
+    def _():
+        key_acc[:, lanes] += key_wg
+        value_acc[:, lanes] += value_wg
+
+    return grad_query
+
+
 def cross_back_kernel(
     context_ref, query_ref, key_ref, value_ref, total_ref, mixed_grad_ref, key_w_ref, value_w_ref,
     query_grad_ref, context_grad_ref, key_wg_ref, value_wg_ref, small_ref,
     context_t, acc, key_acc, value_acc,
 ):
     image, group = pl.program_id(0), pl.program_id(1)
-    last_image, last_group = pl.num_programs(0) - 1, pl.num_programs(1) - 1
-
-    @pl.when(group == 0)
-    def _():
-        context_t[...] = context_ref[...].T
+    images, groups = pl.num_programs(0), pl.num_programs(1)
 
     @pl.when((image == 0) & (group == 0))
     def _():
         small_ref[...] = jnp.zeros_like(small_ref)
 
-    grad_query, grad_key, grad_value = attend_back(
-        query_ref[...], key_ref[...], value_ref[...], total_ref[0, 0:1], mixed_grad_ref[...],
-        key_ref.shape[0],
+    query_grad_ref[...] = cross_back_step(
+        image, group, images, groups, context_ref, query_ref, key_ref, value_ref, total_ref,
+        mixed_grad_ref, key_w_ref, value_w_ref, context_grad_ref, small_ref, context_t, acc,
+        key_acc, value_acc, lambda part: None,
     )
-    query_grad_ref[...] = grad_query
-    lanes = pl.ds(pl.multiple_of(group * SLAB, SLAB), SLAB)
-    small_ref[0:1, lanes] += rows_sum(grad_query.astype(F32))
-    small_ref[1:2, lanes] += rows_sum(grad_value.astype(F32))
-    key_wg = mm(context_t[...], grad_key)
-    value_wg = mm(context_t[...], grad_value)
-    context_part = mm_nt(grad_key, key_w_ref[0]) + mm_nt(grad_value, value_w_ref[0])
-
-    @pl.when(group == 0)
-    def _():
-        acc[...] = context_part
-
-    @pl.when((group > 0) & (group < last_group))
-    def _():
-        acc[...] += context_part
-
-    @pl.when(group == last_group)
-    def _():
-        context_grad_ref[...] = (acc[...] + context_part).astype(BF)
-
-    @pl.when(image == 0)
-    def _():
-        key_acc[:, lanes] = key_wg
-        value_acc[:, lanes] = value_wg
-
-    @pl.when(image > 0)
-    def _():
-        key_acc[:, lanes] += key_wg
-        value_acc[:, lanes] += value_wg
-
-    @pl.when(image == last_image)
-    def _():
-        key_wg_ref[:, lanes] = key_acc[:, lanes].astype(BF)
-        value_wg_ref[:, lanes] = value_acc[:, lanes].astype(BF)
-
-
-def self_back_kernel(
+
+    @pl.when((image == images - 1) & (group == groups - 1))
+    def _():
+        key_wg_ref[...] = key_acc[...].astype(BF)
+        value_wg_ref[...] = value_acc[...].astype(BF)
+
+
+def self_back(
     images, valid, tokens_ref, weight_ref, row_ref, gain_ref, qkv_ref, mixed_ref, total_ref, sum_ref,
-    residual_ref, cross_query_grad_ref,
-    query_grad_ref, cross_wg_ref, self_wg_ref, small_ref, qkv_grad,
+    residual_ref, cross_query_grad_ref, small_ref, qkv_grad, emit, unit,
 ):
-    small_ref[...] = jnp.zeros_like(small_ref)
     tokens = tokens_ref[...]
     rows = tokens.shape[0] // images
     width = tokens.shape[1]
     normed, scale = norm_parts(sum_ref[...])
     first_low = (normed * gain_ref[0:1] + row_ref[1:2]).astype(BF)
     cross_query_grad = cross_query_grad_ref[...]
-    cross_wg_ref[...] = mm(first_low.T, cross_query_grad).astype(BF)
+    emit(4, mm(first_low.T, cross_query_grad))
+    unit()
     first_in = residual_ref[...] + mm_nt(cross_query_grad, weight_ref[4])
     first_grad = norm_back(normed, scale, gain_ref[0:1], first_in)
-    small_ref[2:3] = rows_sum(first_grad)
-    small_ref[3:4] = rows_sum(first_in)
-    small_ref[4:5] = rows_sum(first_in * normed)
+    small_ref[8:9] = rows_sum(first_grad)
+    small_ref[9:10] = rows_sum(first_in)
+    small_ref[14:15] = rows_sum(first_in * normed)
+    unit()
     self_low = first_grad.astype(BF)
-    self_wg_ref[3] = mm(self_low.T, mixed_ref[...]).astype(BF)
+    emit(3, mm(self_low.T, mixed_ref[...]))
+    unit()
     mixed_grad = mm(self_low, weight_ref[3]).astype(BF)
     for image in range(images):
         at = slice(image * rows, (image + 1) * rows)
@@ -396,15 +414,32 @@
             )
             for which in range(3):
                 qkv_grad[which, at, lanes] = grads[which]
+            unit()
     tokens_t = tokens.T
     total = first_grad
     for which in range(3):
         grad = qkv_grad[which]
-        self_wg_ref[which] = mm(tokens_t, grad).astype(BF)
+        emit(which, mm(tokens_t, grad))
+        unit()
         total = total + mm_nt(grad, weight_ref[which])
     small_ref[0:1] = rows_sum(qkv_grad[0].astype(F32))
     small_ref[1:2] = rows_sum(qkv_grad[2].astype(F32))
-    query_grad_ref[...] = total.astype(BF)
+    return total
+
+
+def self_back_kernel(
+    images, valid, tokens_ref, weight_ref, row_ref, gain_ref, qkv_ref, mixed_ref, total_ref, sum_ref,
+    residual_ref, cross_query_grad_ref, query_grad_ref, wg_ref, small_ref, qkv_grad,
+):
+    small_ref[...] = jnp.zeros_like(small_ref)
+
+    def emit(block, value):
+        wg_ref[block] = value.astype(BF)
+
+    query_grad_ref[...] = self_back(
+        images, valid, tokens_ref, weight_ref, row_ref, gain_ref, qkv_ref, mixed_ref, total_ref,
+        sum_ref, residual_ref, cross_query_grad_ref, small_ref, qkv_grad, emit, lambda: None,
+    ).astype(BF)
 
 
 def task_peers(tasks):
@@ -438,54 +473,72 @@
     pl.semaphore_wait(barrier, tasks + depth - 1)
 
 
+LAG = 3
+AHEAD = 2
+RING = 4
+
+
 class Chain:
-    def __init__(self, depth, tasks, near, far, passed, parts, sems):
+    def __init__(self, depth, tasks, sources, near, far, refs):
         self.depth, self.tasks = depth, tasks
-        self.near, self.far, self.passed, self.parts = near, far, passed, parts
-        (self.near_sem, self.far_send, self.far_recv, self.pass_send, self.pass_recv,
-         self.part_send, self.part_recv) = sems
-        self.chunks = passed.shape[1]
-        self.rows, self.half = passed.shape[2:]
+        self.sources, self.near, self.far = sources, near, far
+        (self.near_ring, self.far_ring, self.passed, self.parts,
+         self.near_sem, self.far_sem, self.far_send, self.far_recv, self.pass_send, self.pass_recv,
+         self.part_send, self.part_recv) = refs
+        self.chunks = self.passed.shape[1]
+        self.rows, self.half = self.passed.shape[2:]
+        self.size = self.rows // 2
         self.me = lax.axis_index("dp")
         self.task = lax.axis_index("task")
         self.is_end = (self.me == 0) | (self.me == depth - 1)
+        self.given = sum(source.shape[0] for source in sources)
+
+    SCRATCH = 12
 
     @staticmethod
     def scratch(blocks, rows, half, tasks):
         chunks = 2 * blocks
+        dma = pltpu.SemaphoreType.DMA
         return [
-            pltpu.VMEM((2, blocks, 2 * rows, half), BF),
-            pltpu.VMEM((2, blocks, 2 * rows, half), BF),
+            pltpu.VMEM((RING, 2, rows // 2, half), BF),
+            pltpu.VMEM((RING, 2, rows // 2, half), BF),
             pltpu.VMEM((2, chunks, rows, half), BF),
             pltpu.VMEM((tasks, chunks, rows // tasks, half), BF),
-            pltpu.SemaphoreType.DMA((2, blocks)),
-            pltpu.SemaphoreType.DMA((2, blocks)),
-            pltpu.SemaphoreType.DMA((2, blocks)),
-            pltpu.SemaphoreType.DMA((2, chunks, 2)),
-            pltpu.SemaphoreType.DMA((2, chunks, 2)),
-            pltpu.SemaphoreType.DMA((chunks, tasks - 1)),
-            pltpu.SemaphoreType.DMA((chunks, tasks - 1)),
+            dma((RING, 2)),
+            dma((RING, 2)),
+            dma((2, blocks)),
+            dma((2, blocks)),
+            dma((2, chunks, 2)),
+            dma((2, chunks, 2)),
+            dma((chunks, tasks - 1)),
+            dma((chunks, tasks - 1)),
         ]
 
-    def near_copy(self, source, way, block):
-        return pltpu.make_async_copy(
-            source, self.near.at[way, block], self.near_sem.at[way, block]
-        )
-
     def far_copy(self, source, way, block):
+        rows = pl.ds(way * 2 * self.rows, 2 * self.rows)
         return send(
-            source, self.far.at[way, block], self.far_send.at[way, block],
+            source.at[rows], self.far.at[way, block], self.far_send.at[way, block],
             self.far_recv.at[way, block], tensor=1 - lax.axis_index("tensor"),
         )
 
-    def load(self, block, source):
-        for way in range(2):
-            rows = pl.ds(way * 2 * self.rows, 2 * self.rows)
-            self.near_copy(source.at[rows, pl.ds(0, self.half)], way, block).start()
-            self.far_copy(source.at[rows, pl.ds(self.half, self.half)], way, block).start()
+    def far_arrival(self, way, block):
+        landed = self.far.at[way, block]
+        return send(
+            landed, landed, self.far_send.at[way, block], self.far_recv.at[way, block],
+            tensor=1 - lax.axis_index("tensor"),
+        )
+
+    def exchange(self):
+        base = 0
+        for source in self.sources:
+            for block in range(source.shape[0]):
+                for way in range(2):
+                    columns = pl.ds(self.half, self.half)
+                    self.far_copy(source.at[block, :, columns], way, base + block).start()
+            base += source.shape[0]
 
     def pass_copy(self, way, chunk, sub):
-        rows = pl.ds(sub * (self.rows // 2), self.rows // 2)
+        rows = pl.ds(pl.multiple_of(sub * self.size, self.size), self.size)
         piece = self.passed.at[way, chunk, rows]
         target = self.me - 1 if way == 0 else self.me + 1
         return send(
@@ -503,55 +556,92 @@
             self.part_send.at[chunk, shift], self.part_recv.at[chunk, shift], task=peer,
         )
 
-    def lag(self, way):
+    def hops(self, way):
         return self.depth - 1 - self.me if way == 0 else self.me
 
-    def steps(self):
-        return self.chunks + self.depth - 1
-
-    def step(self, index):
+    def units(self):
+        return 2 * self.chunks + LAG * (self.depth - 1)
+
+    def near_fetch(self, source, slot, way):
+        return pltpu.make_async_copy(
+            source, self.near_ring.at[slot, way], self.near_sem.at[slot, way]
+        )
+
+    def far_fetch(self, source, slot, way):
+        return pltpu.make_async_copy(
+            source, self.far_ring.at[slot, way], self.far_sem.at[slot, way]
+        )
+
+    def fetch(self, index):
+        slot = lax.rem(index, RING)
         for way in range(2):
-            chunk = index - self.lag(way)
-
-            @pl.when((chunk >= 0) & (chunk < self.chunks))
-            def _(way=way, chunk=chunk):
-                self.chunk_step(way, chunk)
-
-    def chunk_step(self, way, chunk):
-        block = chunk // 2
-        part = chunk - 2 * block
-        first, last = self.lag(way) == 0, self.lag(way) == self.depth - 1
-
-        @pl.when(part == 0)
+            at = index - LAG * self.hops(way)
+
+            @pl.when((at >= 0) & (at < 2 * self.chunks))
+            def _(way=way, at=at):
+                block = at // 4
+                place = at - 4 * block
+
+                @pl.when(place == 0)
+                def _():
+                    self.far_arrival(way, block).wait_recv()
+
+                start = pl.multiple_of(place * self.size, self.size)
+                rows = pl.ds(way * 2 * self.rows + start, self.size)
+                base = 0
+                for source in self.sources:
+                    count = source.shape[0]
+
+                    @pl.when((block >= base) & (block < base + count))
+                    def _(source=source, base=base):
+                        columns = pl.ds(0, self.half)
+                        self.near_fetch(source.at[block - base, rows, columns], slot, way).start()
+
+                    base += count
+
+                @pl.when(block >= base)
+                def _():
+                    self.near_fetch(self.near.at[block - base, rows], slot, way).start()
+
+                self.far_fetch(
+                    self.far.at[way, block, pl.ds(start, self.size)], slot, way
+                ).start()
+
+    def unit(self, index):
+        self.fetch(index + AHEAD)
+        slot = lax.rem(index, RING)
+        for way in range(2):
+            at = index - LAG * self.hops(way)
+
+            @pl.when((at >= 0) & (at < 2 * self.chunks))
+            def _(way=way, at=at):
+                chunk = at // 2
+                self.half_step(way, chunk, at - 2 * chunk, slot)
+
+    def half_step(self, way, chunk, sub, slot):
+        first, last = self.hops(way) == 0, self.hops(way) == self.depth - 1
+        piece = self.near_ring.at[slot, way]
+        self.near_fetch(piece, slot, way).wait()
+        self.far_fetch(piece, slot, way).wait()
+        rows = pl.ds(pl.multiple_of(sub * self.size, self.size), self.size)
+        own = self.near_ring[slot, way].astype(F32) + self.far_ring[slot, way].astype(F32)
+
+        @pl.when(first)
         def _():
-            piece = self.near.at[way, block]
-            self.near_copy(piece, way, block).wait()
-            self.far_copy(piece, way, block).wait_recv()
-
-        sub_rows = self.rows // 2
-        for sub in range(2):
-            at = pl.ds(pl.multiple_of(part * self.rows + sub * sub_rows, sub_rows), sub_rows)
-            rows = pl.ds(sub * sub_rows, sub_rows)
-
-            def own():
-                return self.near[way, block, at].astype(F32) + self.far[way, block, at].astype(F32)
-
-            @pl.when(first)
-            def _():
-                self.passed[way, chunk, rows] = own().astype(BF)
-
-            @pl.when(jnp.logical_not(first))
-            def _():
-                self.pass_copy(way, chunk, sub).wait_recv()
-                self.passed[way, chunk, rows] = (
-                    own() + self.passed[way, chunk, rows].astype(F32)
-                ).astype(BF)
-
-            @pl.when(jnp.logical_not(last))
-            def _():
-                self.pass_copy(way, chunk, sub).start()
-
-        @pl.when(last)
+            self.passed[way, chunk, rows] = own.astype(BF)
+
+        @pl.when(jnp.logical_not(first))
+        def _():
+            self.pass_copy(way, chunk, sub).wait_recv()
+            self.passed[way, chunk, rows] = (
+                own + self.passed[way, chunk, rows].astype(F32)
+            ).astype(BF)
+
+        @pl.when(jnp.logical_not(last))
+        def _():
+            self.pass_copy(way, chunk, sub).start()
+
+        @pl.when(last & (sub == 1))
         def _():
             for shift, peer in enumerate(task_peers(self.tasks)):
                 self.part_copy(way, chunk, shift, peer).start()
@@ -566,22 +656,15 @@
             ).wait_recv()
 
     def finish(self):
-        def blocks(block, carry):
-            for way in range(2):
-                self.far_copy(self.near.at[way, block], way, block).wait_send()
-            return carry
-
-        lax.fori_loop(0, self.chunks // 2, blocks, 0)
-
         def chunks(chunk, carry):
             for way in range(2):
 
-                @pl.when(self.lag(way) != self.depth - 1)
+                @pl.when(self.hops(way) != self.depth - 1)
                 def _(way=way):
                     for sub in range(2):
                         self.pass_copy(way, chunk, sub).wait_send()
 
-                @pl.when(self.lag(way) == self.depth - 1)
+                @pl.when(self.hops(way) == self.depth - 1)
                 def _(way=way):
                     for shift, peer in enumerate(task_peers(self.tasks)):
                         self.part_copy(way, chunk, shift, peer).wait_send()
@@ -614,46 +697,35 @@
 
 
 GROUPS = 4
-
-
-def reduce_kernel(depth, tasks, layout, order_ref, small_ref, *refs):
-    sources, refs = refs[: len(layout)], refs[len(layout) :]
-    (update_ref, small_out_ref, gram_ref), refs = refs[:3], refs[3:]
-    chain = Chain(depth, tasks, *refs[:4], refs[4:11])
+UNITS = 4
+
+
+def back_kernel(
+    depth, tasks, images, groups, valid, block_order, order_ref, context_ref, query_ref, key_ref,
+    value_ref, total_ref, mixed_grad_ref, key_w_ref, value_w_ref, tokens_ref, weight_ref, row_ref,
+    gain_ref, qkv_ref, mixed_ref, self_total_ref, sum_ref, residual_ref, small_in_ref, *refs
+):
+    sources, refs = refs[:3], refs[3:]
+    (context_grad_ref, query_grad_ref, update_ref, small_out_ref, gram_ref, near, far), refs = (
+        refs[:7], refs[7:],
+    )
+    (context_t, acc, key_acc, value_acc, cross_query_grad, qkv_grad, stage, stage_sem), refs = (
+        refs[:8], refs[8:],
+    )
+    chain = Chain(depth, tasks, sources, near, far, refs[: Chain.SCRATCH])
+    refs = refs[Chain.SCRATCH :]
     (
-        small_far, small_pass, small_all, small_both, gram_acc, gram_task, gram_core, gram_end,
-        hop, out,
+        small, small_own, small_other, small_far, small_pass, small_all, small_both, gram_acc,
+        gram_task, gram_core, gram_end, hop, out,
         small_far_sem, small_pass_sem, small_task_sem, small_dp_sem, small_core_sem,
-        gram_task_sem, gram_core_sem, gram_dp_sem, hop_sem, out_sem,
-    ) = refs[11:]
+        gram_task_sem, gram_core_sem, gram_dp_sem, hop_sem, out_sem, update_sem,
+    ) = refs
+    step = pl.program_id(0)
+    cross_steps = images * groups
     me, task, core = (lax.axis_index(axis) for axis in ("dp", "task", "tensor"))
     half = chain.half
     is_end = chain.is_end
     top = me == 0
-    greet(depth, tasks)
-    small_copy = send(
-        small_ref.at[:, pl.ds(half, half)], small_far, small_far_sem.at[0], small_far_sem.at[1],
-        tensor=1 - core,
-    )
-    small_copy.start()
-    for index, (source, blocks) in enumerate(zip(sources, layout)):
-        base = sum(len(entry) for entry in layout[:index])
-        for block in range(len(blocks)):
-            chain.load(base + block, source.at[block])
-    block_order = [block for blocks in layout for block in blocks]
-
-    def small_hop():
-        return send(
-            small_pass, small_pass, small_pass_sem.at[0], small_pass_sem.at[1], dp=me - 1
-        )
-
-    def small_task_copy(shift, peer):
-        return send(
-            small_pass, small_all.at[task], small_task_sem.at[0, shift],
-            small_task_sem.at[1, shift], task=peer,
-        )
-
-    gram_acc[...] = jnp.zeros_like(gram_acc)
     pairs = pairs_of(tasks)
 
     def add_products(shares):
@@ -664,13 +736,151 @@
                 total = total + product[row : row + 8]
             gram_acc[index * 8 : index * 8 + 8] += total
 
+    def unit(index):
+        chain.unit(index)
+        since = index - LAG * (depth - 1) - 4
+        landed = since // 2
+
+        @pl.when(is_end & (since >= 0) & (since == 2 * landed))
+        def _():
+            chain.wait_parts(landed)
+            add_products([chain.parts[t, landed].astype(F32) for t in range(tasks)])
+
+    @pl.when(step == 0)
+    def _():
+        greet(depth, tasks)
+        chain.exchange()
+        gram_acc[...] = jnp.zeros_like(gram_acc)
+        small[...] = small_in_ref[...]
+        for index in range(AHEAD):
+            chain.fetch(index)
+
+    given = chain.given
+    slots = stage.shape[0]
+
+    def stage_copies(position):
+        slot = position % slots
+        return [
+            chain.far_copy(stage.at[slot, :, pl.ds(half, half)], way, given + position)
+            for way in range(2)
+        ]
+
+    def emit(position, value):
+        slot = position % slots
+        if position >= slots:
+            for copy in stage_copies(position - slots):
+                copy.wait_send()
+        stage[slot] = value.astype(BF)
+        for copy in stage_copies(position):
+            copy.start()
+        copy = pltpu.make_async_copy(
+            stage.at[slot, :, pl.ds(0, half)], near.at[position], stage_sem
+        )
+        copy.start()
+        copy.wait()
+
+    def finish_reduction(done):
+        rest(
+            chain, unit, done, order_ref, update_ref, small_out_ref, gram_ref, small, small_own,
+            small_other, small_far, small_pass, small_all, small_both, gram_acc, gram_task,
+            gram_core, gram_end, hop, out, small_far_sem, small_pass_sem, small_task_sem,
+            small_dp_sem, small_core_sem, gram_task_sem, gram_core_sem, gram_dp_sem, hop_sem,
+            out_sem, update_sem,
+        )
+        for position in range(len(block_order) - given - slots, len(block_order) - given):
+            for copy in stage_copies(position):
+                copy.wait_send()
+        for block in range(given):
+            for way in range(2):
+                chain.far_arrival(way, block).wait_send()
+
+    @pl.when(step < cross_steps)
+    def _():
+        image = step // groups
+        group = step - image * groups
+
+        def cross_unit(part):
+            if part < 2:
+                unit(step * UNITS + part)
+            else:
+
+                @pl.when(step < cross_steps - 1)
+                def _():
+                    unit(step * UNITS + part)
+
+        grad_query = cross_back_step(
+            image, group, images, groups, context_ref, query_ref, key_ref, value_ref, total_ref,
+            mixed_grad_ref, key_w_ref, value_w_ref, context_grad_ref, small, context_t, acc,
+            key_acc, value_acc, cross_unit,
+        )
+        rows = grad_query.shape[0]
+        cross_query_grad[
+            pl.ds(pl.multiple_of(image * rows, rows), rows),
+            pl.ds(pl.multiple_of(group * SLAB, SLAB), SLAB),
+        ] = grad_query
+
+        @pl.when(step == cross_steps - 1)
+        def _():
+            emit(0, key_acc[...])
+            emit(1, value_acc[...])
+
+    @pl.when(step == cross_steps)
+    def _():
+        done = [cross_steps * UNITS - 2]
+
+        def self_unit():
+            unit(jnp.int32(done[0]))
+            done[0] += 1
+
+        positions = {4: 2, 3: 3, 0: 4, 1: 5, 2: 6}
+        query_grad_ref[...] = self_back(
+            images, valid, tokens_ref, weight_ref, row_ref, gain_ref, qkv_ref, mixed_ref,
+            self_total_ref, sum_ref, residual_ref, cross_query_grad, small, qkv_grad,
+            lambda block, value: emit(positions[block], value), self_unit,
+        ).astype(BF)
+        finish_reduction(done[0])
+
+
+def rest(
+    chain, unit, done, order_ref, update_ref, small_out_ref, gram_ref, small, small_own, small_other,
+    small_far, small_pass, small_all, small_both, gram_acc, gram_task, gram_core, gram_end, hop, out,
+    small_far_sem, small_pass_sem, small_task_sem, small_dp_sem, small_core_sem, gram_task_sem,
+    gram_core_sem, gram_dp_sem, hop_sem, out_sem, update_sem,
+):
+    depth, tasks, half = chain.depth, chain.tasks, chain.half
+    me, task, core = (lax.axis_index(axis) for axis in ("dp", "task", "tensor"))
+    is_end = chain.is_end
+    top = me == 0
+    pairs = pairs_of(tasks)
+    own_lanes = pl.ds(pl.multiple_of(core * half, half), half)
+    other_lanes = pl.ds(pl.multiple_of((1 - core) * half, half), half)
+    small_own[0:8] = small[0:8, 0:half]
+    small_own[8:] = small[8:, own_lanes]
+    small_other[0:8] = small[0:8, half:]
+    small_other[8:] = small[8:, other_lanes]
+    small_copy = send(
+        small_other, small_far, small_far_sem.at[0], small_far_sem.at[1], tensor=1 - core
+    )
+    small_copy.start()
+
+    def small_hop():
+        return send(
+            small_pass, small_pass, small_pass_sem.at[0], small_pass_sem.at[1], dp=me - 1
+        )
+
+    def small_task_copy(shift, peer):
+        return send(
+            small_pass, small_all.at[task], small_task_sem.at[0, shift],
+            small_task_sem.at[1, shift], task=peer,
+        )
+
     def step(index, carry):
-        chain.step(index)
-
-        @pl.when(index == chain.lag(0))
+        unit(index)
+
+        @pl.when(index == done + 1 + LAG * chain.hops(0))
         def _():
             small_copy.wait_recv()
-            total = small_ref[:, pl.ds(0, half)] + small_far[...]
+            total = small_own[...] + small_far[...]
 
             @pl.when(me == depth - 1)
             def _():
@@ -691,16 +901,9 @@
                     small_task_copy(shift, peer).start()
                 small_all[task] = small_pass[...]
 
-        landed = index - (depth - 1) - 2
-
-        @pl.when(is_end & (landed >= 0))
-        def _():
-            chain.wait_parts(landed)
-            add_products([chain.parts[t, landed].astype(F32) for t in range(tasks)])
-
         return carry
 
-    lax.fori_loop(0, chain.steps() + 2, step, 0)
+    lax.fori_loop(done, chain.units() + 4, step, 0)
 
     @pl.when(top)
     def _():
@@ -800,7 +1003,7 @@
         for weight in weights_of(gram, order_ref, tasks)
     ]
 
-    blocks = chain.chunks // 2
+    blocks = out.shape[0]
     group = blocks // GROUPS
     share = chain.rows // tasks
     mine = pl.ds(pl.multiple_of(task * share, share), share)
@@ -816,6 +1019,10 @@
     def out_copy(index, shift, peer):
         piece = out.at[pl.ds(index * group, group), mine]
         return send(piece, piece, out_sem.at[0, index, shift], out_sem.at[1, index, shift], task=peer)
+
+    def update_copy(index):
+        at = pl.ds(index * group, group)
+        return pltpu.make_async_copy(out.at[at], update_ref.at[at], update_sem.at[index])
 
     def weighted(chunk):
         total = weights[0] * chain.parts[0, chunk].astype(F32)
@@ -886,11 +1093,13 @@
             send(
                 piece, piece, out_sem.at[0, index, shift], out_sem.at[1, index, shift], task=peer
             ).wait_recv()
-        for block in range(index * group, (index + 1) * group):
-            update_ref[:, block_order[block], :] = out[block].astype(F32)
+        update_copy(index).start()
 
     small_core_copy().wait_recv()
-    small_out_ref[...] = small_both[...]
+    small_out_ref[0:8, 0:half] = small_both[0, 0:8]
+    small_out_ref[0:8, half:] = small_both[1, 0:8]
+    small_out_ref[8:, own_lanes] = small_both[0, 8:]
+    small_out_ref[8:, other_lanes] = small_both[1, 8:]
 
     small_copy.wait_send()
     small_core_copy().wait_send()
@@ -923,51 +1132,14 @@
             hop_copy(index).wait_send()
 
     for index in range(GROUPS):
+        update_copy(index).wait()
         for shift, peer in enumerate(task_peers(tasks)):
             out_copy(index, shift, peer).wait_send()
 
 
-def reduce_by_chain(order, small, sources, layout, depth, tasks, half):
-    blocks = sum(len(entry) for entry in layout)
-    rows = sources[0].shape[1] // 4
-    pair_rows = 8 * len(pairs_of(tasks))
-    dma = pltpu.SemaphoreType.DMA
-    return pl.pallas_call(
-        functools.partial(reduce_kernel, depth, tasks, layout),
-        out_shape=(
-            jax.ShapeDtypeStruct((rows, blocks, half), F32),
-            jax.ShapeDtypeStruct((2, *small.shape[:1], half), F32),
-            jax.ShapeDtypeStruct((16, 128), F32),
-        ),
-        in_specs=[pl.BlockSpec(memory_space=pltpu.SMEM), whole_spec()]
-        + [any_spec()] * len(sources),
-        out_specs=(whole_spec(), whole_spec(), whole_spec()),
-        scratch_shapes=Chain.scratch(blocks, rows, half, tasks)
-        + [
-            pltpu.VMEM((small.shape[0], half), F32),
-            pltpu.VMEM((small.shape[0], half), F32),
-            pltpu.VMEM((tasks, small.shape[0], half), F32),
-            pltpu.VMEM((2, small.shape[0], half), F32),
-            pltpu.VMEM((pair_rows, half), F32),
-            pltpu.VMEM((tasks, 16, 128), F32),
-            pltpu.VMEM((2, 16, 128), F32),
-            pltpu.VMEM((2, 16, 128), F32),
-            pltpu.VMEM((blocks, rows // tasks, half), BF),
-            pltpu.VMEM((blocks, rows, half), BF),
-            dma((2,)),
-            dma((2,)),
-            dma((2, tasks - 1)),
-            dma((2, depth - 1)),
-            dma((2,)),
-            dma((2, tasks - 1)),
-            dma((2,)),
-            dma((2, 2, depth - 1)),
-            dma((2, GROUPS)),
-            dma((2, GROUPS, tasks - 1)),
-        ],
-        compiler_params=params_for(collective_id=1, has_side_effects=True),
-        name="reduce",
-    )(order, small, *sources)
+def spread_kernel(block_order, parts_ref, update_ref):
+    for index, block in enumerate(block_order):
+        update_ref[:, block, :] = parts_ref[index].astype(F32)
 
 
 def gram_kernel(parts_ref, gram_ref):
@@ -1076,34 +1248,31 @@
         name="self_forward",
     )(tokens, weights, head_f, row_f, gain_f)
 
-    start = (core * images).astype(jnp.int32).reshape(1)
-    context_all = pl.BlockSpec((keys, width), lambda i, g, s: (s[0] + i, 0))
-    slab_q = pl.BlockSpec((padded, SLAB), lambda i, g, *_: (i, g))
-    slab_k = pl.BlockSpec((keys, SLAB), lambda i, g, *_: (i, g))
-    slab_t = pl.BlockSpec((1, 8, stack), lambda i, g, *_: (i * groups + g, 0, 0))
+
+    def own_image(i, g):
+        return lax.axis_index("tensor") * images + i, 0
+
+    context_all = pl.BlockSpec((keys, width), own_image)
+    slab_q = pl.BlockSpec((padded, SLAB), lambda i, g: (i, g))
+    slab_k = pl.BlockSpec((keys, SLAB), lambda i, g: (i, g))
+    slab_t = pl.BlockSpec((1, 8, stack), lambda i, g: (i * groups + g, 0, 0))
 
     def slab_w(block):
-        return pl.BlockSpec((1, width, SLAB), lambda i, g, *_: (block, 0, g))
-
-    def with_start(kernel):
-        return lambda start_ref, *refs: kernel(*refs)
+        return pl.BlockSpec((1, width, SLAB), lambda i, g: (block, 0, g))
 
     key_rows = jax.ShapeDtypeStruct((images * keys, width), BF)
     keys_act, values_act, cross_mixed, cross_total = pl.pallas_call(
-        with_start(cross_kernel),
-        grid_spec=pltpu.PrefetchScalarGridSpec(
-            num_scalar_prefetch=1,
-            grid=(images, groups),
-            in_specs=[
-                context_all, slab_q, slab_w(5), slab_w(6),
-                pl.BlockSpec((16, SLAB), lambda i, g, *_: (0, g)),
-            ],
-            out_specs=(slab_k, slab_k, slab_q, slab_t),
-        ),
+        cross_kernel,
+        grid=(images, groups),
+        in_specs=[
+            context_all, slab_q, slab_w(5), slab_w(6),
+            pl.BlockSpec((16, SLAB), lambda i, g: (0, g)),
+        ],
+        out_specs=(slab_k, slab_k, slab_q, slab_t),
         out_shape=(key_rows, key_rows, low_rows, total_shape),
         compiler_params=params_for(),
         name="cross_forward",
-    )(start, context, cross_query, weights, weights, head_f)
+    )(context, cross_query, weights, weights, head_f)
 
     (
         block_rows, grad_in, grad_out, cross_out_wg, mixed_grad, second_grad, ffn_small,
@@ -1147,36 +1316,152 @@
         head_f, row_f, gain_f,
     )
 
-    cross_query_grad, context_grad, key_wg, value_wg, cross_small = pl.pallas_call(
-        with_start(cross_back_kernel),
-        grid_spec=pltpu.PrefetchScalarGridSpec(
-            num_scalar_prefetch=1,
-            grid=(images, groups),
+    depth, tasks = lax.axis_size("dp"), lax.axis_size("task")
+    by_chain = depth == 4 and tasks == 4 and cores == 2
+
+    def unpad(array):
+        return array.reshape(images, padded, width)[:, :valid].reshape(1, images * valid, width)
+
+    block_out = lax.all_gather(unpad(block_rows), "tensor", axis=1, tiled=True)
+    if by_chain:
+        block_order = [*range(8, block_count), 7, 5, 6, 4, 3, 0, 1, 2]
+        chain_rows = width // depth
+        pair_rows = 8 * len(pairs_of(tasks))
+        dma = pltpu.SemaphoreType.DMA
+        last = images * groups - 1
+
+        def at_step(make):
+            def index_map(step):
+                now = jnp.minimum(step, last)
+                return make(now // groups, now - groups * (now // groups))
+
+            return index_map
+
+        def once(shape):
+            return pl.BlockSpec(
+                shape, lambda step: (0,) * len(shape), pipeline_mode=pl.Buffered(1)
+            )
+
+        step_q = pl.BlockSpec((padded, SLAB), at_step(lambda i, g: (i, g)))
+        step_k = pl.BlockSpec((keys, SLAB), at_step(lambda i, g: (i, g)))
+
+        def step_w(block):
+            return pl.BlockSpec((1, width, SLAB), at_step(lambda i, g: (block, 0, g)))
+
+        small_half = pltpu.VMEM((24, half), F32)
+        (
+            context_grad, token_grad, update_parts, small_out, gram_rows, _, _,
+        ) = pl.pallas_call(
+            functools.partial(
+                back_kernel, depth, tasks, images, groups, valid, block_order
+            ),
+            grid=(images * groups + 1,),
+            out_shape=(
+                key_rows, low_rows,
+                jax.ShapeDtypeStruct((block_count, chain_rows, half), BF),
+                small_shape,
+                jax.ShapeDtypeStruct((16, 128), F32),
+                jax.ShapeDtypeStruct((7, width, half), BF),
+                jax.ShapeDtypeStruct((2, block_count, width // 2, half), BF),
+            ),
             in_specs=[
-                context_all, slab_q, slab_k, slab_k, slab_t, slab_q, slab_w(5), slab_w(6),
+                pl.BlockSpec(memory_space=pltpu.SMEM),
+                pl.BlockSpec((keys, width), at_step(own_image)),
+                step_q, step_k, step_k,
+                pl.BlockSpec((1, 8, stack), at_step(lambda i, g: (i * groups + g, 0, 0))),
+                step_q, step_w(5), step_w(6),
+                once((rows, width)), once((5, width, width)), once((8, width)), once((8, width)),
+                once((3, rows, width)), once((rows, width)), once(total_shape.shape),
+                once((rows, width)), once((rows, width)), once((24, width)),
+                any_spec(), any_spec(), any_spec(),
             ],
             out_specs=(
-                slab_q,
-                pl.BlockSpec((keys, width), lambda i, g, *_: (i, 0)),
-                const((width, width), 0, 0), const((width, width), 0, 0), small_spec,
+                pl.BlockSpec((keys, width), at_step(lambda i, g: (i, 0))),
+                once((rows, width)), any_spec(), once((24, width)), once((16, 128)),
+                any_spec(), any_spec(),
             ),
             scratch_shapes=[
                 pltpu.VMEM((width, keys), BF),
                 pltpu.VMEM((keys, width), F32),
                 pltpu.VMEM((width, width), F32),
                 pltpu.VMEM((width, width), F32),
+                pltpu.VMEM((rows, width), BF),
+                pltpu.VMEM((3, rows, width), BF),
+                pltpu.VMEM((3, width, width), BF),
+                dma(()),
+                *Chain.scratch(block_count, chain_rows, half, tasks),
+                pltpu.VMEM((24, width), F32),
+                small_half, small_half, small_half, small_half,
+                pltpu.VMEM((tasks, 24, half), F32),
+                pltpu.VMEM((2, 24, half), F32),
+                pltpu.VMEM((pair_rows, half), F32),
+                pltpu.VMEM((tasks, 16, 128), F32),
+                pltpu.VMEM((2, 16, 128), F32),
+                pltpu.VMEM((2, 16, 128), F32),
+                pltpu.VMEM((block_count, chain_rows // tasks, half), BF),
+                pltpu.VMEM((block_count, chain_rows, half), BF),
+                dma((2,)),
+                dma((2,)),
+                dma((2, tasks - 1)),
+                dma((2, depth - 1)),
+                dma((2,)),
+                dma((2, tasks - 1)),
+                dma((2,)),
+                dma((2, 2, depth - 1)),
+                dma((2, GROUPS)),
+                dma((2, GROUPS, tasks - 1)),
+                dma((GROUPS,)),
             ],
+            compiler_params=params_for(collective_id=1, has_side_effects=True),
+            name="backward",
+        )(
+            task_order, context, cross_query, keys_act, values_act, cross_total, mixed_grad, weights,
+            weights, tokens, weights, row_f, gain_f, qkv, self_mixed, self_total, first_sum,
+            second_grad, ffn_small, grad_in, grad_out, cross_out_wg[None],
+        )
+        tile = chain_rows // 4
+        param_update = pl.pallas_call(
+            functools.partial(spread_kernel, block_order),
+            grid=(4,),
+            out_shape=jax.ShapeDtypeStruct((chain_rows, block_count, half), F32),
+            in_specs=[pl.BlockSpec((block_count, tile, half), lambda r: (0, r, 0))],
+            out_specs=pl.BlockSpec((tile, block_count, half), lambda r: (r, 0, 0)),
+            compiler_params=params_for(),
+            name="spread",
+        )(update_parts)
+        return (
+            block_out, unpad(token_grad), context_grad[None], param_update, small_out[:8, :half],
+            small_out[8:14].reshape(3, 2, width), small_out[14:17],
+            gram_rows[: tasks * tasks, 0].reshape(tasks, tasks),
+        )
+
+    cross_query_grad, context_grad, key_wg, value_wg, cross_small = pl.pallas_call(
+        cross_back_kernel,
+        grid=(images, groups),
+        in_specs=[
+            context_all, slab_q, slab_k, slab_k, slab_t, slab_q, slab_w(5), slab_w(6),
+        ],
+        out_specs=(
+            slab_q,
+            pl.BlockSpec((keys, width), lambda i, g: (i, 0)),
+            const((width, width), 0, 0), const((width, width), 0, 0), small_spec,
         ),
+        scratch_shapes=[
+            pltpu.VMEM((width, keys), BF),
+            pltpu.VMEM((keys, width), F32),
+            pltpu.VMEM((width, width), F32),
+            pltpu.VMEM((width, width), F32),
+        ],
         out_shape=(low_rows, key_rows, one_block, one_block, small_shape),
         compiler_params=params_for(),
         name="cross_backward",
-    )(start, context, cross_query, keys_act, values_act, cross_total, mixed_grad, weights, weights)
-
-    token_grad, cross_query_wg, self_wg, self_small = pl.pallas_call(
+    )(context, cross_query, keys_act, values_act, cross_total, mixed_grad, weights, weights)
+
+    token_grad, self_wg, self_small = pl.pallas_call(
         functools.partial(self_back_kernel, images, valid),
         grid=(1,),
         out_shape=(
-            low_rows, one_block, jax.ShapeDtypeStruct((4, width, width), BF), small_shape,
+            low_rows, jax.ShapeDtypeStruct((5, width, width), BF), small_shape,
         ),
         in_specs=[
             rows_spec, const((5, width, width), 0, 0, 0), vec8, vec8,
@@ -1184,7 +1469,7 @@
             rows_spec, rows_spec, rows_spec,
         ],
         out_specs=(
-            rows_spec, const((width, width), 0, 0), const((4, width, width), 0, 0, 0), small_spec,
+            rows_spec, const((5, width, width), 0, 0, 0), small_spec,
         ),
         scratch_shapes=[pltpu.VMEM((3, rows, width), BF)],
         compiler_params=params_for(),
@@ -1194,61 +1479,19 @@
         cross_query_grad,
     )
 
-    def unpad(array):
-        return array.reshape(images, padded, width)[:, :valid].reshape(1, images * valid, width)
-
-    block_out = lax.all_gather(unpad(block_rows), "tensor", axis=1, tiled=True)
     query_grad = unpad(token_grad)
     memory_grad = context_grad[None]
 
-    def by_halves(array):
-        halves = array.reshape(array.shape[0], cores, half)
-        return jnp.where(core == 0, halves, halves[:, ::-1]).reshape(array.shape)
-
-    small = jnp.concatenate(
-        [
-            self_small[0:2], cross_small[0:2], ffn_small[4:8],
-            by_halves(
-                jnp.concatenate(
-                    [self_small[2:4], ffn_small[10:14], self_small[4:5], ffn_small[15:17]], axis=0
-                )
-            ),
-            jnp.zeros((7, width), F32),
-        ],
-        axis=0,
-    )
-    depth, tasks = lax.axis_size("dp"), lax.axis_size("task")
-    if depth == 4 and tasks == 4 and cores == 2:
-        param_update, small_update, gram_rows = reduce_by_chain(
-            task_order, small,
-            [grad_in, grad_out, self_wg, cross_query_wg[None], key_wg[None], value_wg[None],
-             cross_out_wg[None]],
-            [range(8, 8 + blocks), range(8 + blocks, block_count), range(4), [4], [5], [6], [7]],
-            depth, tasks, half,
-        )
-        row_update = by_halves(
-            jnp.concatenate([small_update[0, 8:17], small_update[1, 8:17]], axis=1)
-        )
-        return (
-            block_out, query_grad, memory_grad, param_update, small_update[0, :8],
-            row_update[:6].reshape(3, 2, width), row_update[6:9],
-            gram_rows[: tasks * tasks, 0].reshape(tasks, tasks),
-        )
+    small = self_small + cross_small + ffn_small
     grads = jnp.concatenate(
-        [
-            self_wg,
-            jnp.stack([cross_query_wg, key_wg, value_wg, cross_out_wg]),
-            grad_in,
-            grad_out,
-        ],
-        axis=0,
+        [self_wg, jnp.stack([key_wg, value_wg, cross_out_wg]), grad_in, grad_out], axis=0
     )
     swap = [(0, 1), (1, 0)]
     grads = (
         grads[:, :, :half].astype(F32) + lax.ppermute(grads[:, :, half:], "tensor", swap).astype(F32)
     ).astype(BF)
     head_small = small[:8, :half] + lax.ppermute(small[:8, half:], "tensor", swap)
-    row_small = lax.psum(by_halves(small[8:17]), ("dp", "tensor"))
+    row_small = lax.psum(small[8:17], ("dp", "tensor"))
     head_small = lax.psum(head_small, "dp")
     shard = lax.psum_scatter(grads, "dp", scatter_dimension=1, tiled=True)
     all_shards = lax.all_gather(shard, "task", axis=0, tiled=False)

time: 364 us -> 327 us (0.90)
  Pallas kernels: 334 us -> 299 us
    pallas_call x4 -> x3, Pallas kernels: 284 us -> 248 us  [the longest x1 217 us: body(): pl.pallas_call(functools.partial(back_kernel, depth, tasks, images, group...]
where the time goes in v3:
time: 327 us; the launch traced here: 328 us
  Pallas kernels  299 us (91%)
  local copies, waits for them, and re-layouts  22.3 us (7%)
    pallas_call x1, Pallas kernels, body(): pl.pallas_call(functools.partial(back_kernel, depth, tasks, images, group...  217 us
    pallas_call x1, Pallas kernels, body(): pl.pallas_call(cross_kernel, grid=(images, groups), in_specs=[context_all...  25.6 us
    pallas_call x1, Pallas kernels, body(): pl.pallas_call(functools.partial(ffn_kernel, images, blocks), grid=(2 * b...  25.3 us
    pallas_call x1, Pallas kernels, body(): pl.pallas_call(gather_kernel, grid=(width // chunk,), out_shape=(jax.Shap...  16.6 us
    pallas_call x1, Pallas kernels, body(): pl.pallas_call(functools.partial(self_kernel, images, valid), grid=(1,),...  8.85 us

profile of v3, /device:TPU:8, one launch (start us, length us, event | category | flops | bytes accessed | tf_op | source)
XLA Modules:
  0.0 327.8 jit_solution(2693190039569801555)
XLA Ops:
  0.6 0.0 copy-start
  0.7 1.2 fusion.counts_ref
  1.9 0.0 copy-done
  1.9 0.6 dynamic-slice_bitcast_fusion.matches_ref
  2.5 1.3 pad.24.bias_ref
  3.8 0.7 reshape.45
  4.5 1.3 pad_convert_fusion
  5.8 1.3 reshape_squeeze.9
  7.1 1.3 reshape_squeeze.10
  8.4 0.1 constant_dynamic-slice_fusion.1
  8.5 0.8 pad.29
  9.3 0.8 pad.23
  10.1 16.6 %gather_weights.1 = (bf16[16,768,768]{2,1,0:T(8,128)(2,1)}, bf16[16,768]{1,0:T(8,128)(2,1)}) custom-call(bf16[768,16,384]{2,1,0:T(8,128)(2,1)} %own_ref.1, bf16[16,384]{1,0:T(8,128)(2,1)} %pad.24.bias_ref), custom_call_target="tpu_custom_call" | custom-call | tf_op jit(solution)/shard_map/gather_weights/pallas_call | solution.py:1199
  26.8 1.3 convert_element_type.14.head_ref
  28.1 8.9 %self_forward.1 = (bf16[3,336,768]{2,1,0:T(8,128)(2,1)}, bf16[336,768]{1,0:T(8,128)(2,1)}, f32[9,8,448]{2,1,0:T(8,128)}, f32[336,768]{1,0:T(8,128)}, bf16[336,768]{1,0:T(8,128)(2,1)}) custom-call(bf16[336,768]{1,0:T(8,128)(2,1)} %bitcast.14, bf16[16,768,768]{2,1,0:T(8,128)(2,1)} %get-tuple-element.31.weight_ref.key_w_ref.value_w_ref.cross_w_ref.in_ref.out_ref, ...), custom_call_target="tpu_custom_call" | custom-call | tf_op jit(solution)/shard_map/self_forward/pallas_call | solution.py:1236
  37.0 25.6 %cross_forward.1 = (bf16[3600,768]{1,0:T(8,128)(2,1)}, bf16[3600,768]{1,0:T(8,128)(2,1)}, bf16[336,768]{1,0:T(8,128)(2,1)}, f32[9,8,448]{2,1,0:T(8,128)}) custom-call(bf16[7200,768]{1,0:T(8,128)(2,1)} %bitcast.11, bf16[336,768]{1,0:T(8,128)(2,1)} %get-tuple-element.34.query_ref, ...), custom_call_target="tpu_custom_call" | custom-call | tf_op jit(solution)/shard_map/cross_forward/pallas_call | solution.py:1264
  62.5 25.3 %ffn.1 = (bf16[336,768]{1,0:T(8,128)(2,1)}, bf16[4,768,768]{2,1,0:T(8,128)(2,1)}, bf16[4,768,768]{2,1,0:T(8,128)(2,1)}, bf16[768,768]{1,0:T(8,128)(2,1)}, bf16[3...) custom-call(f32[336,768]{1,0:T(8,128)} %get-tuple-element.33.sum_ref, ...), custom_call_target="tpu_custom_call" | custom-call | tf_op jit(solution)/shard_map/ffn/pallas_call | solution.py:1279
  87.9 217.3 %backward.1 = (bf16[3600,768]{1,0:T(8,128)(2,1)}, bf16[336,768]{1,0:T(8,128)(2,1)}, bf16[16,192,384]{2,1,0:T(8,128)(2,1)}, f32[24,768]{1,0:T(8,128)}, f32[16,128...) custom-call(s32[4]{0:T(128)} %order_ref.1, bf16[7200,768]{1,0:T(8,128)(2,1)} %bitcast.12, ...), custom_call_target="tpu_custom_call" | custom-call | tf_op jit(solution)/shard_map/backward/pallas_call | solution.py:1354
  305.3 1.1 slice.25
  306.3 0.8 reshape.50
  307.2 0.8 slice_reduce_fusion
  308.0 0.7 reshape_squeeze.11
  308.6 1.4 slice.22
  310.0 1.3 slice.20
  311.4 0.7 slice.21
  312.1 0.6 reshape.51
  312.7 0.2 reshape.52
  312.9 3.1 all_gather.3
  316.1 1.1 copy.20
  317.1 5.1 %spread.1 = f32[192,16,384]{2,1,0:T(8,128)} custom-call(bf16[16,192,384]{2,1,0:T(8,128)(2,1)} %get-tuple-element.51.parts_ref), custom_call_target="tpu_custom_call" | custom-call | tf_op jit(solution)/shard_map/spread/pallas_call | solution.py:1423
  322.2 5.4 %copy.22 = bf16[1,3600,768]{2,1,0:T(8,128)(2,1)} copy(bf16[1,3600,768]{2,1,0:T(8,128)(2,1)} %bitcast.13) | data formatting | bytes 11059200
  327.6 0.0 copy-done.1
  (4 shorter events, 0.0 us)
Async XLA Ops:
  0.6 1.3 copy-start
  87.8 217.4 %copy-start.2 = (bf16[336,768]{1,0:T(8,128)(2,1)S(1)}, bf16[336,768]{1,0:T(8,128)(2,1)}, u32[]{:S(2)}) copy-start(bf16[336,768]{1,0:T(8,128)(2,1)} %get-tuple-element.36) | copy-start | bytes 1548292
  317.1 10.5 %copy-start.1 = (s32[1,6,100]{2,0,1:T(1,128)S(1)}, s32[1,6,100]{2,0,1:T(1,128)}, u32[]{:S(2)}) copy-start(s32[1,6,100]{2,0,1:T(1,128)} %param.13) | copy-start | bytes 7204

commit v4 on v3

--- a/solution.py
+++ b/solution.py
@@ -46,6 +46,14 @@
     return lax.dot_general(a, b, (((0,), (0,)), ((), ())), preferred_element_type=F32)
 
 
+def row_of(row_ref, which):
+    return row_ref[which // 2, which % 2 : which % 2 + 1].astype(F32)
+
+
+def gain_of(gain_ref, which):
+    return gain_ref[which : which + 1].astype(F32)
+
+
 def norm_parts(residual):
     row_mean = jnp.mean(residual, axis=-1, keepdims=True)
     centred = residual - row_mean
@@ -131,7 +139,23 @@
     return grad_query.astype(BF), grad_key.astype(BF), grad_value.astype(BF)
 
 
-def gather_kernel(own_ref, bias_ref, full_ref, full_bias_ref, turned, bias_own, remote_send,
+def pad_rows(source_ref, target_ref, images, valid):
+    first = lax.axis_index("tensor") == 0
+    padded = target_ref.shape[0] // images
+    for image in range(images):
+        here, there = (
+            source_ref[(core * images + image) * valid : (core * images + image + 1) * valid]
+            for core in range(2)
+        )
+        rows = jnp.where(first, here.astype(F32), there.astype(F32))
+        fill = jnp.zeros((padded - valid, rows.shape[1]), F32)
+        target_ref[image * padded : (image + 1) * padded] = jnp.concatenate(
+            [rows, fill], axis=0
+        ).astype(target_ref.dtype)
+
+
+def gather_kernel(images, valid, own_ref, bias_ref, queries_ref, cotangent_ref, full_ref,
+                  full_bias_ref, tokens_ref, own_cotangent_ref, turned, bias_own, remote_send,
                   remote_recv, local_sem):
     step, steps = pl.program_id(0), pl.num_programs(0)
     other = 1 - lax.axis_index("tensor")
@@ -163,7 +187,8 @@
         barrier = pltpu.get_barrier_semaphore()
         pl.semaphore_signal(barrier, inc=1, device_id={"tensor": other}, device_id_type=MESH_ID)
         pl.semaphore_wait(barrier, 1)
-        bias_own[...] = bias_ref[...]
+        bias_own[...] = jnp.zeros_like(bias_own)
+        bias_own[0 : bias_ref.shape[0]] = bias_ref[...]
         for copy in bias_copies():
             copy.start()
 
@@ -173,6 +198,8 @@
 
     @pl.when(step == steps - 1)
     def _():
+        pad_rows(queries_ref, tokens_ref, images, valid)
+        pad_rows(cotangent_ref, own_cotangent_ref, images, valid)
         for copy in bias_copies():
             copy.wait()
 
@@ -201,9 +228,9 @@
     tokens = tokens_ref[...]
     rows = tokens.shape[0] // images
     width = tokens.shape[1]
-    qkv_ref[0] = (mm(tokens, weight_ref[0]) + head_ref[0:1]).astype(BF)
+    qkv_ref[0] = (mm(tokens, weight_ref[0]) + head_ref[0:1].astype(F32)).astype(BF)
     qkv_ref[1] = mm(tokens, weight_ref[1]).astype(BF)
-    qkv_ref[2] = (mm(tokens, weight_ref[2]) + head_ref[1:2]).astype(BF)
+    qkv_ref[2] = (mm(tokens, weight_ref[2]) + head_ref[1:2].astype(F32)).astype(BF)
     for image in range(images):
         at = slice(image * rows, (image + 1) * rows)
         for group in range(width // SLAB):
@@ -215,17 +242,17 @@
             total_ref[image * (width // SLAB) + group] = jnp.broadcast_to(
                 log_total, total_ref.shape[1:]
             )
-    first_sum = tokens.astype(F32) + mm_nt(mixed_ref[...], weight_ref[3]) + row_ref[0:1]
+    first_sum = tokens.astype(F32) + mm_nt(mixed_ref[...], weight_ref[3]) + row_of(row_ref, 0)
     sum_ref[...] = first_sum
-    first_low = (norm_parts(first_sum)[0] * gain_ref[0:1] + row_ref[1:2]).astype(BF)
-    cross_query_ref[...] = (mm(first_low, weight_ref[4]) + head_ref[2:3]).astype(BF)
+    first_low = (norm_parts(first_sum)[0] * gain_of(gain_ref, 0) + row_of(row_ref, 1)).astype(BF)
+    cross_query_ref[...] = (mm(first_low, weight_ref[4]) + head_ref[2:3].astype(F32)).astype(BF)
 
 
 def cross_kernel(context_ref, query_ref, key_w_ref, value_w_ref, head_ref, key_ref, value_ref,
                  mixed_ref, total_ref):
     context = context_ref[...]
     key_ref[...] = mm(context, key_w_ref[0]).astype(BF)
-    value_ref[...] = (mm(context, value_w_ref[0]) + head_ref[3:4]).astype(BF)
+    value_ref[...] = (mm(context, value_w_ref[0]) + head_ref[3:4].astype(F32)).astype(BF)
     mixed, log_total = attend(query_ref[...], key_ref[...], value_ref[...], key_ref.shape[0])
     mixed_ref[...] = mixed.astype(BF)
     total_ref[0] = jnp.broadcast_to(log_total, total_ref.shape[1:])
@@ -235,25 +262,26 @@
     images, blocks, sum_ref, mixed_ref, cotangent_ref, matches_ref, counts_ref, cross_w_ref, in_ref,
     out_ref, head_ref, row_ref, gain_ref,
     block_ref, grad_in_ref, grad_out_ref, cross_grad_ref, mixed_grad_ref, residual_ref, small_ref,
-    second_sum, second_low_t, low_t, hidden, activated, branch, third_grad,
+    second_sum, second_low_t, low_t, hidden, activated, branch, third_grad, hidden_bias,
 ):
     step = pl.program_id(0)
     rows = sum_ref.shape[0] // images
 
     @pl.when(step == 0)
     def _():
-        first_out = norm_parts(sum_ref[...])[0] * gain_ref[0:1] + row_ref[1:2]
-        second_sum[...] = first_out + mm_nt(mixed_ref[...], cross_w_ref[0]) + row_ref[2:3]
+        first_out = norm_parts(sum_ref[...])[0] * gain_of(gain_ref, 0) + row_of(row_ref, 1)
+        second_sum[...] = first_out + mm_nt(mixed_ref[...], cross_w_ref[0]) + row_of(row_ref, 2)
         branch[...] = jnp.zeros_like(branch)
         small_ref[...] = jnp.zeros_like(small_ref)
+        hidden_bias[0:blocks] = head_ref[4 : 4 + blocks].astype(F32)
 
     def second_out():
-        return norm_parts(second_sum[...])[0] * gain_ref[1:2] + row_ref[3:4]
+        return norm_parts(second_sum[...])[0] * gain_of(gain_ref, 1) + row_of(row_ref, 3)
 
     @pl.when(step < blocks)
     def _():
         second_low = second_out().astype(BF)
-        pre = mm(second_low, in_ref[0]) + head_ref[pl.ds(4 + step, 1)]
+        pre = mm(second_low, in_ref[0]) + hidden_bias[pl.ds(step, 1)]
         hidden[step] = pre
         act = gelu_tanh(pre).astype(BF)
         activated[step] = act
@@ -263,20 +291,21 @@
     def _():
         second = second_out()
         second_low_t[...] = second.astype(BF).T
-        third_sum = second + branch[...] + row_ref[4:5]
+        third_sum = second + branch[...] + row_of(row_ref, 4)
         normed, scale = norm_parts(third_sum)
-        block_ref[...] = (normed * gain_ref[2:3] + row_ref[5:6]).astype(BF)
+        block_ref[...] = (normed * gain_of(gain_ref, 2) + row_of(row_ref, 5)).astype(BF)
         count = matches_ref.shape[2]
         slot = lax.broadcasted_iota(jnp.int32, (rows, count), 0)
         box = lax.broadcasted_iota(jnp.int32, (rows, count), 1)
         grads = []
         for image in range(images):
-            live = (matches_ref[image] == slot) & (box < counts_ref[image])
+            own = lax.axis_index("tensor") * images + image
+            live = (matches_ref[0, pl.ds(own, 1)] == slot) & (box < counts_ref[0, own])
             mask = jnp.sum(jnp.where(live, 1.0, 0.0), axis=1, keepdims=True)
             cot = cotangent_ref[image * rows : (image + 1) * rows].astype(F32)
             grads.append(cot * mask)
         out_grad = jnp.concatenate(grads, axis=0)
-        grad = norm_back(normed, scale, gain_ref[2:3], out_grad)
+        grad = norm_back(normed, scale, gain_of(gain_ref, 2), out_grad)
         third_grad[...] = grad
         low_t[...] = grad.astype(BF).T
         small_ref[12:13] = rows_sum(grad)
@@ -299,7 +328,7 @@
     def _():
         second_in = third_grad[...] + branch[...]
         normed, scale = norm_parts(second_sum[...])
-        grad = norm_back(normed, scale, gain_ref[1:2], second_in)
+        grad = norm_back(normed, scale, gain_of(gain_ref, 1), second_in)
         residual_ref[...] = grad
         small_ref[10:11] = rows_sum(grad)
         small_ref[11:12] = rows_sum(second_in)
@@ -310,9 +339,8 @@
 
 
 def cross_back_step(
-    image, group, images, groups, context_ref, query_ref, key_ref, value_ref, total_ref,
-    mixed_grad_ref, key_w_ref, value_w_ref, context_grad_ref, small_ref, context_t, acc, key_acc,
-    value_acc, unit,
+    image, group, context_ref, query_ref, key_ref, value_ref, total_ref, mixed_grad_ref, small_ref,
+    context_t, key_acc, value_acc, unit,
 ):
     @pl.when(group == 0)
     def _():
@@ -328,22 +356,7 @@
     small_ref[3:4, lanes] += rows_sum(grad_value.astype(F32))
     unit(1)
     key_wg = mm(context_t[...], grad_key)
-    unit(2)
     value_wg = mm(context_t[...], grad_value)
-    unit(3)
-    context_part = mm_nt(grad_key, key_w_ref[0]) + mm_nt(grad_value, value_w_ref[0])
-
-    @pl.when(group == 0)
-    def _():
-        acc[...] = context_part
-
-    @pl.when((group > 0) & (group < groups - 1))
-    def _():
-        acc[...] += context_part
-
-    @pl.when(group == groups - 1)
-    def _():
-        context_grad_ref[...] = (acc[...] + context_part).astype(BF)
 
     @pl.when(image == 0)
     def _():
@@ -355,7 +368,7 @@
         key_acc[:, lanes] += key_wg
         value_acc[:, lanes] += value_wg
 
-    return grad_query
+    return grad_query, grad_key, grad_value
 
 
 def cross_back_kernel(
@@ -370,11 +383,23 @@
     def _():
         small_ref[...] = jnp.zeros_like(small_ref)
 
-    query_grad_ref[...] = cross_back_step(
-        image, group, images, groups, context_ref, query_ref, key_ref, value_ref, total_ref,
-        mixed_grad_ref, key_w_ref, value_w_ref, context_grad_ref, small_ref, context_t, acc,
-        key_acc, value_acc, lambda part: None,
+    query_grad_ref[...], grad_key, grad_value = cross_back_step(
+        image, group, context_ref, query_ref, key_ref, value_ref, total_ref, mixed_grad_ref,
+        small_ref, context_t, key_acc, value_acc, lambda part: None,
     )
+    context_part = mm_nt(grad_key, key_w_ref[0]) + mm_nt(grad_value, value_w_ref[0])
+
+    @pl.when(group == 0)
+    def _():
+        acc[...] = context_part
+
+    @pl.when(group > 0)
+    def _():
+        acc[...] += context_part
+
+    @pl.when(group == groups - 1)
+    def _():
+        context_grad_ref[...] = acc[...].astype(BF)
 
     @pl.when((image == images - 1) & (group == groups - 1))
     def _():
@@ -390,12 +415,12 @@
     rows = tokens.shape[0] // images
     width = tokens.shape[1]
     normed, scale = norm_parts(sum_ref[...])
-    first_low = (normed * gain_ref[0:1] + row_ref[1:2]).astype(BF)
+    first_low = (normed * gain_of(gain_ref, 0) + row_of(row_ref, 1)).astype(BF)
     cross_query_grad = cross_query_grad_ref[...]
     emit(4, mm(first_low.T, cross_query_grad))
     unit()
     first_in = residual_ref[...] + mm_nt(cross_query_grad, weight_ref[4])
-    first_grad = norm_back(normed, scale, gain_ref[0:1], first_in)
+    first_grad = norm_back(normed, scale, gain_of(gain_ref, 0), first_in)
     small_ref[8:9] = rows_sum(first_grad)
     small_ref[9:10] = rows_sum(first_in)
     small_ref[14:15] = rows_sum(first_in * normed)
@@ -473,9 +498,9 @@
     pl.semaphore_wait(barrier, tasks + depth - 1)
 
 
-LAG = 3
-AHEAD = 2
-RING = 4
+LAG = 2
+AHEAD = 1
+RING = 2
 
 
 class Chain:
@@ -487,7 +512,6 @@
          self.part_send, self.part_recv) = refs
         self.chunks = self.passed.shape[1]
         self.rows, self.half = self.passed.shape[2:]
-        self.size = self.rows // 2
         self.me = lax.axis_index("dp")
         self.task = lax.axis_index("task")
         self.is_end = (self.me == 0) | (self.me == depth - 1)
@@ -500,18 +524,18 @@
         chunks = 2 * blocks
         dma = pltpu.SemaphoreType.DMA
         return [
-            pltpu.VMEM((RING, 2, rows // 2, half), BF),
-            pltpu.VMEM((RING, 2, rows // 2, half), BF),
+            pltpu.VMEM((RING, 2, rows, half), BF),
+            pltpu.VMEM((RING, 2, rows, half), BF),
             pltpu.VMEM((2, chunks, rows, half), BF),
             pltpu.VMEM((tasks, chunks, rows // tasks, half), BF),
             dma((RING, 2)),
             dma((RING, 2)),
             dma((2, blocks)),
             dma((2, blocks)),
-            dma((2, chunks, 2)),
-            dma((2, chunks, 2)),
-            dma((chunks, tasks - 1)),
-            dma((chunks, tasks - 1)),
+            dma((2, chunks)),
+            dma((2, chunks)),
+            dma((blocks, tasks - 1)),
+            dma((blocks, tasks - 1)),
         ]
 
     def far_copy(self, source, way, block):
@@ -537,30 +561,29 @@
                     self.far_copy(source.at[block, :, columns], way, base + block).start()
             base += source.shape[0]
 
-    def pass_copy(self, way, chunk, sub):
-        rows = pl.ds(pl.multiple_of(sub * self.size, self.size), self.size)
-        piece = self.passed.at[way, chunk, rows]
+    def pass_copy(self, way, chunk):
+        piece = self.passed.at[way, chunk]
         target = self.me - 1 if way == 0 else self.me + 1
         return send(
-            piece, piece, self.pass_send.at[way, chunk, sub], self.pass_recv.at[way, chunk, sub],
-            dp=target,
+            piece, piece, self.pass_send.at[way, chunk], self.pass_recv.at[way, chunk], dp=target
         )
 
     def part_rows(self, peer):
         size = self.rows // self.tasks
         return pl.ds(pl.multiple_of(peer * size, size), size)
 
-    def part_copy(self, way, chunk, shift, peer):
+    def part_copy(self, way, block, shift, peer):
+        chunks = pl.ds(2 * block, 2)
         return send(
-            self.passed.at[way, chunk, self.part_rows(peer)], self.parts.at[self.task, chunk],
-            self.part_send.at[chunk, shift], self.part_recv.at[chunk, shift], task=peer,
+            self.passed.at[way, chunks, self.part_rows(peer)], self.parts.at[self.task, chunks],
+            self.part_send.at[block, shift], self.part_recv.at[block, shift], task=peer,
         )
 
     def hops(self, way):
         return self.depth - 1 - self.me if way == 0 else self.me
 
     def units(self):
-        return 2 * self.chunks + LAG * (self.depth - 1)
+        return self.chunks + LAG * (self.depth - 1)
 
     def near_fetch(self, source, slot, way):
         return pltpu.make_async_copy(
@@ -575,19 +598,19 @@
     def fetch(self, index):
         slot = lax.rem(index, RING)
         for way in range(2):
-            at = index - LAG * self.hops(way)
-
-            @pl.when((at >= 0) & (at < 2 * self.chunks))
-            def _(way=way, at=at):
-                block = at // 4
-                place = at - 4 * block
+            chunk = index - LAG * self.hops(way)
+
+            @pl.when((chunk >= 0) & (chunk < self.chunks))
+            def _(way=way, chunk=chunk):
+                block = chunk // 2
+                place = chunk - 2 * block
 
                 @pl.when(place == 0)
                 def _():
                     self.far_arrival(way, block).wait_recv()
 
-                start = pl.multiple_of(place * self.size, self.size)
-                rows = pl.ds(way * 2 * self.rows + start, self.size)
+                start = pl.multiple_of(place * self.rows, self.rows)
+                rows = pl.ds(way * 2 * self.rows + start, self.rows)
                 base = 0
                 for source in self.sources:
                     count = source.shape[0]
@@ -604,74 +627,74 @@
                     self.near_fetch(self.near.at[block - base, rows], slot, way).start()
 
                 self.far_fetch(
-                    self.far.at[way, block, pl.ds(start, self.size)], slot, way
+                    self.far.at[way, block, pl.ds(start, self.rows)], slot, way
                 ).start()
 
     def unit(self, index):
         self.fetch(index + AHEAD)
         slot = lax.rem(index, RING)
         for way in range(2):
-            at = index - LAG * self.hops(way)
-
-            @pl.when((at >= 0) & (at < 2 * self.chunks))
-            def _(way=way, at=at):
-                chunk = at // 2
-                self.half_step(way, chunk, at - 2 * chunk, slot)
-
-    def half_step(self, way, chunk, sub, slot):
+            chunk = index - LAG * self.hops(way)
+
+            @pl.when((chunk >= 0) & (chunk < self.chunks))
+            def _(way=way, chunk=chunk):
+                self.chunk_step(way, chunk, slot)
+
+    def chunk_step(self, way, chunk, slot):
         first, last = self.hops(way) == 0, self.hops(way) == self.depth - 1
         piece = self.near_ring.at[slot, way]
         self.near_fetch(piece, slot, way).wait()
         self.far_fetch(piece, slot, way).wait()
-        rows = pl.ds(pl.multiple_of(sub * self.size, self.size), self.size)
         own = self.near_ring[slot, way].astype(F32) + self.far_ring[slot, way].astype(F32)
 
         @pl.when(first)
         def _():
-            self.passed[way, chunk, rows] = own.astype(BF)
+            self.passed[way, chunk] = own.astype(BF)
 
         @pl.when(jnp.logical_not(first))
         def _():
-            self.pass_copy(way, chunk, sub).wait_recv()
-            self.passed[way, chunk, rows] = (
-                own + self.passed[way, chunk, rows].astype(F32)
-            ).astype(BF)
+            self.pass_copy(way, chunk).wait_recv()
+            self.passed[way, chunk] = (own + self.passed[way, chunk].astype(F32)).astype(BF)
 
         @pl.when(jnp.logical_not(last))
         def _():
-            self.pass_copy(way, chunk, sub).start()
-
-        @pl.when(last & (sub == 1))
+            self.pass_copy(way, chunk).start()
+
+        block = chunk // 2
+
+        @pl.when(last & (chunk == 2 * block + 1))
         def _():
             for shift, peer in enumerate(task_peers(self.tasks)):
-                self.part_copy(way, chunk, shift, peer).start()
-            self.parts[self.task, chunk] = self.passed[way, chunk, self.part_rows(self.task)]
-
-    def wait_parts(self, chunk):
+                self.part_copy(way, block, shift, peer).start()
+            own_rows = self.part_rows(self.task)
+            self.parts[self.task, chunk - 1] = self.passed[way, chunk - 1, own_rows]
+            self.parts[self.task, chunk] = self.passed[way, chunk, own_rows]
+
+    def wait_parts(self, block):
         for shift, peer in enumerate(task_senders(self.tasks)):
-            landed = self.parts.at[peer, chunk]
+            landed = self.parts.at[peer, pl.ds(2 * block, 2)]
             send(
-                landed, landed, self.part_send.at[chunk, shift], self.part_recv.at[chunk, shift],
+                landed, landed, self.part_send.at[block, shift], self.part_recv.at[block, shift],
                 task=peer,
             ).wait_recv()
 
     def finish(self):
-        def chunks(chunk, carry):
+        def blocks(block, carry):
             for way in range(2):
 
                 @pl.when(self.hops(way) != self.depth - 1)
                 def _(way=way):
-                    for sub in range(2):
-                        self.pass_copy(way, chunk, sub).wait_send()
+                    for part in range(2):
+                        self.pass_copy(way, 2 * block + part).wait_send()
 
                 @pl.when(self.hops(way) == self.depth - 1)
                 def _(way=way):
                     for shift, peer in enumerate(task_peers(self.tasks)):
-                        self.part_copy(way, chunk, shift, peer).wait_send()
+                        self.part_copy(way, block, shift, peer).wait_send()
 
             return carry
 
-        lax.fori_loop(0, self.chunks, chunks, 0)
+        lax.fori_loop(0, self.chunks // 2, blocks, 0)
 
 
 def pairs_of(tasks):
@@ -697,35 +720,137 @@
 
 
 GROUPS = 4
-UNITS = 4
+UNITS = 2
+TILE = 240
+
+
+class ContextGrad:
+    def __init__(self, key_grad, value_grad, result, refs):
+        self.grads, self.result = (key_grad, value_grad), result
+        (self.weights, self.staged, self.ring, self.done, self.weight_sem, self.staged_sem,
+         self.ring_sem, self.done_sem) = refs
+        self.tile, width = self.done.shape[1:]
+        self.lanes = [pl.ds(0, width), pl.ds(width, width)]
+        self.tiles = result.shape[0] // self.tile
+
+    SCRATCH = 8
+
+    @staticmethod
+    def scratch(keys, width):
+        dma = pltpu.SemaphoreType.DMA
+        return [
+            pltpu.VMEM((width, 2 * width), BF),
+            pltpu.VMEM((2, 2, keys, SLAB), BF),
+            pltpu.VMEM((2, TILE, 2 * width), BF),
+            pltpu.VMEM((2, TILE, width), BF),
+            dma((2,)),
+            dma((2, 2)),
+            dma((2, 2)),
+            dma((2,)),
+        ]
+
+    def weight_copies(self, sources):
+        return [
+            pltpu.make_async_copy(source, self.weights.at[:, lanes], self.weight_sem.at[which])
+            for which, (source, lanes) in enumerate(zip(sources, self.lanes))
+        ]
+
+    def staged_copies(self, step, image, group):
+        slot = lax.rem(step, 2)
+        keys = self.staged.shape[2]
+        rows = pl.ds(pl.multiple_of(image * keys, keys), keys)
+        lanes = pl.ds(pl.multiple_of(group * SLAB, SLAB), SLAB)
+        return [
+            pltpu.make_async_copy(
+                self.staged.at[slot, which], self.grads[which].at[rows, lanes],
+                self.staged_sem.at[slot, which],
+            )
+            for which in range(2)
+        ]
+
+    def put(self, step, image, group, values):
+        @pl.when(step >= 2)
+        def _():
+            for copy in self.staged_copies(step, image, group):
+                copy.wait()
+
+        for which, value in enumerate(values):
+            self.staged[lax.rem(step, 2), which] = value
+        for copy in self.staged_copies(step, image, group):
+            copy.start()
+
+    def settle(self):
+        for step in range(2):
+            for copy in self.staged_copies(step, 0, 0):
+                copy.wait()
+
+    def fetches(self, index):
+        slot = lax.rem(index, 2)
+        rows = pl.ds(pl.multiple_of(index * self.tile, self.tile), self.tile)
+        return [
+            pltpu.make_async_copy(
+                self.grads[which].at[rows], self.ring.at[slot, :, self.lanes[which]],
+                self.ring_sem.at[slot, which],
+            )
+            for which in range(2)
+        ]
+
+    def store(self, index):
+        slot = lax.rem(index, 2)
+        rows = pl.ds(pl.multiple_of(index * self.tile, self.tile), self.tile)
+        return pltpu.make_async_copy(
+            self.done.at[slot], self.result.at[rows], self.done_sem.at[slot]
+        )
+
+    def compute(self, index):
+        @pl.when(index < self.tiles)
+        def _():
+            for copy in self.fetches(index):
+                copy.wait()
+
+            @pl.when(index + 1 < self.tiles)
+            def _():
+                for copy in self.fetches(index + 1):
+                    copy.start()
+
+            @pl.when(index >= 2)
+            def _():
+                self.store(index - 2).wait()
+
+            slot = lax.rem(index, 2)
+            self.done[slot] = mm_nt(self.ring[slot], self.weights[...]).astype(BF)
+            self.store(index).start()
+
+    def finish(self):
+        for index in range(self.tiles - 2, self.tiles):
+            self.store(jnp.int32(index)).wait()
 
 
 def back_kernel(
     depth, tasks, images, groups, valid, block_order, order_ref, context_ref, query_ref, key_ref,
-    value_ref, total_ref, mixed_grad_ref, key_w_ref, value_w_ref, tokens_ref, weight_ref, row_ref,
-    gain_ref, qkv_ref, mixed_ref, self_total_ref, sum_ref, residual_ref, small_in_ref, *refs
+    value_ref, total_ref, mixed_grad_ref, tokens_ref, weight_ref, row_ref,
+    gain_ref, qkv_ref, mixed_ref, self_total_ref, sum_ref, residual_ref, small_in_ref, all_w_ref,
+    block_ref, *refs
 ):
     sources, refs = refs[:3], refs[3:]
-    (context_grad_ref, query_grad_ref, update_ref, small_out_ref, gram_ref, near, far), refs = (
-        refs[:7], refs[7:],
+    (
+        context_grad_ref, query_grad_ref, update_ref, small_out_ref, gram_ref, block_far, near, far,
+        key_grad, value_grad,
+    ), refs = refs[:10], refs[10:]
+    (
+        context_t, key_acc, value_acc, cross_query_grad, qkv_grad, stage, stage_sem, block_sem,
+    ), refs = refs[:8], refs[8:]
+    context_back = ContextGrad(
+        key_grad, value_grad, context_grad_ref, refs[: ContextGrad.SCRATCH]
     )
-    (context_t, acc, key_acc, value_acc, cross_query_grad, qkv_grad, stage, stage_sem), refs = (
-        refs[:8], refs[8:],
-    )
+    refs = refs[ContextGrad.SCRATCH :]
     chain = Chain(depth, tasks, sources, near, far, refs[: Chain.SCRATCH])
     refs = refs[Chain.SCRATCH :]
-    (
-        small, small_own, small_other, small_far, small_pass, small_all, small_both, gram_acc,
-        gram_task, gram_core, gram_end, hop, out,
-        small_far_sem, small_pass_sem, small_task_sem, small_dp_sem, small_core_sem,
-        gram_task_sem, gram_core_sem, gram_dp_sem, hop_sem, out_sem, update_sem,
-    ) = refs
+    gram_acc = refs[7]
     step = pl.program_id(0)
     cross_steps = images * groups
-    me, task, core = (lax.axis_index(axis) for axis in ("dp", "task", "tensor"))
     half = chain.half
     is_end = chain.is_end
-    top = me == 0
     pairs = pairs_of(tasks)
 
     def add_products(shares):
@@ -738,20 +863,31 @@
 
     def unit(index):
         chain.unit(index)
-        since = index - LAG * (depth - 1) - 4
-        landed = since // 2
-
-        @pl.when(is_end & (since >= 0) & (since == 2 * landed))
+        since = index - LAG * (depth - 1) - 3
+        block = since // 2
+
+        @pl.when(is_end & (since >= 0) & (since == 2 * block))
         def _():
-            chain.wait_parts(landed)
-            add_products([chain.parts[t, landed].astype(F32) for t in range(tasks)])
+            chain.wait_parts(block)
+            for part in range(2):
+                add_products(
+                    [chain.parts[t, 2 * block + part].astype(F32) for t in range(tasks)]
+                )
+
+    block_copy = send(
+        block_ref, block_far, block_sem.at[0], block_sem.at[1], tensor=1 - lax.axis_index("tensor")
+    )
+    weight_copies = context_back.weight_copies([all_w_ref.at[5], all_w_ref.at[6]])
 
     @pl.when(step == 0)
     def _():
         greet(depth, tasks)
         chain.exchange()
+        block_copy.start()
+        for copy in weight_copies:
+            copy.start()
         gram_acc[...] = jnp.zeros_like(gram_acc)
-        small[...] = small_in_ref[...]
+        refs[0][...] = small_in_ref[...]
         for index in range(AHEAD):
             chain.fetch(index)
 
@@ -779,13 +915,59 @@
         copy.start()
         copy.wait()
 
-    def finish_reduction(done):
+    @pl.when(step < cross_steps)
+    def _():
+        image = step // groups
+        group = step - image * groups
+
+        def cross_unit(part):
+            if part == 0:
+                unit(step * UNITS)
+            else:
+
+                @pl.when(step < cross_steps - 1)
+                def _():
+                    unit(step * UNITS + part)
+
+        grad_query, *grads = cross_back_step(
+            image, group, context_ref, query_ref, key_ref, value_ref, total_ref, mixed_grad_ref,
+            refs[0], context_t, key_acc, value_acc, cross_unit,
+        )
+        context_back.put(step, image, group, grads)
+        rows = grad_query.shape[0]
+        cross_query_grad[
+            pl.ds(pl.multiple_of(image * rows, rows), rows),
+            pl.ds(pl.multiple_of(group * SLAB, SLAB), SLAB),
+        ] = grad_query
+
+        @pl.when(step == cross_steps - 1)
+        def _():
+            emit(0, key_acc[...])
+            emit(1, value_acc[...])
+
+    @pl.when(step == cross_steps)
+    def _():
+        calls, done = [0], [cross_steps * UNITS - 1]
+
+        def self_unit():
+            if calls[0] % 2 == 0:
+                unit(jnp.int32(done[0]))
+                done[0] += 1
+            calls[0] += 1
+
+        context_back.settle()
+        for copy in context_back.fetches(jnp.int32(0)):
+            copy.start()
+        for copy in weight_copies:
+            copy.wait()
+        positions = {4: 2, 3: 3, 0: 4, 1: 5, 2: 6}
+        query_grad_ref[...] = self_back(
+            images, valid, tokens_ref, weight_ref, row_ref, gain_ref, qkv_ref, mixed_ref,
+            self_total_ref, sum_ref, residual_ref, cross_query_grad, refs[0], qkv_grad,
+            lambda block, value: emit(positions[block], value), self_unit,
+        ).astype(BF)
         rest(
-            chain, unit, done, order_ref, update_ref, small_out_ref, gram_ref, small, small_own,
-            small_other, small_far, small_pass, small_all, small_both, gram_acc, gram_task,
-            gram_core, gram_end, hop, out, small_far_sem, small_pass_sem, small_task_sem,
-            small_dp_sem, small_core_sem, gram_task_sem, gram_core_sem, gram_dp_sem, hop_sem,
-            out_sem, update_sem,
+            chain, unit, context_back, done[0], order_ref, update_ref, small_out_ref, gram_ref, refs
         )
         for position in range(len(block_order) - given - slots, len(block_order) - given):
             for copy in stage_copies(position):
@@ -793,60 +975,19 @@
         for block in range(given):
             for way in range(2):
                 chain.far_arrival(way, block).wait_send()
-
-    @pl.when(step < cross_steps)
-    def _():
-        image = step // groups
-        group = step - image * groups
-
-        def cross_unit(part):
-            if part < 2:
-                unit(step * UNITS + part)
-            else:
-
-                @pl.when(step < cross_steps - 1)
-                def _():
-                    unit(step * UNITS + part)
-
-        grad_query = cross_back_step(
-            image, group, images, groups, context_ref, query_ref, key_ref, value_ref, total_ref,
-            mixed_grad_ref, key_w_ref, value_w_ref, context_grad_ref, small, context_t, acc,
-            key_acc, value_acc, cross_unit,
-        )
-        rows = grad_query.shape[0]
-        cross_query_grad[
-            pl.ds(pl.multiple_of(image * rows, rows), rows),
-            pl.ds(pl.multiple_of(group * SLAB, SLAB), SLAB),
-        ] = grad_query
-
-        @pl.when(step == cross_steps - 1)
-        def _():
-            emit(0, key_acc[...])
-            emit(1, value_acc[...])
-
-    @pl.when(step == cross_steps)
-    def _():
-        done = [cross_steps * UNITS - 2]
-
-        def self_unit():
-            unit(jnp.int32(done[0]))
-            done[0] += 1
-
-        positions = {4: 2, 3: 3, 0: 4, 1: 5, 2: 6}
-        query_grad_ref[...] = self_back(
-            images, valid, tokens_ref, weight_ref, row_ref, gain_ref, qkv_ref, mixed_ref,
-            self_total_ref, sum_ref, residual_ref, cross_query_grad, small, qkv_grad,
-            lambda block, value: emit(positions[block], value), self_unit,
-        ).astype(BF)
-        finish_reduction(done[0])
+        block_copy.wait()
+        context_back.finish()
 
 
 def rest(
-    chain, unit, done, order_ref, update_ref, small_out_ref, gram_ref, small, small_own, small_other,
-    small_far, small_pass, small_all, small_both, gram_acc, gram_task, gram_core, gram_end, hop, out,
-    small_far_sem, small_pass_sem, small_task_sem, small_dp_sem, small_core_sem, gram_task_sem,
-    gram_core_sem, gram_dp_sem, hop_sem, out_sem, update_sem,
+    chain, unit, context_back, done, order_ref, update_ref, small_out_ref, gram_ref, refs
 ):
+    (
+        small, small_own, small_other, small_far, small_pass, small_all, small_both, gram_acc,
+        gram_task, gram_core, gram_end, hop, out,
+        small_far_sem, small_pass_sem, small_task_sem, small_dp_sem, small_core_sem,
+        gram_task_sem, gram_core_sem, gram_dp_sem, hop_sem, out_sem, update_sem,
+    ) = refs
     depth, tasks, half = chain.depth, chain.tasks, chain.half
     me, task, core = (lax.axis_index(axis) for axis in ("dp", "task", "tensor"))
     is_end = chain.is_end
@@ -876,6 +1017,7 @@
 
     def step(index, carry):
         unit(index)
+        context_back.compute(index - done)
 
         @pl.when(index == done + 1 + LAG * chain.hops(0))
         def _():
@@ -903,7 +1045,7 @@
 
         return carry
 
-    lax.fori_loop(done, chain.units() + 4, step, 0)
+    lax.fori_loop(done, max(chain.units() + 2, done + context_back.tiles), step, 0)
 
     @pl.when(top)
     def _():
@@ -1137,9 +1279,38 @@
             out_copy(index, shift, peer).wait_send()
 
 
-def spread_kernel(block_order, parts_ref, update_ref):
+def spread_kernel(
+    images, valid, tasks, block_order, parts_ref, context_grad_ref, query_grad_ref, block_ref,
+    block_far_ref, small_ref, gram_in_ref,
+    update_ref, context_out_ref, query_out_ref, block_out_ref, head_ref, row_ref, gain_ref, gram_ref,
+):
     for index, block in enumerate(block_order):
         update_ref[:, block, :] = parts_ref[index].astype(F32)
+    context_out_ref[...] = context_grad_ref[...]
+
+    @pl.when(pl.program_id(0) == 0)
+    def _():
+        padded = query_grad_ref.shape[0] // images
+        first = lax.axis_index("tensor") == 0
+
+        def rows(ref, image):
+            return ref[image * padded : (image + 1) * padded].astype(F32)[:valid]
+
+        for image in range(images):
+            at = slice(image * valid, (image + 1) * valid)
+            after = slice((images + image) * valid, (images + image + 1) * valid)
+            query_out_ref[at] = rows(query_grad_ref, image).astype(BF)
+            near, far = rows(block_ref, image), rows(block_far_ref, image)
+            block_out_ref[at] = jnp.where(first, near, far).astype(BF)
+            block_out_ref[after] = jnp.where(first, far, near).astype(BF)
+        head_ref[...] = small_ref[0:8, 0 : head_ref.shape[1]]
+        for which in range(6):
+            row_ref[which // 2, which % 2 : which % 2 + 1] = small_ref[8 + which : 9 + which]
+        gain_ref[...] = small_ref[14:17]
+        for a in range(tasks):
+            for b in range(tasks):
+                at = a * tasks + b
+                gram_ref[a : a + 1, b : b + 1] = gram_in_ref[at : at + 1, 0:1]
 
 
 def gram_kernel(parts_ref, gram_ref):
@@ -1182,32 +1353,27 @@
     stack = GROUP * padded
     core = lax.axis_index("tensor")
 
-    def own_rows(array):
-        split = array[0].reshape(all_images, valid, width)
-        mine = lax.dynamic_slice_in_dim(split, core * images, images, 0)
-        return jnp.pad(mine, ((0, 0), (0, padded - valid), (0, 0))).reshape(rows, width)
-
-    tokens = own_rows(queries)
-    own_cotangent = own_rows(cotangent)
-    own_matches = lax.dynamic_slice_in_dim(matches[0], core * images, images, 0)[:, None, :]
-    own_counts = lax.dynamic_slice_in_dim(counts[0], core * images, images, 0)
-    context = memory[0]
-    row_f = jnp.pad(row_bias.astype(F32).reshape(6, width), ((0, 2), (0, 0)))
-    gain_f = jnp.pad(norm_gain.astype(F32), ((0, 5), (0, 0)))
-    own_bias = jnp.pad(head_bias, ((0, 8), (0, 0)))
     chunk = 96
-    weights, full_bias = pl.pallas_call(
-        gather_kernel,
+    weights, head_rows, tokens, own_cotangent = pl.pallas_call(
+        functools.partial(gather_kernel, images, valid),
         grid=(width // chunk,),
         out_shape=(
             jax.ShapeDtypeStruct((block_count, width, cores * half), BF),
             jax.ShapeDtypeStruct((16, cores * half), BF),
+            jax.ShapeDtypeStruct((rows, width), BF),
+            jax.ShapeDtypeStruct((rows, width), BF),
         ),
         in_specs=[
             pl.BlockSpec((chunk, block_count, half), lambda i: (i, 0, 0)),
-            pl.BlockSpec((16, half), lambda i: (0, 0)),
+            pl.BlockSpec((8, half), lambda i: (0, 0)),
+            pl.BlockSpec((None, *queries.shape[1:]), lambda i: (0, 0, 0)),
+            pl.BlockSpec((None, *queries.shape[1:]), lambda i: (0, 0, 0)),
         ],
-        out_specs=(any_spec(), any_spec()),
+        out_specs=(
+            any_spec(), any_spec(),
+            pl.BlockSpec((rows, width), lambda i: (0, 0)),
+            pl.BlockSpec((rows, width), lambda i: (0, 0)),
+        ),
         scratch_shapes=[
             pltpu.VMEM((block_count, width, half), BF),
             pltpu.VMEM((16, half), BF),
@@ -1217,8 +1383,7 @@
         ],
         compiler_params=params_for(collective_id=0, has_side_effects=True),
         name="gather_weights",
-    )(params, own_bias)
-    head_f = full_bias.astype(F32)
+    )(params, head_bias, queries, cotangent)
 
     def const(shape, *index):
         return pl.BlockSpec(shape, lambda *_: index)
@@ -1229,7 +1394,8 @@
     small_shape = jax.ShapeDtypeStruct((24, width), F32)
     one_block = jax.ShapeDtypeStruct((width, width), BF)
     small_spec = const((24, width), 0, 0)
-    vec8 = const((8, width), 0, 0)
+    row_spec = const(row_bias.shape, 0, 0, 0)
+    gain_spec = const(norm_gain.shape, 0, 0)
     head_spec = const((16, width), 0, 0)
     rows_spec = const((rows, width), 0, 0)
 
@@ -1239,20 +1405,20 @@
         out_shape=(
             jax.ShapeDtypeStruct((3, rows, width), BF), low_rows, total_shape, full_rows, low_rows,
         ),
-        in_specs=[rows_spec, const((5, width, width), 0, 0, 0), head_spec, vec8, vec8],
+        in_specs=[rows_spec, const((5, width, width), 0, 0, 0), head_spec, row_spec, gain_spec],
         out_specs=(
             const((3, rows, width), 0, 0, 0), rows_spec, const(total_shape.shape, 0, 0, 0),
             rows_spec, rows_spec,
         ),
         compiler_params=params_for(),
         name="self_forward",
-    )(tokens, weights, head_f, row_f, gain_f)
+    )(tokens, weights, head_rows, row_bias, norm_gain)
 
 
     def own_image(i, g):
-        return lax.axis_index("tensor") * images + i, 0
-
-    context_all = pl.BlockSpec((keys, width), own_image)
+        return 0, lax.axis_index("tensor") * images + i, 0
+
+    context_all = pl.BlockSpec((None, keys, width), own_image)
     slab_q = pl.BlockSpec((padded, SLAB), lambda i, g: (i, g))
     slab_k = pl.BlockSpec((keys, SLAB), lambda i, g: (i, g))
     slab_t = pl.BlockSpec((1, 8, stack), lambda i, g: (i * groups + g, 0, 0))
@@ -1272,7 +1438,7 @@
         out_shape=(key_rows, key_rows, low_rows, total_shape),
         compiler_params=params_for(),
         name="cross_forward",
-    )(context, cross_query, weights, weights, head_f)
+    )(memory, cross_query, weights, weights, head_rows)
 
     (
         block_rows, grad_in, grad_out, cross_out_wg, mixed_grad, second_grad, ffn_small,
@@ -1287,12 +1453,12 @@
         ),
         in_specs=[
             rows_spec, rows_spec, rows_spec,
-            const(own_matches.shape, 0, 0, 0),
+            const(matches.shape, 0, 0, 0),
             pl.BlockSpec(memory_space=pltpu.SMEM),
             const((1, width, width), 7, 0, 0),
             pl.BlockSpec((1, width, width), lambda s: (8 + s % blocks, 0, 0)),
             pl.BlockSpec((1, width, width), lambda s: (8 + blocks + s % blocks, 0, 0)),
-            head_spec, vec8, vec8,
+            head_spec, row_spec, gain_spec,
         ],
         out_specs=(
             rows_spec,
@@ -1308,21 +1474,18 @@
             pltpu.VMEM((blocks, rows, width), BF),
             pltpu.VMEM((rows, width), F32),
             pltpu.VMEM((rows, width), F32),
+            pltpu.VMEM((8, width), F32),
         ],
         compiler_params=params_for(),
         name="ffn",
     )(
-        first_sum, cross_mixed, own_cotangent, own_matches, own_counts, weights, weights, weights,
-        head_f, row_f, gain_f,
+        first_sum, cross_mixed, own_cotangent, matches, counts, weights, weights, weights,
+        head_rows, row_bias, norm_gain,
     )
 
     depth, tasks = lax.axis_size("dp"), lax.axis_size("task")
     by_chain = depth == 4 and tasks == 4 and cores == 2
 
-    def unpad(array):
-        return array.reshape(images, padded, width)[:, :valid].reshape(1, images * valid, width)
-
-    block_out = lax.all_gather(unpad(block_rows), "tensor", axis=1, tiled=True)
     if by_chain:
         block_order = [*range(8, block_count), 7, 5, 6, 4, 3, 0, 1, 2]
         chain_rows = width // depth
@@ -1345,12 +1508,9 @@
         step_q = pl.BlockSpec((padded, SLAB), at_step(lambda i, g: (i, g)))
         step_k = pl.BlockSpec((keys, SLAB), at_step(lambda i, g: (i, g)))
 
-        def step_w(block):
-            return pl.BlockSpec((1, width, SLAB), at_step(lambda i, g: (block, 0, g)))
-
         small_half = pltpu.VMEM((24, half), F32)
         (
-            context_grad, token_grad, update_parts, small_out, gram_rows, _, _,
+            context_grad, token_grad, update_parts, small_out, gram_rows, block_far, *_,
         ) = pl.pallas_call(
             functools.partial(
                 back_kernel, depth, tasks, images, groups, valid, block_order
@@ -1361,34 +1521,37 @@
                 jax.ShapeDtypeStruct((block_count, chain_rows, half), BF),
                 small_shape,
                 jax.ShapeDtypeStruct((16, 128), F32),
+                low_rows,
                 jax.ShapeDtypeStruct((7, width, half), BF),
                 jax.ShapeDtypeStruct((2, block_count, width // 2, half), BF),
+                key_rows, key_rows,
             ),
             in_specs=[
                 pl.BlockSpec(memory_space=pltpu.SMEM),
-                pl.BlockSpec((keys, width), at_step(own_image)),
+                pl.BlockSpec((None, keys, width), at_step(own_image)),
                 step_q, step_k, step_k,
                 pl.BlockSpec((1, 8, stack), at_step(lambda i, g: (i * groups + g, 0, 0))),
-                step_q, step_w(5), step_w(6),
-                once((rows, width)), once((5, width, width)), once((8, width)), once((8, width)),
+                step_q,
+                once((rows, width)), once((5, width, width)), once(row_bias.shape),
+                once(norm_gain.shape),
                 once((3, rows, width)), once((rows, width)), once(total_shape.shape),
                 once((rows, width)), once((rows, width)), once((24, width)),
-                any_spec(), any_spec(), any_spec(),
+                any_spec(), any_spec(), any_spec(), any_spec(), any_spec(),
             ],
             out_specs=(
-                pl.BlockSpec((keys, width), at_step(lambda i, g: (i, 0))),
-                once((rows, width)), any_spec(), once((24, width)), once((16, 128)),
-                any_spec(), any_spec(),
+                any_spec(), once((rows, width)), any_spec(), once((24, width)), once((16, 128)),
+                *[any_spec()] * 5,
             ),
             scratch_shapes=[
                 pltpu.VMEM((width, keys), BF),
-                pltpu.VMEM((keys, width), F32),
                 pltpu.VMEM((width, width), F32),
                 pltpu.VMEM((width, width), F32),
                 pltpu.VMEM((rows, width), BF),
                 pltpu.VMEM((3, rows, width), BF),
                 pltpu.VMEM((3, width, width), BF),
                 dma(()),
+                dma((2,)),
+                *ContextGrad.scratch(keys, width),
                 *Chain.scratch(block_count, chain_rows, half, tasks),
                 pltpu.VMEM((24, width), F32),
                 small_half, small_half, small_half, small_half,
@@ -1415,26 +1578,52 @@
             compiler_params=params_for(collective_id=1, has_side_effects=True),
             name="backward",
         )(
-            task_order, context, cross_query, keys_act, values_act, cross_total, mixed_grad, weights,
-            weights, tokens, weights, row_f, gain_f, qkv, self_mixed, self_total, first_sum,
-            second_grad, ffn_small, grad_in, grad_out, cross_out_wg[None],
-        )
-        tile = chain_rows // 4
-        param_update = pl.pallas_call(
-            functools.partial(spread_kernel, block_order),
-            grid=(4,),
-            out_shape=jax.ShapeDtypeStruct((chain_rows, block_count, half), F32),
-            in_specs=[pl.BlockSpec((block_count, tile, half), lambda r: (0, r, 0))],
-            out_specs=pl.BlockSpec((tile, block_count, half), lambda r: (r, 0, 0)),
+            task_order, memory, cross_query, keys_act, values_act, cross_total, mixed_grad,
+            tokens, weights, row_bias, norm_gain, qkv, self_mixed, self_total, first_sum,
+            second_grad, ffn_small, weights, block_rows, grad_in, grad_out, cross_out_wg[None],
+        )
+        tile = chain_rows // images
+        (
+            param_update, memory_grad, query_grad, block_out, head_update, row_update, gain_update,
+            gram,
+        ) = pl.pallas_call(
+            functools.partial(spread_kernel, images, valid, tasks, block_order),
+            grid=(images,),
+            out_shape=(
+                jax.ShapeDtypeStruct((chain_rows, block_count, half), F32),
+                key_rows,
+                jax.ShapeDtypeStruct((images * valid, width), BF),
+                jax.ShapeDtypeStruct((all_images * valid, width), BF),
+                jax.ShapeDtypeStruct((8, half), F32),
+                jax.ShapeDtypeStruct((3, 2, width), F32),
+                jax.ShapeDtypeStruct((3, width), F32),
+                jax.ShapeDtypeStruct((tasks, tasks), F32),
+            ),
+            in_specs=[
+                pl.BlockSpec((block_count, tile, half), lambda r: (0, r, 0)),
+                pl.BlockSpec((keys, width), lambda r: (r, 0)),
+                rows_spec, rows_spec, rows_spec, small_spec, const((16, 128), 0, 0),
+            ],
+            out_specs=(
+                pl.BlockSpec((tile, block_count, half), lambda r: (r, 0, 0)),
+                pl.BlockSpec((keys, width), lambda r: (r, 0)),
+                const((images * valid, width), 0, 0),
+                const((all_images * valid, width), 0, 0),
+                const((8, half), 0, 0), const((3, 2, width), 0, 0, 0),
+                const((3, width), 0, 0), const((tasks, tasks), 0, 0),
+            ),
             compiler_params=params_for(),
             name="spread",
-        )(update_parts)
+        )(update_parts, context_grad, token_grad, block_rows, block_far, small_out, gram_rows)
         return (
-            block_out, unpad(token_grad), context_grad[None], param_update, small_out[:8, :half],
-            small_out[8:14].reshape(3, 2, width), small_out[14:17],
-            gram_rows[: tasks * tasks, 0].reshape(tasks, tasks),
-        )
-
+            block_out[None], query_grad[None], memory_grad[None], param_update, head_update,
+            row_update, gain_update, gram,
+        )
+
+    def unpad(array):
+        return array.reshape(images, padded, width)[:, :valid].reshape(1, images * valid, width)
+
+    block_out = lax.all_gather(unpad(block_rows), "tensor", axis=1, tiled=True)
     cross_query_grad, context_grad, key_wg, value_wg, cross_small = pl.pallas_call(
         cross_back_kernel,
         grid=(images, groups),
@@ -1455,7 +1644,7 @@
         out_shape=(low_rows, key_rows, one_block, one_block, small_shape),
         compiler_params=params_for(),
         name="cross_backward",
-    )(context, cross_query, keys_act, values_act, cross_total, mixed_grad, weights, weights)
+    )(memory, cross_query, keys_act, values_act, cross_total, mixed_grad, weights, weights)
 
     token_grad, self_wg, self_small = pl.pallas_call(
         functools.partial(self_back_kernel, images, valid),
@@ -1464,7 +1653,7 @@
             low_rows, jax.ShapeDtypeStruct((5, width, width), BF), small_shape,
         ),
         in_specs=[
-            rows_spec, const((5, width, width), 0, 0, 0), vec8, vec8,
+            rows_spec, const((5, width, width), 0, 0, 0), row_spec, gain_spec,
             const((3, rows, width), 0, 0, 0), rows_spec, const(total_shape.shape, 0, 0, 0),
             rows_spec, rows_spec, rows_spec,
         ],
@@ -1475,7 +1664,7 @@
         compiler_params=params_for(),
         name="self_backward",
     )(
-        tokens, weights, row_f, gain_f, qkv, self_mixed, self_total, first_sum, second_grad,
+        tokens, weights, row_bias, norm_gain, qkv, self_mixed, self_total, first_sum, second_grad,
         cross_query_grad,
     )
 

time: 327 us -> 289 us (0.88)
  local copies, waits for them, and re-layouts: 22.3 us -> 1.28 us
  Pallas kernels: 299 us -> 288 us
    pallas_call x1, Pallas kernels: 217 us -> 200 us  [body(): pl.pallas_call(functools.partial(back_kernel, depth, tasks, images, group...]
    pallas_call x2, Pallas kernels: 21.7 us -> 28.1 us  [the longest x1 18.2 us: body(): pl.pallas_call(functools.partial(gather_kernel, images, valid), grid=(wid...]
    slice x6 -> x0, local copies, waits for them, and re-layouts: 5.35 us -> none  [the longest x1 1.4 us: body(): small_out[14:17]]
    unnamed x8 -> x1, local copies, waits for them, and re-layouts: 6.45 us -> 1.28 us
where the time goes in v4:
time: 289 us; the launch traced here: 290 us
  Pallas kernels  288 us (100%)
    pallas_call x1, Pallas kernels, body(): pl.pallas_call(functools.partial(back_kernel, depth, tasks, images, group...  200 us
    pallas_call x1, Pallas kernels, body(): pl.pallas_call(cross_kernel, grid=(images, groups), in_specs=[context_all...  25.6 us
    pallas_call x1, Pallas kernels, body(): pl.pallas_call(functools.partial(ffn_kernel, images, blocks), grid=(2 * b...  25.2 us
    pallas_call x1, Pallas kernels, body(): pl.pallas_call(functools.partial(gather_kernel, images, valid), grid=(wid...  18.2 us
    pallas_call x1, Pallas kernels, body(): pl.pallas_call(functools.partial(spread_kernel, images, valid, tasks, blo...  9.95 us
    pallas_call x1, Pallas kernels, body(): pl.pallas_call(functools.partial(self_kernel, images, valid), grid=(1,),...  8.89 us

profile of v4, /device:TPU:8, one launch (start us, length us, event | category | flops | bytes accessed | tf_op | source)
XLA Modules:
  0.0 290.2 jit_solution(6405284716873398231)
XLA Ops:
  0.6 1.3 copy.18.matches_ref
  1.9 18.2 %gather_weights.1 = (bf16[16,768,768]{2,1,0:T(8,128)(2,1)}, bf16[16,768]{1,0:T(8,128)(2,1)}, bf16[336,768]{1,0:T(8,128)(2,1)}, bf16[336,768]{1,0:T(8,128)(2,1)}) custom-call(bf16[768,16,384]{2,1,0:T(8,128)(2,1)} %own_ref.1, bf16[8,384]{1,0:T(8,128)(2,1)} %bias_ref.1, bf16[1,600,768]{2,1,0:T(8,128)(2,1)} %queries_ref.1, bf16[1,600,768]{2,1,0:T(8,128)(2,1)} %cotangent_ref.1), custom_call_target="tpu_custom_call" | custom-call | tf_op jit(solution)/shard_map/gather_weights/pallas_call | solution.py:1357
  20.1 8.9 %self_forward.1 = (bf16[3,336,768]{2,1,0:T(8,128)(2,1)}, bf16[336,768]{1,0:T(8,128)(2,1)}, f32[9,8,448]{2,1,0:T(8,128)}, f32[336,768]{1,0:T(8,128)}, bf16[336,768]{1,0:T(8,128)(2,1)}) custom-call(bf16[336,768]{1,0:T(8,128)(2,1)} %get-tuple-element.42.tokens_ref, ...), custom_call_target="tpu_custom_call" | custom-call | tf_op jit(solution)/shard_map/self_forward/pallas_call | solution.py:1402
  29.0 25.6 %cross_forward.1 = (bf16[3600,768]{1,0:T(8,128)(2,1)}, bf16[3600,768]{1,0:T(8,128)(2,1)}, bf16[336,768]{1,0:T(8,128)(2,1)}, f32[9,8,448]{2,1,0:T(8,128)}) custom-call(bf16[1,7200,768]{2,1,0:T(8,128)(2,1)} %context_ref.3, bf16[336,768]{1,0:T(8,128)(2,1)} %get-tuple-element.45.query_ref, ...), custom_call_target="tpu_custom_call" | custom-call | tf_op jit(solution)/shard_map/cross_forward/pallas_call | solution.py:1430
  54.6 25.2 %ffn.1 = (bf16[336,768]{1,0:T(8,128)(2,1)}, bf16[4,768,768]{2,1,0:T(8,128)(2,1)}, bf16[4,768,768]{2,1,0:T(8,128)(2,1)}, bf16[768,768]{1,0:T(8,128)(2,1)}, bf16[3...) custom-call(f32[336,768]{1,0:T(8,128)} %get-tuple-element.49.sum_ref, ...), custom_call_target="tpu_custom_call" | custom-call | tf_op jit(solution)/shard_map/ffn/pallas_call | solution.py:1445
  79.8 200.2 %backward.1 = (bf16[3600,768]{1,0:T(8,128)(2,1)}, bf16[336,768]{1,0:T(8,128)(2,1)}, bf16[16,192,384]{2,1,0:T(8,128)(2,1)}, f32[24,768]{1,0:T(8,128)}, f32[16,128...) custom-call(s32[4]{0:T(128)} %order_ref.1, ...), custom_call_target="tpu_custom_call" | custom-call | tf_op jit(solution)/shard_map/backward/pallas_call | solution.py:1514
  280.0 10.0 %spread.1 = (f32[192,16,384]{2,1,0:T(8,128)}, bf16[3600,768]{1,0:T(8,128)(2,1)}, bf16[300,768]{1,0:T(8,128)(2,1)}, bf16[600,768]{1,0:T(8,128)(2,1)}, f32[8,384]{...) custom-call(bf16[16,192,384]{2,1,0:T(8,128)(2,1)} %get-tuple-element.62.parts_ref, ...), custom_call_target="tpu_custom_call" | custom-call | tf_op jit(solution)/shard_map/spread/pallas_call | solution.py:1589

commit v5 on v4

--- a/solution.py
+++ b/solution.py
@@ -74,18 +74,11 @@
 
 
 def gelu_tanh(hidden):
-    return (
-        0.5
-        * hidden
-        * (1.0 + jnp.tanh(0.7978845608028654 * (hidden + 0.044715 * hidden * hidden * hidden)))
-    )
-
-
-def gelu_slope(hidden):
     square = hidden * hidden
-    tanh = jnp.tanh(0.7978845608028654 * (hidden + 0.044715 * hidden * square))
-    inner = 0.7978845608028654 * (1.0 + 3 * 0.044715 * square)
-    return 0.5 * (1.0 + tanh) + 0.5 * hidden * (1.0 - tanh * tanh) * inner
+    tanh = jnp.tanh(hidden * (0.7978845608028654 + 0.7978845608028654 * 0.044715 * square))
+    half = 0.5 * (1.0 + tanh)
+    inner = 0.7978845608028654 + 0.7978845608028654 * 3 * 0.044715 * square
+    return hidden * half, half + 0.5 * hidden * (1.0 - tanh * tanh) * inner
 
 
 def head_mask(head, rows, dtype):
@@ -261,36 +254,58 @@
 def ffn_kernel(
     images, blocks, sum_ref, mixed_ref, cotangent_ref, matches_ref, counts_ref, cross_w_ref, in_ref,
     out_ref, head_ref, row_ref, gain_ref,
-    block_ref, grad_in_ref, grad_out_ref, cross_grad_ref, mixed_grad_ref, residual_ref, small_ref,
-    second_sum, second_low_t, low_t, hidden, activated, branch, third_grad, hidden_bias,
+    block_ref, left_ref, right_ref, mixed_grad_ref, residual_ref, small_ref,
+    second_sum, second_low, left, right, slope, branch, third_grad, hidden_bias, left_sem, right_sem,
 ):
     step = pl.program_id(0)
+    per = in_ref.shape[0]
+    half_steps = blocks // per
     rows = sum_ref.shape[0] // images
 
+    def left_copy(which):
+        return pltpu.make_async_copy(left.at[which], left_ref.at[which], left_sem.at[which])
+
+    def right_copy(which):
+        return pltpu.make_async_copy(right.at[which], right_ref.at[which], right_sem.at[which])
+
+    mixed_copy = pltpu.make_async_copy(
+        mixed_ref, right_ref.at[2 * blocks], right_sem.at[2 * blocks]
+    )
+
     @pl.when(step == 0)
     def _():
+        mixed_copy.start()
         first_out = norm_parts(sum_ref[...])[0] * gain_of(gain_ref, 0) + row_of(row_ref, 1)
-        second_sum[...] = first_out + mm_nt(mixed_ref[...], cross_w_ref[0]) + row_of(row_ref, 2)
+        second = first_out + mm_nt(mixed_ref[...], cross_w_ref[0]) + row_of(row_ref, 2)
+        second_sum[...] = second
+        second_low[...] = (
+            norm_parts(second)[0] * gain_of(gain_ref, 1) + row_of(row_ref, 3)
+        ).astype(BF)
         branch[...] = jnp.zeros_like(branch)
         small_ref[...] = jnp.zeros_like(small_ref)
         hidden_bias[0:blocks] = head_ref[4 : 4 + blocks].astype(F32)
-
-    def second_out():
-        return norm_parts(second_sum[...])[0] * gain_of(gain_ref, 1) + row_of(row_ref, 3)
-
-    @pl.when(step < blocks)
-    def _():
-        second_low = second_out().astype(BF)
-        pre = mm(second_low, in_ref[0]) + hidden_bias[pl.ds(step, 1)]
-        hidden[step] = pre
-        act = gelu_tanh(pre).astype(BF)
-        activated[step] = act
-        branch[...] += mm_nt(act, out_ref[0])
-
-    @pl.when(step == blocks - 1)
-    def _():
-        second = second_out()
-        second_low_t[...] = second.astype(BF).T
+        left[0] = second_low[...].T
+        left_copy(0).start()
+
+    @pl.when(step < half_steps)
+    def _():
+        low = second_low[...]
+        pres = [
+            mm(low, in_ref[k]) + hidden_bias[pl.ds(step * per + k, 1)] for k in range(per)
+        ]
+        total = branch[...]
+        for k in range(per):
+            act, grad = gelu_tanh(pres[k])
+            act = act.astype(BF)
+            slope[step * per + k] = grad
+            right[blocks + step * per + k] = act
+            right_copy(blocks + step * per + k).start()
+            total = total + mm_nt(act, out_ref[k])
+        branch[...] = total
+
+    @pl.when(step == half_steps - 1)
+    def _():
+        second = norm_parts(second_sum[...])[0] * gain_of(gain_ref, 1) + row_of(row_ref, 3)
         third_sum = second + branch[...] + row_of(row_ref, 4)
         normed, scale = norm_parts(third_sum)
         block_ref[...] = (normed * gain_of(gain_ref, 2) + row_of(row_ref, 5)).astype(BF)
@@ -307,24 +322,28 @@
         out_grad = jnp.concatenate(grads, axis=0)
         grad = norm_back(normed, scale, gain_of(gain_ref, 2), out_grad)
         third_grad[...] = grad
-        low_t[...] = grad.astype(BF).T
+        left[1] = grad.astype(BF).T
+        left_copy(1).start()
         small_ref[12:13] = rows_sum(grad)
         small_ref[13:14] = rows_sum(out_grad)
         small_ref[16:17] = rows_sum(out_grad * normed)
         branch[...] = jnp.zeros_like(branch)
 
-    @pl.when(step >= blocks)
-    def _():
-        block = step - blocks
+    @pl.when(step >= half_steps)
+    def _():
         ffn_low = third_grad[...].astype(BF)
-        grad_out_ref[0] = mm(low_t[...], activated[block]).astype(BF)
-        grad_hidden = mm(ffn_low, out_ref[0]) * gelu_slope(hidden[block])
-        grad_low = grad_hidden.astype(BF)
-        small_ref[pl.ds(4 + block, 1)] = rows_sum(grad_low.astype(F32))
-        grad_in_ref[0] = mm(second_low_t[...], grad_low).astype(BF)
-        branch[...] += mm_nt(grad_low, in_ref[0])
-
-    @pl.when(step == 2 * blocks - 1)
+        first = (step - half_steps) * per
+        grads = [mm(ffn_low, out_ref[k]) for k in range(per)]
+        total = branch[...]
+        for k in range(per):
+            grad_low = (grads[k] * slope[first + k]).astype(BF)
+            right[first + k] = grad_low
+            right_copy(first + k).start()
+            small_ref[pl.ds(4 + first + k, 1)] = rows_sum(grad_low.astype(F32))
+            total = total + mm_nt(grad_low, in_ref[k])
+        branch[...] = total
+
+    @pl.when(step == 2 * half_steps - 1)
     def _():
         second_in = third_grad[...] + branch[...]
         normed, scale = norm_parts(second_sum[...])
@@ -334,8 +353,14 @@
         small_ref[11:12] = rows_sum(second_in)
         small_ref[15:16] = rows_sum(second_in * normed)
         cross_low = grad.astype(BF)
-        cross_grad_ref[...] = mm(cross_low.T, mixed_ref[...]).astype(BF)
+        left[2] = cross_low.T
+        left_copy(2).start()
         mixed_grad_ref[...] = mm(cross_low, cross_w_ref[0]).astype(BF)
+        mixed_copy.wait()
+        for which in range(3):
+            left_copy(which).wait()
+        for which in range(2 * blocks):
+            right_copy(which).wait()
 
 
 def cross_back_step(
@@ -417,7 +442,8 @@
     normed, scale = norm_parts(sum_ref[...])
     first_low = (normed * gain_of(gain_ref, 0) + row_of(row_ref, 1)).astype(BF)
     cross_query_grad = cross_query_grad_ref[...]
-    emit(4, mm(first_low.T, cross_query_grad))
+    first_low_t = first_low.T
+    emit(4, lambda lanes: mm(first_low_t, cross_query_grad_ref[:, lanes]))
     unit()
     first_in = residual_ref[...] + mm_nt(cross_query_grad, weight_ref[4])
     first_grad = norm_back(normed, scale, gain_of(gain_ref, 0), first_in)
@@ -426,7 +452,8 @@
     small_ref[14:15] = rows_sum(first_in * normed)
     unit()
     self_low = first_grad.astype(BF)
-    emit(3, mm(self_low.T, mixed_ref[...]))
+    self_low_t = self_low.T
+    emit(3, lambda lanes: mm(self_low_t, mixed_ref[:, lanes]))
     unit()
     mixed_grad = mm(self_low, weight_ref[3]).astype(BF)
     for image in range(images):
@@ -444,7 +471,7 @@
     total = first_grad
     for which in range(3):
         grad = qkv_grad[which]
-        emit(which, mm(tokens_t, grad))
+        emit(which, lambda lanes, which=which: mm(tokens_t, qkv_grad[which, :, lanes]))
         unit()
         total = total + mm_nt(grad, weight_ref[which])
     small_ref[0:1] = rows_sum(qkv_grad[0].astype(F32))
@@ -459,7 +486,9 @@
     small_ref[...] = jnp.zeros_like(small_ref)
 
     def emit(block, value):
-        wg_ref[block] = value.astype(BF)
+        for lane in range(0, wg_ref.shape[2], SLAB):
+            lanes = slice(lane, lane + SLAB)
+            wg_ref[block, :, lanes] = value(lanes).astype(BF)
 
     query_grad_ref[...] = self_back(
         images, valid, tokens_ref, weight_ref, row_ref, gain_ref, qkv_ref, mixed_ref, total_ref,
@@ -486,16 +515,18 @@
 def greet(depth, tasks):
     me = lax.axis_index("dp")
     barrier = pltpu.get_barrier_semaphore()
+    other = 1 - lax.axis_index("tensor")
     for peer in task_peers(tasks):
         pl.semaphore_signal(barrier, inc=1, device_id={"task": peer}, device_id_type=MESH_ID)
+        pl.semaphore_signal(
+            barrier, inc=1, device_id={"task": peer, "tensor": other}, device_id_type=MESH_ID
+        )
     for shift in range(1, depth):
         pl.semaphore_signal(
             barrier, inc=1, device_id={"dp": lax.rem(me + shift, depth)}, device_id_type=MESH_ID
         )
-    pl.semaphore_signal(
-        barrier, inc=1, device_id={"tensor": 1 - lax.axis_index("tensor")}, device_id_type=MESH_ID
-    )
-    pl.semaphore_wait(barrier, tasks + depth - 1)
+    pl.semaphore_signal(barrier, inc=1, device_id={"tensor": other}, device_id_type=MESH_ID)
+    pl.semaphore_wait(barrier, 2 * (tasks - 1) + depth)
 
 
 LAG = 2
@@ -504,9 +535,9 @@
 
 
 class Chain:
-    def __init__(self, depth, tasks, sources, near, far, refs):
+    def __init__(self, depth, tasks, near, far, refs):
         self.depth, self.tasks = depth, tasks
-        self.sources, self.near, self.far = sources, near, far
+        self.near, self.far = near, far
         (self.near_ring, self.far_ring, self.passed, self.parts,
          self.near_sem, self.far_sem, self.far_send, self.far_recv, self.pass_send, self.pass_recv,
          self.part_send, self.part_recv) = refs
@@ -515,7 +546,6 @@
         self.me = lax.axis_index("dp")
         self.task = lax.axis_index("task")
         self.is_end = (self.me == 0) | (self.me == depth - 1)
-        self.given = sum(source.shape[0] for source in sources)
 
     SCRATCH = 12
 
@@ -552,15 +582,6 @@
             tensor=1 - lax.axis_index("tensor"),
         )
 
-    def exchange(self):
-        base = 0
-        for source in self.sources:
-            for block in range(source.shape[0]):
-                for way in range(2):
-                    columns = pl.ds(self.half, self.half)
-                    self.far_copy(source.at[block, :, columns], way, base + block).start()
-            base += source.shape[0]
-
     def pass_copy(self, way, chunk):
         piece = self.passed.at[way, chunk]
         target = self.me - 1 if way == 0 else self.me + 1
@@ -611,21 +632,7 @@
 
                 start = pl.multiple_of(place * self.rows, self.rows)
                 rows = pl.ds(way * 2 * self.rows + start, self.rows)
-                base = 0
-                for source in self.sources:
-                    count = source.shape[0]
-
-                    @pl.when((block >= base) & (block < base + count))
-                    def _(source=source, base=base):
-                        columns = pl.ds(0, self.half)
-                        self.near_fetch(source.at[block - base, rows, columns], slot, way).start()
-
-                    base += count
-
-                @pl.when(block >= base)
-                def _():
-                    self.near_fetch(self.near.at[block - base, rows], slot, way).start()
-
+                self.near_fetch(self.near.at[block, rows], slot, way).start()
                 self.far_fetch(
                     self.far.at[way, block, pl.ds(start, self.rows)], slot, way
                 ).start()
@@ -830,9 +837,8 @@
     depth, tasks, images, groups, valid, block_order, order_ref, context_ref, query_ref, key_ref,
     value_ref, total_ref, mixed_grad_ref, tokens_ref, weight_ref, row_ref,
     gain_ref, qkv_ref, mixed_ref, self_total_ref, sum_ref, residual_ref, small_in_ref, all_w_ref,
-    block_ref, *refs
+    block_ref, left_first_ref, right_first_ref, left_ref, right_ref, *refs
 ):
-    sources, refs = refs[:3], refs[3:]
     (
         context_grad_ref, query_grad_ref, update_ref, small_out_ref, gram_ref, block_far, near, far,
         key_grad, value_grad,
@@ -844,7 +850,7 @@
         key_grad, value_grad, context_grad_ref, refs[: ContextGrad.SCRATCH]
     )
     refs = refs[ContextGrad.SCRATCH :]
-    chain = Chain(depth, tasks, sources, near, far, refs[: Chain.SCRATCH])
+    chain = Chain(depth, tasks, near, far, refs[: Chain.SCRATCH])
     refs = refs[Chain.SCRATCH :]
     gram_acc = refs[7]
     step = pl.program_id(0)
@@ -879,54 +885,71 @@
     )
     weight_copies = context_back.weight_copies([all_w_ref.at[5], all_w_ref.at[6]])
 
+    slots = stage.shape[0]
+
+    def far_copies(position):
+        slot = lax.rem(position, slots)
+        return [
+            chain.far_copy(stage.at[slot, :, pl.ds(half, half)], way, position) for way in range(2)
+        ]
+
+    def near_copy(position):
+        slot = lax.rem(position, slots)
+        return pltpu.make_async_copy(
+            stage.at[slot, :, pl.ds(0, half)], near.at[position], stage_sem.at[slot]
+        )
+
+    def emit(position, value):
+        position = jnp.int32(position)
+
+        @pl.when(position >= slots)
+        def _():
+            for copy in far_copies(position - slots):
+                copy.wait_send()
+
+        for lane in range(0, 2 * half, SLAB):
+            stage[lax.rem(position, slots), :, lane : lane + SLAB] = value(
+                slice(lane, lane + SLAB)
+            ).astype(BF)
+        for copy in far_copies(position):
+            copy.start()
+        near_copy(position).start()
+
     @pl.when(step == 0)
     def _():
         greet(depth, tasks)
-        chain.exchange()
+        emit(0, lambda lanes: mm(left_first_ref[0], right_first_ref[0, :, lanes]))
         block_copy.start()
         for copy in weight_copies:
             copy.start()
         gram_acc[...] = jnp.zeros_like(gram_acc)
         refs[0][...] = small_in_ref[...]
-        for index in range(AHEAD):
-            chain.fetch(index)
-
-    given = chain.given
-    slots = stage.shape[0]
-
-    def stage_copies(position):
-        slot = position % slots
-        return [
-            chain.far_copy(stage.at[slot, :, pl.ds(half, half)], way, given + position)
-            for way in range(2)
-        ]
-
-    def emit(position, value):
-        slot = position % slots
-        if position >= slots:
-            for copy in stage_copies(position - slots):
-                copy.wait_send()
-        stage[slot] = value.astype(BF)
-        for copy in stage_copies(position):
-            copy.start()
-        copy = pltpu.make_async_copy(
-            stage.at[slot, :, pl.ds(0, half)], near.at[position], stage_sem
-        )
-        copy.start()
-        copy.wait()
 
     @pl.when(step < cross_steps)
     def _():
         image = step // groups
         group = step - image * groups
+
+        emitted = step < cross_steps - 1
+
+        @pl.when(emitted)
+        def _():
+            emit(step + 1, lambda lanes: mm(left_ref[0], right_ref[0, :, lanes]))
+
+        @pl.when(step == 0)
+        def _():
+            near_copy(jnp.int32(0)).wait()
+            for index in range(AHEAD):
+                chain.fetch(jnp.int32(index))
 
         def cross_unit(part):
             if part == 0:
                 unit(step * UNITS)
             else:
 
-                @pl.when(step < cross_steps - 1)
+                @pl.when(emitted)
                 def _():
+                    near_copy(step + 1).wait()
                     unit(step * UNITS + part)
 
         grad_query, *grads = cross_back_step(
@@ -942,8 +965,10 @@
 
         @pl.when(step == cross_steps - 1)
         def _():
-            emit(0, key_acc[...])
-            emit(1, value_acc[...])
+            emit(cross_steps, lambda lanes: key_acc[:, lanes])
+            emit(cross_steps + 1, lambda lanes: value_acc[:, lanes])
+            near_copy(jnp.int32(cross_steps)).wait()
+            near_copy(jnp.int32(cross_steps + 1)).wait()
 
     @pl.when(step == cross_steps)
     def _():
@@ -960,21 +985,27 @@
             copy.start()
         for copy in weight_copies:
             copy.wait()
-        positions = {4: 2, 3: 3, 0: 4, 1: 5, 2: 6}
+        pending = []
+
+        def self_emit(block, value):
+            for position in pending:
+                near_copy(jnp.int32(position)).wait()
+            pending[:] = [block_order.index(block)]
+            emit(pending[0], value)
+
         query_grad_ref[...] = self_back(
             images, valid, tokens_ref, weight_ref, row_ref, gain_ref, qkv_ref, mixed_ref,
             self_total_ref, sum_ref, residual_ref, cross_query_grad, refs[0], qkv_grad,
-            lambda block, value: emit(positions[block], value), self_unit,
+            self_emit, self_unit,
         ).astype(BF)
+        for position in pending:
+            near_copy(jnp.int32(position)).wait()
         rest(
             chain, unit, context_back, done[0], order_ref, update_ref, small_out_ref, gram_ref, refs
         )
-        for position in range(len(block_order) - given - slots, len(block_order) - given):
-            for copy in stage_copies(position):
+        for position in range(len(block_order) - slots, len(block_order)):
+            for copy in far_copies(jnp.int32(position)):
                 copy.wait_send()
-        for block in range(given):
-            for way in range(2):
-                chain.far_arrival(way, block).wait_send()
         block_copy.wait()
         context_back.finish()
 
@@ -984,9 +1015,9 @@
 ):
     (
         small, small_own, small_other, small_far, small_pass, small_all, small_both, gram_acc,
-        gram_task, gram_core, gram_end, hop, out,
+        gram_plane, gram_end, hop, out,
         small_far_sem, small_pass_sem, small_task_sem, small_dp_sem, small_core_sem,
-        gram_task_sem, gram_core_sem, gram_dp_sem, hop_sem, out_sem, update_sem,
+        gram_plane_sem, gram_dp_sem, hop_sem, out_sem, update_sem,
     ) = refs
     depth, tasks, half = chain.depth, chain.tasks, chain.half
     me, task, core = (lax.axis_index(axis) for axis in ("dp", "task", "tensor"))
@@ -1055,18 +1086,22 @@
                 landed, landed, small_task_sem.at[0, shift], small_task_sem.at[1, shift], task=peer
             ).wait_recv()
 
-    lanes = gram_task.shape[2]
-
-    def gram_task_copy(shift, peer):
+    lanes = gram_plane.shape[2]
+    plane = 2 * tasks
+    mine = 2 * task + core
+
+    def gram_copy(shift):
+        to = lax.rem(mine + shift, plane)
         return send(
-            gram_task.at[task], gram_task.at[task], gram_task_sem.at[0, shift],
-            gram_task_sem.at[1, shift], task=peer,
-        )
-
-    def gram_core_copy(which):
+            gram_plane.at[mine], gram_plane.at[mine], gram_plane_sem.at[0, shift - 1],
+            gram_plane_sem.at[1, shift - 1], task=to // 2, tensor=lax.rem(to, 2),
+        )
+
+    def gram_arrival(shift):
+        place = lax.rem(mine + plane - shift, plane)
         return send(
-            gram_core.at[which], gram_core.at[which], gram_core_sem.at[0], gram_core_sem.at[1],
-            tensor=1 - core,
+            gram_plane.at[place], gram_plane.at[place], gram_plane_sem.at[0, shift - 1],
+            gram_plane_sem.at[1, shift - 1], task=place // 2, tensor=lax.rem(place, 2),
         )
 
     def gram_dp_copy(end, shift):
@@ -1078,51 +1113,33 @@
     def one_number(values):
         return jnp.sum(jnp.sum(values, axis=0, keepdims=True), axis=1, keepdims=True)
 
+    @pl.when(top & (task == 0))
+    def _():
+        small_values = [small_all[t] for t in range(tasks)]
+        for index, (a, b) in enumerate(pairs):
+            product = small_values[a] * small_values[b]
+            gram_acc[index * 8 : index * 8 + 8] += product[0:8] + product[8:16] + product[16:24]
+
     @pl.when(is_end)
     def _():
-        gram_task[task] = jnp.zeros(gram_task.shape[1:], F32)
+        gram_plane[mine] = jnp.zeros(gram_plane.shape[1:], F32)
         for index in range(len(pairs)):
-            gram_task[task, index : index + 1] = jnp.broadcast_to(
+            gram_plane[mine, index : index + 1] = jnp.broadcast_to(
                 one_number(gram_acc[index * 8 : index * 8 + 8]), (1, lanes)
             )
-        for shift, peer in enumerate(task_peers(tasks)):
-            gram_task_copy(shift, peer).start()
-
-    @pl.when(top)
-    def _():
-        small_all_values = [small_all[t] for t in range(tasks)]
-        for index, (a, b) in enumerate(pairs):
-            gram_end[0, index : index + 1] = jnp.broadcast_to(
-                one_number(small_all_values[a] * small_all_values[b]), (1, lanes)
-            )
-
-    @pl.when(is_end)
-    def _():
-        for shift, peer in enumerate(task_senders(tasks)):
-            landed = gram_task.at[peer]
-            send(
-                landed, landed, gram_task_sem.at[0, shift], gram_task_sem.at[1, shift], task=peer
-            ).wait_recv()
-        total = gram_task[0]
-        for t in range(1, tasks):
-            total = total + gram_task[t]
-
-        @pl.when(top)
-        def _():
-            gram_core[core] = total + gram_end[0]
-
-        @pl.when(jnp.logical_not(top))
-        def _():
-            gram_core[core] = total
-
-        gram_core_copy(core).start()
-        gram_core_copy(1 - core).wait_recv()
+        for shift in range(1, plane):
+            gram_copy(shift).start()
+        for shift in range(1, plane):
+            gram_arrival(shift).wait_recv()
 
     for end in range(2):
 
         @pl.when(me == (depth - 1) * end)
         def _(end=end):
-            gram_end[end] = gram_core[0] + gram_core[1]
+            total = gram_plane[0]
+            for place in range(1, plane):
+                total = total + gram_plane[place]
+            gram_end[end] = total
             for shift in range(depth - 1):
                 gram_dp_copy(end, shift).start()
 
@@ -1148,19 +1165,29 @@
     blocks = out.shape[0]
     group = blocks // GROUPS
     share = chain.rows // tasks
-    mine = pl.ds(pl.multiple_of(task * share, share), share)
+    own_share = pl.ds(pl.multiple_of(task * share, share), share)
     own_part = jnp.minimum(me, 1)
 
     def hop_copy(index):
         return send(
-            hop.at[pl.ds(index * group, group)], out.at[pl.ds(index * group, group), mine],
+            hop.at[pl.ds(index * group, group)], out.at[pl.ds(index * group, group), own_share],
             hop_sem.at[0, index], hop_sem.at[1, index],
             dp=jnp.where(top, 1, depth - 2),
         )
 
-    def out_copy(index, shift, peer):
-        piece = out.at[pl.ds(index * group, group), mine]
-        return send(piece, piece, out_sem.at[0, index, shift], out_sem.at[1, index, shift], task=peer)
+    beside = [task + 1 - 2 * lax.rem(task, 2), task + 2 - 4 * (task // 2)]
+    across = tasks - 1 - task
+
+    def out_piece(index, owner):
+        rows = pl.ds(pl.multiple_of(owner * share, share), share)
+        return out.at[pl.ds(index * group, group), rows]
+
+    def out_copy(index, which, owner):
+        piece = out_piece(index, owner)
+        peer = beside[which] if which < 2 else beside[1 if index < GROUPS // 2 else 0]
+        return send(
+            piece, piece, out_sem.at[0, index, which], out_sem.at[1, index, which], task=peer
+        )
 
     def update_copy(index):
         at = pl.ds(index * group, group)
@@ -1205,19 +1232,19 @@
             hop_copy(index).start()
 
             def own(block, carry):
-                out[block, mine] = weighted(2 * block + own_part)
+                out[block, own_share] = weighted(2 * block + own_part)
                 return carry
 
             lax.fori_loop(index * group, (index + 1) * group, own, 0)
-            for shift, peer in enumerate(task_peers(tasks)):
-                out_copy(index, shift, peer).start()
+            for which in range(2):
+                out_copy(index, which, task).start()
 
     @pl.when(jnp.logical_not(is_end))
     def _():
         for index in range(GROUPS):
             hop_copy(index).wait_recv()
-            for shift, peer in enumerate(task_peers(tasks)):
-                out_copy(index, shift, peer).start()
+            for which in range(2):
+                out_copy(index, which, task).start()
 
     for shift in range(depth - 1):
 
@@ -1228,13 +1255,11 @@
     small_core_copy().start()
 
     for index in range(GROUPS):
-        for shift, peer in enumerate(task_senders(tasks)):
-            piece = out.at[
-                pl.ds(index * group, group), pl.ds(pl.multiple_of(peer * share, share), share)
-            ]
-            send(
-                piece, piece, out_sem.at[0, index, shift], out_sem.at[1, index, shift], task=peer
-            ).wait_recv()
+        for which in range(2):
+            out_copy(index, which, beside[which]).wait_recv()
+        out_copy(index, 2, beside[0 if index < GROUPS // 2 else 1]).start()
+    for index in range(GROUPS):
+        out_copy(index, 2, across).wait_recv()
         update_copy(index).start()
 
     small_core_copy().wait_recv()
@@ -1267,16 +1292,15 @@
 
     @pl.when(is_end)
     def _():
-        gram_core_copy(core).wait_send()
-        for shift, peer in enumerate(task_peers(tasks)):
-            gram_task_copy(shift, peer).wait_send()
+        for shift in range(1, plane):
+            gram_copy(shift).wait_send()
         for index in range(GROUPS):
             hop_copy(index).wait_send()
 
     for index in range(GROUPS):
         update_copy(index).wait()
-        for shift, peer in enumerate(task_peers(tasks)):
-            out_copy(index, shift, peer).wait_send()
+        for which in range(3):
+            out_copy(index, which, task).wait_send()
 
 
 def spread_kernel(
@@ -1284,8 +1308,8 @@
     block_far_ref, small_ref, gram_in_ref,
     update_ref, context_out_ref, query_out_ref, block_out_ref, head_ref, row_ref, gain_ref, gram_ref,
 ):
-    for index, block in enumerate(block_order):
-        update_ref[:, block, :] = parts_ref[index].astype(F32)
+    ordered = [parts_ref[block_order.index(block)] for block in range(len(block_order))]
+    update_ref[...] = jnp.swapaxes(jnp.stack(ordered), 0, 1).astype(F32)
     context_out_ref[...] = context_grad_ref[...]
 
     @pl.when(pl.program_id(0) == 0)
@@ -1440,41 +1464,39 @@
         name="cross_forward",
     )(memory, cross_query, weights, weights, head_rows)
 
-    (
-        block_rows, grad_in, grad_out, cross_out_wg, mixed_grad, second_grad, ffn_small,
-    ) = pl.pallas_call(
+    per = 2 if blocks % 2 == 0 else 1
+    block_rows, left, right, mixed_grad, second_grad, ffn_small = pl.pallas_call(
         functools.partial(ffn_kernel, images, blocks),
-        grid=(2 * blocks,),
+        grid=(2 * blocks // per,),
         out_shape=(
             low_rows,
-            jax.ShapeDtypeStruct((blocks, width, width), BF),
-            jax.ShapeDtypeStruct((blocks, width, width), BF),
-            one_block, low_rows, full_rows, small_shape,
+            jax.ShapeDtypeStruct((3, width, rows), BF),
+            jax.ShapeDtypeStruct((2 * blocks + 1, rows, width), BF),
+            low_rows, full_rows, small_shape,
         ),
         in_specs=[
             rows_spec, rows_spec, rows_spec,
             const(matches.shape, 0, 0, 0),
             pl.BlockSpec(memory_space=pltpu.SMEM),
             const((1, width, width), 7, 0, 0),
-            pl.BlockSpec((1, width, width), lambda s: (8 + s % blocks, 0, 0)),
-            pl.BlockSpec((1, width, width), lambda s: (8 + blocks + s % blocks, 0, 0)),
+            pl.BlockSpec((per, width, width), lambda s: (8 // per + s % (blocks // per), 0, 0)),
+            pl.BlockSpec(
+                (per, width, width), lambda s: ((8 + blocks) // per + s % (blocks // per), 0, 0)
+            ),
             head_spec, row_spec, gain_spec,
         ],
-        out_specs=(
-            rows_spec,
-            pl.BlockSpec((1, width, width), lambda s: (jnp.maximum(s - blocks, 0), 0, 0)),
-            pl.BlockSpec((1, width, width), lambda s: (jnp.maximum(s - blocks, 0), 0, 0)),
-            const((width, width), 0, 0), rows_spec, rows_spec, small_spec,
-        ),
+        out_specs=(rows_spec, any_spec(), any_spec(), rows_spec, rows_spec, small_spec),
         scratch_shapes=[
             pltpu.VMEM((rows, width), F32),
-            pltpu.VMEM((width, rows), BF),
-            pltpu.VMEM((width, rows), BF),
+            pltpu.VMEM((rows, width), BF),
+            pltpu.VMEM((3, width, rows), BF),
+            pltpu.VMEM((2 * blocks, rows, width), BF),
             pltpu.VMEM((blocks, rows, width), F32),
-            pltpu.VMEM((blocks, rows, width), BF),
             pltpu.VMEM((rows, width), F32),
             pltpu.VMEM((rows, width), F32),
             pltpu.VMEM((8, width), F32),
+            pltpu.SemaphoreType.DMA((3,)),
+            pltpu.SemaphoreType.DMA((2 * blocks + 1,)),
         ],
         compiler_params=params_for(),
         name="ffn",
@@ -1499,6 +1521,9 @@
                 return make(now // groups, now - groups * (now // groups))
 
             return index_map
+
+        def ahead(step):
+            return jnp.minimum(step + 1, 2 * blocks)
 
         def once(shape):
             return pl.BlockSpec(
@@ -1522,7 +1547,7 @@
                 small_shape,
                 jax.ShapeDtypeStruct((16, 128), F32),
                 low_rows,
-                jax.ShapeDtypeStruct((7, width, half), BF),
+                jax.ShapeDtypeStruct((block_count, width, half), BF),
                 jax.ShapeDtypeStruct((2, block_count, width // 2, half), BF),
                 key_rows, key_rows,
             ),
@@ -1536,7 +1561,10 @@
                 once(norm_gain.shape),
                 once((3, rows, width)), once((rows, width)), once(total_shape.shape),
                 once((rows, width)), once((rows, width)), once((24, width)),
-                any_spec(), any_spec(), any_spec(), any_spec(), any_spec(),
+                any_spec(), any_spec(),
+                once((1, width, rows)), once((1, rows, width)),
+                pl.BlockSpec((1, width, rows), lambda step: (ahead(step) // blocks, 0, 0)),
+                pl.BlockSpec((1, rows, width), lambda step: (ahead(step), 0, 0)),
             ],
             out_specs=(
                 any_spec(), once((rows, width)), any_spec(), once((24, width)), once((16, 128)),
@@ -1549,7 +1577,7 @@
                 pltpu.VMEM((rows, width), BF),
                 pltpu.VMEM((3, rows, width), BF),
                 pltpu.VMEM((3, width, width), BF),
-                dma(()),
+                dma((3,)),
                 dma((2,)),
                 *ContextGrad.scratch(keys, width),
                 *Chain.scratch(block_count, chain_rows, half, tasks),
@@ -1558,8 +1586,7 @@
                 pltpu.VMEM((tasks, 24, half), F32),
                 pltpu.VMEM((2, 24, half), F32),
                 pltpu.VMEM((pair_rows, half), F32),
-                pltpu.VMEM((tasks, 16, 128), F32),
-                pltpu.VMEM((2, 16, 128), F32),
+                pltpu.VMEM((2 * tasks, 16, 128), F32),
                 pltpu.VMEM((2, 16, 128), F32),
                 pltpu.VMEM((block_count, chain_rows // tasks, half), BF),
                 pltpu.VMEM((block_count, chain_rows, half), BF),
@@ -1568,8 +1595,7 @@
                 dma((2, tasks - 1)),
                 dma((2, depth - 1)),
                 dma((2,)),
-                dma((2, tasks - 1)),
-                dma((2,)),
+                dma((2, 2 * tasks - 1)),
                 dma((2, 2, depth - 1)),
                 dma((2, GROUPS)),
                 dma((2, GROUPS, tasks - 1)),
@@ -1580,7 +1606,7 @@
         )(
             task_order, memory, cross_query, keys_act, values_act, cross_total, mixed_grad,
             tokens, weights, row_bias, norm_gain, qkv, self_mixed, self_total, first_sum,
-            second_grad, ffn_small, weights, block_rows, grad_in, grad_out, cross_out_wg[None],
+            second_grad, ffn_small, weights, block_rows, left, right, left, right,
         )
         tile = chain_rows // images
         (
@@ -1672,6 +1698,10 @@
     memory_grad = context_grad[None]
 
     small = self_small + cross_small + ffn_small
+    product = functools.partial(jnp.einsum, "dr,jre->jde", preferred_element_type=F32)
+    grad_in = product(left[0], right[:blocks]).astype(BF)
+    grad_out = product(left[1], right[blocks : 2 * blocks]).astype(BF)
+    cross_out_wg = product(left[2], right[2 * blocks :])[0].astype(BF)
     grads = jnp.concatenate(
         [self_wg, jnp.stack([key_wg, value_wg, cross_out_wg]), grad_in, grad_out], axis=0
     )

time: 289 us -> 275 us (0.952)
  Pallas kernels: 288 us -> 275 us
    pallas_call x1, Pallas kernels: 25.2 us -> 19.1 us  [body(): pl.pallas_call(functools.partial(ffn_kernel, images, blocks), grid=(2 * b...]
    pallas_call x1, Pallas kernels: 200 us -> 194 us  [body(): pl.pallas_call(functools.partial(back_kernel, depth, tasks, images, group...]
where the time goes in v5:
time: 275 us; the launch traced here: 277 us
  Pallas kernels  275 us (100%)
    pallas_call x1, Pallas kernels, body(): pl.pallas_call(functools.partial(back_kernel, depth, tasks, images, group...  194 us
    pallas_call x1, Pallas kernels, body(): pl.pallas_call(cross_kernel, grid=(images, groups), in_specs=[context_all...  25.6 us
    pallas_call x1, Pallas kernels, body(): pl.pallas_call(functools.partial(ffn_kernel, images, blocks), grid=(2 * b...  19.1 us
    pallas_call x1, Pallas kernels, body(): pl.pallas_call(functools.partial(gather_kernel, images, valid), grid=(wid...  18.2 us
    pallas_call x1, Pallas kernels, body(): pl.pallas_call(functools.partial(spread_kernel, images, valid, tasks, blo...  9.28 us
    pallas_call x1, Pallas kernels, body(): pl.pallas_call(functools.partial(self_kernel, images, valid), grid=(1,),...  8.86 us

profile of v5, /device:TPU:8, one launch (start us, length us, event | category | flops | bytes accessed | tf_op | source)
XLA Modules:
  0.0 277.4 jit_solution(8619337690351716664)
XLA Ops:
  0.6 1.3 copy.18.matches_ref
  1.9 18.2 %gather_weights.1 = (bf16[16,768,768]{2,1,0:T(8,128)(2,1)}, bf16[16,768]{1,0:T(8,128)(2,1)}, bf16[336,768]{1,0:T(8,128)(2,1)}, bf16[336,768]{1,0:T(8,128)(2,1)}) custom-call(bf16[768,16,384]{2,1,0:T(8,128)(2,1)} %own_ref.1, bf16[8,384]{1,0:T(8,128)(2,1)} %bias_ref.1, bf16[1,600,768]{2,1,0:T(8,128)(2,1)} %queries_ref.1, bf16[1,600,768]{2,1,0:T(8,128)(2,1)} %cotangent_ref.1), custom_call_target="tpu_custom_call" | custom-call | tf_op jit(solution)/shard_map/gather_weights/pallas_call | solution.py:1381
  20.1 8.9 %self_forward.1 = (bf16[3,336,768]{2,1,0:T(8,128)(2,1)}, bf16[336,768]{1,0:T(8,128)(2,1)}, f32[9,8,448]{2,1,0:T(8,128)}, f32[336,768]{1,0:T(8,128)}, bf16[336,768]{1,0:T(8,128)(2,1)}) custom-call(bf16[336,768]{1,0:T(8,128)(2,1)} %get-tuple-element.41.tokens_ref, ...), custom_call_target="tpu_custom_call" | custom-call | tf_op jit(solution)/shard_map/self_forward/pallas_call | solution.py:1426
  28.9 25.6 %cross_forward.1 = (bf16[3600,768]{1,0:T(8,128)(2,1)}, bf16[3600,768]{1,0:T(8,128)(2,1)}, bf16[336,768]{1,0:T(8,128)(2,1)}, f32[9,8,448]{2,1,0:T(8,128)}) custom-call(bf16[1,7200,768]{2,1,0:T(8,128)(2,1)} %context_ref.3, bf16[336,768]{1,0:T(8,128)(2,1)} %get-tuple-element.44.query_ref, ...), custom_call_target="tpu_custom_call" | custom-call | tf_op jit(solution)/shard_map/cross_forward/pallas_call | solution.py:1454
  54.5 19.1 %ffn.1 = (bf16[336,768]{1,0:T(8,128)(2,1)}, bf16[3,768,336]{2,1,0:T(8,128)(2,1)}, bf16[9,336,768]{2,1,0:T(8,128)(2,1)}, bf16[336,768]{1,0:T(8,128)(2,1)}, f32[336,768]{1,0:T(8,128)}, /*index=5*/f32[24,768]{1,0:T(8,128)}) custom-call(f32[336,768]{1,0:T(8,128)} %get-tuple-element.48.sum_ref, bf16[336,768]{1,0:T(8,128)(2,1)} %get-tuple-element.49.mixed_ref, ...), custom_call_target="tpu_custom_call" | custom-call | tf_op jit(solution)/shard_map/ffn/pallas_call | solution.py:1468
  73.7 194.2 %backward.1 = (bf16[3600,768]{1,0:T(8,128)(2,1)}, bf16[336,768]{1,0:T(8,128)(2,1)}, bf16[16,192,384]{2,1,0:T(8,128)(2,1)}, f32[24,768]{1,0:T(8,128)}, f32[16,128...) custom-call(s32[4]{0:T(128)} %order_ref.1, ...), custom_call_target="tpu_custom_call" | custom-call | tf_op jit(solution)/shard_map/backward/pallas_call | solution.py:1539
  267.9 9.3 %spread.1 = (f32[192,16,384]{2,1,0:T(8,128)}, bf16[3600,768]{1,0:T(8,128)(2,1)}, bf16[300,768]{1,0:T(8,128)(2,1)}, bf16[600,768]{1,0:T(8,128)(2,1)}, f32[8,384]{...) custom-call(bf16[16,192,384]{2,1,0:T(8,128)(2,1)} %get-tuple-element.60.parts_ref, ...), custom_call_target="tpu_custom_call" | custom-call | tf_op jit(solution)/shard_map/spread/pallas_call | solution.py:1615
